TPU v7x, 128 devices: a whole 4x4x4 slice. The times are simulated.
128 devices in a mesh: row: 8 (over x, core), col: 16 (over y, z).
Axes of the slice: x: 4, y: 4, z: 4, core: 2. Of those that a mesh axis runs over, the one named last changes fastest.
Arguments:
- slip_rate: float32 [2, 16777216], P(None, ('row', 'col')), may hold values from -6 to 6
- source_cluster: int32 [65536], P(('row', 'col')), may hold values from 0 to 65535, as said below
- near_kernel: float32 [8, 16, 16, 512, 512], P('row', 'col'), may hold values from -0.1875 to 0.1875
- near_pattern: int32 [8, 16, 2, 16], P('row', 'col'), may hold values from 0 to 511, as said below
- far_left: bfloat16 [8, 16, 96, 32, 512], P('row', 'col'), may hold values from -0.3125 to 0.3125
- far_right: bfloat16 [8, 16, 96, 32, 512], P('row', 'col'), may hold values from -0.25 to 0.25
- far_pattern: int32 [8, 16, 2, 96], P('row', 'col'), may hold values from 0 to 511, as said below
- stress: float32 [2, 262144], P(None, ('row', 'col')), may hold values from -1 to 1
- state: float32 [262144], P(('row', 'col')), may hold values from -0.5 to 0.5
- fault_of_row: int32 [262144], P(('row', 'col')), may hold values from 0 to 39
- direct_effect: float32 [40], replicated, may hold values from 0.5 to 1
- evolution_effect: float32 [40], replicated, may hold values from 0.5 to 1.5
- normal_stress: float32 [40], replicated, may hold values from 2 to 4
Outputs:
- new_stress: float32 [2, 262144], P(None, ('row', 'col'))
- new_rate: float32 [262144], P(('row', 'col'))
- new_state: float32 [262144], P(('row', 'col'))
Inputs may be any that keep to these rules, and one draw needn't show every extreme that they name: `source_cluster`: A permutation of the 65536 fault clusters. Of the 512 positions held by one device, at most 8 name clusters of one and the same device's block of 512 fault clusters, and some pair reaches 8. `near_pattern`: entries [.., 0, n] are below 128, entries [.., 1, n] below 512. On one device, the dense and far blocks of one piece have distinct row clusters. `far_pattern`: as for near_pattern, jointly with it.
All inputs are finite; a program needn't handle non-finite values.
Results may differ from a plain program's by a relative error of at most 0.0016.
Values sent between devices are 32-bit elements; how exact they have to be, the bound alone decides.
No kernel may reach another device: no remote copies, remote signals or barrier semaphores. Data moves between devices by JAX's collectives and lax.ppermute only.
A program may use at most 128 MiB of HBM per device.

v0:
```python
import jax
import jax.numpy as jnp
from jax import lax
from jax.sharding import PartitionSpec as P

B = 256
CLU_DEV = 512
RC_DEV = 128
NP = 2
FP = 12


STEP_SIZE = 0.25


def request_slots(wanted, senders, capacity):
    ordering = jnp.argsort(wanted, stable=True)
    ordered = wanted[ordering]
    owners = ordered // CLU_DEV
    labels = jnp.arange(senders, dtype=jnp.int32)
    counts = jnp.sum((owners[None, :] == labels[:, None]).astype(jnp.int32), axis=1)
    starts = jnp.cumsum(counts) - counts
    rank_in = jnp.arange(wanted.shape[0], dtype=jnp.int32) - starts[owners]
    slot_sorted = owners * capacity + rank_in
    requests = jnp.zeros((senders * capacity,), jnp.int32).at[slot_sorted].set(ordered % CLU_DEV)
    slot_of = jnp.zeros(wanted.shape, jnp.int32).at[ordering].set(slot_sorted)
    return (requests, slot_of)


def block_sums(
    summed, kernel_rows, sources, near_rows, lefts, rights, far_sources, far_rows, row_labels
):
    highest = lax.Precision.HIGHEST
    near_count = kernel_rows.shape[0]
    far_count = lefts.shape[0]
    product = jnp.einsum("nij,nj->ni", kernel_rows, sources, precision=highest).reshape(
        near_count, 2, B
    )
    selector = (near_rows[None, :] == row_labels[:, None]).astype(jnp.float32)
    summed = jnp.einsum("in,ncj->cij", selector, product, precision=highest)
    far_sources = far_sources.astype(jnp.bfloat16)
    coefficients = jnp.einsum(
        "nkj,nj->nk", rights, far_sources, preferred_element_type=jnp.float32
    ).astype(jnp.bfloat16)
    far_product = jnp.einsum(
        "nki,nk->ni", lefts, coefficients, preferred_element_type=jnp.float32
    ).reshape(far_count, 2, B)
    far_selector = (far_rows[None, :] == row_labels[:, None]).astype(jnp.float32)
    return summed + jnp.einsum("in,ncj->cij", far_selector, far_product, precision=highest)


def body(
    slip_rate,
    source_cluster,
    near_kernel,
    near_pattern,
    far_left,
    far_right,
    far_pattern,
    stress,
    state,
    fault_of_row,
    direct_effect,
    evolution_effect,
    normal_stress,
):
    highest = lax.Precision.HIGHEST
    row_count = lax.axis_size("row")
    col_count = lax.axis_size("col")
    senders = row_count * col_count
    capacity = 2 * CLU_DEV // senders
    local_slip = slip_rate.reshape(2, CLU_DEV, B)
    near_blocks = near_kernel[0, 0]
    near_index = near_pattern[0, 0]
    left_factor = far_left[0, 0]
    right_factor = far_right[0, 0]
    far_index = far_pattern[0, 0]
    row_labels = jnp.arange(RC_DEV, dtype=jnp.int32)
    empty = jnp.zeros((2, RC_DEV, B), jnp.float32)
    requests, slot_of = request_slots(source_cluster, senders, capacity)
    replies = lax.all_to_all(
        jnp.take(
            local_slip,
            lax.all_to_all(
                requests.reshape(senders, capacity),
                ("row", "col"),
                split_axis=0,
                concat_axis=0,
                tiled=True,
            ),
            axis=1,
        ),
        ("row", "col"),
        split_axis=1,
        concat_axis=1,
        tiled=True,
    )
    flat = replies.reshape(2, senders * capacity, B)
    own_piece = jnp.take(flat, slot_of, axis=1).reshape(2, source_cluster.shape[0] * B)
    arrived = lax.all_gather(own_piece, "row", axis=1, tiled=True)
    piece_count = arrived.shape[1] // (CLU_DEV * B)
    clusters = arrived.reshape(2, piece_count * CLU_DEV, B)
    near_count = piece_count * NP
    within = jnp.arange(near_count, dtype=jnp.int32) // NP * CLU_DEV + near_index[1]
    sources = jnp.transpose(jnp.take(clusters, within, axis=1), (1, 0, 2)).reshape(
        near_count, 2 * B
    )
    far_count = piece_count * FP
    far_within = jnp.arange(far_count, dtype=jnp.int32) // FP * CLU_DEV + far_index[1]
    far_sources = jnp.transpose(jnp.take(clusters, far_within, axis=1), (1, 0, 2)).reshape(
        far_count, 2 * B
    )
    summed = block_sums(
        empty,
        near_blocks,
        sources,
        near_index[0],
        left_factor,
        right_factor,
        far_sources,
        far_index[0],
        row_labels,
    )
    partial_value = summed.reshape(2, RC_DEV * B)
    share_rows = RC_DEV * B // col_count
    summed_all = lax.psum(partial_value, "col")
    rate_now = lax.dynamic_slice_in_dim(
        summed_all, lax.axis_index("col") * share_rows, share_rows, 1
    )
    faults = direct_effect.shape[0]
    fault_table = jnp.stack([direct_effect, evolution_effect, normal_stress])
    selector_rows = (fault_of_row[None, :] == jnp.arange(faults, dtype=jnp.int32)[:, None]).astype(
        jnp.float32
    )
    per_row = jnp.dot(fault_table, selector_rows, precision=highest)
    new_stress = stress + STEP_SIZE * rate_now
    magnitude = jnp.sqrt(new_stress[0] * new_stress[0] + new_stress[1] * new_stress[1] + 1.0)
    new_rate = 2.0 * jnp.exp(-state / per_row[0]) * jnp.sinh(magnitude / (per_row[0] * per_row[2]))
    new_state = state + STEP_SIZE * per_row[1] * (jnp.exp(-state / per_row[1]) - new_rate)
    return (new_stress, new_rate, new_state)


def solution(mesh):
    return jax.shard_map(
        body,
        mesh=mesh,
        in_specs=(
            P(None, ("row", "col")),
            P(("row", "col")),
            P("row", "col", None, None, None),
            P("row", "col", None, None),
            P("row", "col", None, None, None),
            P("row", "col", None, None, None),
            P("row", "col", None, None),
            P(None, ("row", "col")),
            P(("row", "col")),
            P(("row", "col")),
            P(),
            P(),
            P(),
        ),
        out_specs=(P(None, ("row", "col")), P(("row", "col")), P(("row", "col"))),
        check_vma=False,
    )
```

profile of v0, /device:TPU:0, one launch (start us, length us, event | category | flops | bytes accessed | tf_op | source)
XLA Modules:
  0.0 272.8 jit_solution(1959033231854321005)
XLA Ops:
  7.2 4.6 %sort.17 = (s32[512]{0:T(512)}, s32[512]{0:T(512)S(1)}) sort(s32[512]{0:T(512)} %param.14, s32[512]{0:T(512)S(1)} %iota.34), dimensions={0}, to_apply=%region_0.0 | sort | flops 4608 | bytes 8192 | tf_op jit(solution)/shard_map/jit(argsort)/sort | solution.py:17
  11.8 3.6 %gather_fusion = s32[512]{0:T(512)S(1)} fusion(s32[512]{0:T(512)} %param.14, s32[1024]{0:T(1024)S(1)} %pad_clamp_fusion.4), kind=kCustom, calls=%fused_computation | custom fusion | bytes 6144 | tf_op jit(solution)/shard_map/gather | solution.py:18
  16.0 3.3 %gather_fusion.1 = s32[512]{0:T(512)S(1)} fusion(s32[128]{0:T(128)S(1)} %sub.42, s32[1024]{0:T(1024)S(1)} %pad_clamp_fusion.3), kind=kCustom, calls=%fused_computation.1 | custom fusion | bytes 6144 | tf_op jit(solution)/shard_map/gather | solution.py:23
  19.4 2.4 scatter_custom_fusion.1
  21.9 20.4 %all_to_all.20 = s32[128,1,8]{2,1,0:T(1,128)S(1)} all-to-all(s32[128,1,8]{2,1,0:T(1,128)S(1)} %bitcast.85), channel_id=1, replica_groups=mesh['row'=8,'col'=16] {'row','col'}, dimensions={0} | all-to-all | bytes 8192 | tf_op jit(solution)/shard_map/all_to_all | solution.py:84
  42.5 10.1 %gather_fusion.2 = f32[1024,2,256]{2,1,0:T(2,128)} fusion(f32[2,512,256]{2,0,1:T(2,128)} %bitcast.79, s32[1024]{0:T(1024)S(1)} %broadcast_clamp_fusion), kind=kCustom, calls=%fused_computation.2 | custom fusion | bytes 4198400 | tf_op jit(solution)/shard_map/jit(_take)/gather | solution.py:82
  52.6 5.2 %select_bitcast_fusion = f32[2,128,8,256]{3,0,2,1:T(2,128)} fusion(f32[128,8,2,256]{3,2,1,0:T(2,128)} %bitcast.77, pred[128,8]{1,0:T(8,128)(4,1)S(1)} %compare_and_fusion), kind=kLoop, calls=%fused_computation.14 | loop fusion | flops 524288 | bytes 4195328 | tf_op jit(solution)/shard_map/jit(_take)/select_n | solution.py:82
  57.8 5.8 %all-to-all-start.1 = ((f32[2,128,8,256]{3,0,2,1:T(2,128)}), f32[2,128,8,256]{3,0,2,1:T(2,128)}, u32[]{:S(2)}, u32[]{:S(2)}) async-start(f32[2,128,8,256]{3,0,2,1:T(2,128)} %select_bitcast_fusion), calls=%async_computation.1 | async-start | bytes 4194304 | tf_op jit(solution)/shard_map/all_to_all | solution.py:81
  63.7 2.4 scatter_custom_fusion
  66.5 26.4 %all-to-all-done.1 = f32[2,128,8,256]{3,0,2,1:T(2,128)} async-done(((f32[2,128,8,256]{3,0,2,1:T(2,128)}), f32[2,128,8,256]{3,0,2,1:T(2,128)}, u32[]{:S(2)}, u32[]{:S(2)}) %all-to-all-start.1) | async-done | bytes 2097184 | tf_op jit(solution)/shard_map/all_to_all | solution.py:81
  92.9 4.5 %gather_fusion.3 = f32[512,2,256]{2,1,0:T(2,128)} fusion(f32[2,1024,256]{2,0,1:T(2,128)} %bitcast.12, s32[1024]{0:T(1024)S(1)} %pad_clamp_fusion.2), kind=kCustom, calls=%fused_computation.3 | custom fusion | bytes 2099200 | tf_op jit(solution)/shard_map/jit(_take)/gather | solution.py:99
  97.4 3.0 %broadcast_select_fusion = f32[2,131072]{1,0:T(2,128)} fusion(f32[2,131072]{1,0:T(2,128)} %bitcast.78, pred[131072]{0:T(1024)(128)(4,1)S(1)} %broadcast_in_dim.64), kind=kLoop, calls=%fused_computation.17 | loop fusion | flops 262144 | bytes 2228224 | tf_op jit(solution)/shard_map/jit(_take)/select_n | solution.py:99
  100.9 0.8 fusion.7
  101.7 44.6 %all-gather.2.cloned.1.call-done = f32[2,1048576]{1,0:T(2,128)} async-done(((f32[2,131072]{1,0:T(2,128)}), f32[2,1048576]{1,0:T(2,128)}) %all-gather.2.cloned.1.call-update) | async-done | bytes 8388624 | tf_op jit(solution)/shard_map/all_gather | solution.py:100
  146.3 4.2 %gather_fusion.5 = bf16[96,2,256]{2,1,0:T(2,128)(2,1)S(1)} fusion(f32[2,4096,256]{2,0,1:T(2,128)} %bitcast.97, s32[1024]{0:T(1024)S(1)} %pad_clamp_fusion), kind=kCustom, calls=%fused_computation.5 | custom fusion | bytes 196992 | tf_op jit(solution)/shard_map/jit(_take)/gather | solution.py:110
  150.8 2.8 %fusion.4 = f32[96,1,32]{2,1,0:T(1,128)S(1)} fusion(bf16[96,512,1]{1,2,0:T(2,128)(2,1)S(1)} %reshape.435, bf16[1,1,96,32,512]{4,3,2,1,0:T(8,128)(2,1)} %param.18), kind=kOutput, calls=%fused_computation.12 | convolution fusion | flops 3145728 | bytes 3256320 | tf_op jit(solution)/shard_map/nkj,nj->nk/dot_general | solution.py:42
  154.1 0.7 copy.36
  154.8 4.0 %gather_fusion.4 = f32[16,2,256]{2,1,0:T(2,128)S(1)} fusion(f32[2,4096,256]{2,0,1:T(2,128)} %bitcast.98, s32[1024]{0:T(1024)S(1)} %pad_clamp_fusion.1), kind=kCustom, calls=%fused_computation.4 | custom fusion | bytes 65600 | tf_op jit(solution)/shard_map/jit(_take)/gather | solution.py:105
  159.0 17.2 %fusion = f32[16,1,512]{2,1,0:T(1,128)S(1)} fusion(f32[16,512,1]{1,2,0:T(1,128)S(1)} %reshape.433, f32[1,1,16,512,512]{4,3,2,1,0:T(8,128)} %param.15), kind=kOutput, calls=%fused_computation.8 | convolution fusion | flops 50331648 | bytes 16842752 | tf_op jit(solution)/shard_map/nij,nj->ni/dot_general | solution.py:36
  177.1 0.8 copy.30
  177.9 1.8 copy.39
  179.8 84.7 %all-reduce.2.cloned.1.call-done = f32[2,32768]{1,0:T(2,128)} async-done(((f32[2,32768]{1,0:T(2,128)}), f32[2,32768]{1,0:T(2,128)}) %all-reduce.2.cloned.1.call-update) | async-done | bytes 262160 | tf_op jit(solution)/shard_map/psum | solution.py:126
  264.5 0.7 multiply_add_fusion
  265.3 0.6 multiply_add_fusion.1
  (70 shorter events, 3.3 us)
Async XLA Ops:
  7.2 146.4 %copy-start = (bf16[1,1,96,32,512]{4,3,2,1,0:T(8,128)(2,1)S(1)}, bf16[1,1,96,32,512]{4,3,2,1,0:T(8,128)(2,1)}, u32[]{:S(2)}) copy-start(bf16[1,1,96,32,512]{4,3,2,1,0:T(8,128)(2,1)} %param.17) | copy-start | bytes 9437188
  57.8 35.1 %all-to-all-start.1 = ((f32[2,128,8,256]{3,0,2,1:T(2,128)}), f32[2,128,8,256]{3,0,2,1:T(2,128)}, u32[]{:S(2)}, u32[]{:S(2)}) async-start(f32[2,128,8,256]{3,0,2,1:T(2,128)} %select_bitcast_fusion), calls=%async_computation.1 | async-start | bytes 4194304 | tf_op jit(solution)/shard_map/all_to_all | solution.py:81
  63.6 37.1 %copy-start.8 = (s32[1,1,2,96]{3,2,1,0:T(2,128)S(1)}, s32[1,1,2,96]{3,2,1,0:T(2,128)}, u32[]{:S(2)}) copy-start(s32[1,1,2,96]{3,2,1,0:T(2,128)} %param.19) | copy-start | bytes 2308
  63.6 37.1 %copy-start.7 = (s32[1,1,2,16]{3,2,1,0:T(2,128)S(1)}, s32[1,1,2,16]{3,2,1,0:T(2,128)}, u32[]{:S(2)}) copy-start(s32[1,1,2,16]{3,2,1,0:T(2,128)} %param.16) | copy-start | bytes 388
  63.6 37.2 %copy-start.6 = (s32[2048]{0:T(1024)S(1)}, s32[2048]{0:T(1024)}, u32[]{:S(2)}) copy-start(s32[2048]{0:T(1024)} %param.22) | copy-start | bytes 24580
  63.6 37.2 %copy-start.9 = (f32[40]{0:T(128)S(1)}, f32[40]{0:T(128)}, u32[]{:S(2)}) copy-start(f32[40]{0:T(128)} %param.25) | copy-start | bytes 484
  63.6 37.2 %copy-start.10 = (f32[40]{0:T(128)S(1)}, f32[40]{0:T(128)}, u32[]{:S(2)}) copy-start(f32[40]{0:T(128)} %param.24) | copy-start | bytes 484
  63.7 37.2 %copy-start.11 = (f32[40]{0:T(128)S(1)}, f32[40]{0:T(128)}, u32[]{:S(2)}) copy-start(f32[40]{0:T(128)} %param.23) | copy-start | bytes 484
  63.7 82.6 %all-gather.2.cloned.1.call-start = ((), (), s32[]{:S(2)}) async-start(), calls=%async_computation.2 | async-start | bytes 9437184 | tf_op jit(solution)/shard_map/all_gather | solution.py:100
  100.4 164.1 %all-reduce.2.cloned.1.call-start = ((), (), s32[]{:S(2)}) async-start(), calls=%async_computation.3 | async-start | bytes 524288 | tf_op jit(solution)/shard_map/psum | solution.py:126
  158.9 17.7 %copy-start.1 = (f32[96,1,512]{2,0,1:T(8,128)S(1)}, f32[96,1,512]{2,0,1:T(8,128)}, u32[]{:S(2)}) copy-start(f32[96,1,512]{2,0,1:T(8,128)} %copy.36) | copy-start | bytes 589828
  158.9 20.8 %copy-start.3 = (f32[3,2048]{1,0:T(4,128)S(1)}, f32[3,2048]{1,0:T(4,128)}, u32[]{:S(2)}) copy-start(f32[3,2048]{1,0:T(4,128)} %fusion.7) | copy-start | bytes 73732
  158.9 105.6 %copy-start.4 = (f32[2,2048]{1,0:T(2,128)S(1)}, f32[2,2048]{1,0:T(2,128)}, u32[]{:S(2)}) copy-start(f32[2,2048]{1,0:T(2,128)} %param.20) | copy-start | bytes 49156
  159.0 106.4 %copy-start.5 = (f32[2048]{0:T(1024)S(1)}, f32[2048]{0:T(1024)}, u32[]{:S(2)}) copy-start(f32[2048]{0:T(1024)} %param.21) | copy-start | bytes 24580
  265.3 0.7 copy-start.2
Sparse Core Ops, SparseCore 0:
  100.6 45.7 all-gather.1
  179.9 84.6 all-reduce.1
where the time goes:
time: 273 us
  waiting for transfers between devices  156 us (57%)
  local copies, waits for them, and re-layouts  38.8 us (14%)
  matrix products  22.2 us (8%)
  blocking collectives  20.4 us (7%)
  other arithmetic  15.1 us (6%)
  between operations  14.5 us (5%)
  starting transfers between devices  6.05 us (2%)
    psum x1, waiting for transfers between devices, body(): summed_all = lax.psum(partial_value, 'col')  84.7 us
    all_gather x1, waiting for transfers between devices, body(): arrived = lax.all_gather(own_piece, 'row', axis=1, tiled=True)  44.6 us
    all_to_all x1, waiting for transfers between devices, body(): lax.all_to_all(jnp.take(local_slip, lax.all_to_all(requests.reshape(sende...  26.4 us
    all_to_all x1, blocking collectives, body(): lax.all_to_all(requests.reshape(senders, capacity), ('row', 'col'), split...  20.4 us
    dot_general x1, matrix products, block_sums(): jnp.einsum('nij,nj->ni', kernel_rows, sources, precision=highest)  17.2 us
    gather x1, local copies, waits for them, and re-layouts, body(): jnp.take(local_slip, lax.all_to_all(requests.reshape(senders, capacity),...  10.1 us
    all_to_all x1, starting transfers between devices, body(): lax.all_to_all(jnp.take(local_slip, lax.all_to_all(requests.reshape(sende...  5.78 us
  transfers between devices with their start and end apart: 3, of which 3 were waited for; matrix products, arithmetic and copies ran while one was open for 1% of the time, Pallas kernels for 0%

commit v1 on v0

v1 whole, which is shorter than its diff:
```python
import functools

import jax
import jax.numpy as jnp
from jax import lax
from jax.experimental import pallas as pl
from jax.experimental.pallas import tpu as pltpu
from jax.sharding import PartitionSpec as P

B = 256
R = 32
CLU_DEV = 512
RC_DEV = 128
NP = 2
FP = 12
N_ROW = 8
N_COL = 16
NEAR = N_ROW * NP
FAR = N_ROW * FP
BLOCKS = NEAR + FAR
LANES = 128
CAP = 8
ROUNDS = 16
FAULTS = 40
STEP_SIZE = 0.25

VMEM = pl.BlockSpec(memory_space=pltpu.VMEM)
SMEM = pl.BlockSpec(memory_space=pltpu.SMEM)
f32 = jnp.float32
bf16 = jnp.bfloat16
i32 = jnp.int32


def iota(shape, dim):
    return lax.broadcasted_iota(i32, shape, dim)


def piece_of(n):
    return jnp.where(n < NEAR, n >> 1, ((n - NEAR) * 43) >> 9)


def active_in(n, rnd):
    piece = piece_of(n)
    within = jnp.where(n < NEAR, n & 1, 2 + (n - NEAR) - FP * piece)
    half = (within >= 7).astype(i32)
    return (n < BLOCKS) & ((rnd < 0) | ((piece == (rnd >> 1)) & (half == (rnd & 1))))


def index_kernel(info_ref, g_ref, req_ref, pos_ref):
    rho = info_ref[0]
    rnd = info_ref[1]
    tables = g_ref[:, 0:CLU_DEV]
    m = g_ref[:, CLU_DEV : CLU_DEV + LANES]
    n = iota((N_ROW, LANES), 1)
    active = active_in(n, rnd)
    tab = jnp.concatenate([tables >> 8, tables & 255], axis=0).astype(f32).astype(bf16)
    piece_mask = (iota((N_ROW, LANES), 0) == piece_of(n)).astype(f32)
    place = iota((CLU_DEV, LANES), 0)
    rows = []
    for r in range(N_ROW):
        onehot = (place == m[r : r + 1, :]).astype(f32).astype(bf16)
        found = jnp.dot(tab, onehot, preferred_element_type=f32)
        value = found[0:N_ROW] * 256.0 + found[N_ROW : 2 * N_ROW]
        rows.append(jnp.sum(value * piece_mask, axis=0, keepdims=True))
    gid = jnp.concatenate(rows, axis=0).astype(i32)
    owner = jnp.where(active, gid >> 9, -1)
    local = gid & (CLU_DEV - 1)
    eye = (iota((LANES, LANES), 0) == iota((LANES, LANES), 1)).astype(f32).astype(bf16)
    owner_t = lax.dot_general(
        eye, owner.astype(f32).astype(bf16), (((1,), (1,)), ((), ())), preferred_element_type=f32
    ).astype(i32)
    before = iota((LANES, LANES), 0) < iota((LANES, LANES), 1)
    slots = []
    for r in range(N_ROW):
        same = (owner_t[:, r : r + 1] == owner[r : r + 1, :]) & before
        slots.append(jnp.sum(same.astype(f32), axis=0, keepdims=True))
    slot = jnp.concatenate(slots, axis=0).astype(i32)
    over = jnp.max(jnp.where(active & (slot >= CAP), 1.0, 0.0))
    pos_ref[...] = jnp.clip(owner * CAP + slot, 0, N_ROW * N_COL * CAP - 1)
    mine = (owner >> 4) == rho
    col_label = iota((N_COL, LANES), 0)
    target = iota((LANES, LANES), 0)
    total = jnp.zeros((2 * N_COL, LANES), f32)
    for r in range(N_ROW):
        sel = (col_label == (owner[r : r + 1, :] & (N_COL - 1))) & mine[r : r + 1, :]
        part = jnp.concatenate(
            [
                jnp.where(sel, local[r : r + 1, :] >> 8, 0),
                jnp.where(sel, local[r : r + 1, :] & 255, 0),
            ],
            axis=0,
        )
        want = jnp.where(slot[r : r + 1, :] < CAP, r * CAP + slot[r : r + 1, :], -1)
        put = (target == want).astype(f32).astype(bf16)
        total = total + lax.dot_general(
            part.astype(f32).astype(bf16), put, (((1,), (1,)), ((), ())), preferred_element_type=f32
        )
    req = total[0:N_COL] * 256.0 + total[N_COL : 2 * N_COL]
    req = jnp.where(iota((N_COL, LANES), 1) == N_ROW * CAP, over, req)
    req_ref[...] = req.astype(i32)


def make_index(info, gathered):
    return pl.pallas_call(
        index_kernel,
        out_shape=(
            jax.ShapeDtypeStruct((N_COL, LANES), i32),
            jax.ShapeDtypeStruct((N_ROW, LANES), i32),
        ),
        in_specs=[SMEM, VMEM],
        out_specs=(VMEM, VMEM),
        name="index",
    )(info, gathered)


def gather_kernel(idx_ref, slip_ref, out_ref, over_ref):
    def one_col(c, over):
        for r in range(N_ROW):
            for k in range(CAP):
                j = idx_ref[c, r * CAP + k]
                out_ref[(r * N_COL + c) * CAP + k] = slip_ref[j]
        return jnp.maximum(over, idx_ref[c, N_ROW * CAP])

    over_ref[0] = lax.fori_loop(0, N_COL, one_col, jnp.int32(0))


def gather_rows(idx, slip):
    return pl.pallas_call(
        gather_kernel,
        out_shape=(
            jax.ShapeDtypeStruct((N_ROW * N_COL * CAP, 2, B), f32),
            jax.ShapeDtypeStruct((1,), i32),
        ),
        in_specs=[SMEM, VMEM],
        out_specs=(VMEM, SMEM),
        name="gather",
    )(idx, slip)


def blocks_kernel(
    info_ref, pos_ref, near_row_ref, far_row_ref, x_ref, near_ref, left_ref, right_ref, out_ref, acc_ref
):
    p = pl.program_id(0)
    me = info_ref[0]

    @pl.when(p == 0)
    def _():
        out_ref[...] = jnp.zeros_like(out_ref)
        acc_ref[...] = jnp.zeros_like(acc_ref)

    chunk = 64
    lane = iota((chunk, LANES), 1)
    for t in range(NP):
        n = p * NP + t
        x = x_ref[pos_ref[me, n]]
        x0, x1 = x[0:1, :], x[1:2, :]
        here = lane == near_row_ref[0, n]
        for s in range(0, 2 * B, chunk):
            rows = pl.ds(s, chunk)
            prod = near_ref[t, rows, 0:B] * x0 + near_ref[t, rows, B : 2 * B] * x1
            total = jnp.sum(prod[:, 0:LANES] + prod[:, LANES:B], axis=1, keepdims=True)
            old = acc_ref[rows, :]
            acc_ref[rows, :] = jnp.where(here, old + total, old)
    for t in range(FP):
        n = p * FP + t
        x = x_ref[pos_ref[me, NEAR + n]].astype(bf16).astype(f32)
        right = right_ref[t].astype(f32)
        prod = right[:, 0:B] * x[0:1, :] + right[:, B : 2 * B] * x[1:2, :]
        coef = jnp.sum(prod[:, 0:LANES] + prod[:, LANES:B], axis=1, keepdims=True)
        coef = coef.astype(bf16).astype(f32)
        far = jnp.sum(left_ref[t].astype(f32) * coef, axis=0, keepdims=True)
        row = pl.ds(far_row_ref[0, n], 1)
        out_ref[row, :] = out_ref[row, :] + far

    @pl.when(p == N_ROW - 1)
    def _():
        out_ref[...] = out_ref[...] + acc_ref[...].T


def block_sums(info, pos, near_index, far_index, x, near, left, right):
    return pl.pallas_call(
        blocks_kernel,
        grid=(N_ROW,),
        out_shape=jax.ShapeDtypeStruct((RC_DEV, 2 * B), f32),
        in_specs=[
            SMEM,
            SMEM,
            SMEM,
            SMEM,
            pl.BlockSpec(x.shape, lambda p: (0, 0, 0)),
            pl.BlockSpec((NP, 2 * B, 2 * B), lambda p: (p, 0, 0)),
            pl.BlockSpec((FP, R, 2 * B), lambda p: (p, 0, 0)),
            pl.BlockSpec((FP, R, 2 * B), lambda p: (p, 0, 0)),
        ],
        out_specs=pl.BlockSpec((RC_DEV, 2 * B), lambda p: (0, 0)),
        scratch_shapes=[pltpu.VMEM((2 * B, LANES), f32)],
        compiler_params=pltpu.CompilerParams(vmem_limit_bytes=24 * 1024 * 1024),
        name="blocks",
    )(info, pos, near_index, far_index, x, near, left, right)


def final_kernel(
    a_ref, b_ref, s_ref, parts_ref, stress_ref, state_ref, fault_ref, out_stress, out_rate, out_state
):
    total = parts_ref[0]
    for c in range(1, N_COL):
        total = total + parts_ref[c]
    groups = RC_DEV // N_COL
    for h in range(2):
        every = pl.ds(h, groups, stride=2)
        state = state_ref[every, :]
        fault = fault_ref[every, :]
        a = jnp.zeros_like(state)
        b = jnp.zeros_like(state)
        sigma = jnp.zeros_like(state)
        for f in range(FAULTS):
            here = fault == f
            a = jnp.where(here, a_ref[f], a)
            b = jnp.where(here, b_ref[f], b)
            sigma = jnp.where(here, s_ref[f], sigma)
        square = jnp.ones_like(state)
        for k in range(2):
            old = jnp.concatenate(
                [
                    stress_ref[k : k + 1, g * B + h * LANES : g * B + (h + 1) * LANES]
                    for g in range(groups)
                ],
                axis=0,
            )
            new = old + STEP_SIZE * total[:, k * B + h * LANES : k * B + (h + 1) * LANES]
            for g in range(groups):
                out_stress[k : k + 1, g * B + h * LANES : g * B + (h + 1) * LANES] = new[g : g + 1, :]
            square = square + new * new
        z = jnp.sqrt(square) / (a * sigma)
        u = state / a
        rate = jnp.exp(z - u) - jnp.exp(-z - u)
        out_rate[every, :] = rate
        out_state[every, :] = state + STEP_SIZE * b * (jnp.exp(-state / b) - rate)


def finish(a, b, s, parts, stress, state, fault):
    rows = stress.shape[1] // LANES
    new_stress, new_rate, new_state = pl.pallas_call(
        final_kernel,
        out_shape=(
            jax.ShapeDtypeStruct(stress.shape, f32),
            jax.ShapeDtypeStruct((rows, LANES), f32),
            jax.ShapeDtypeStruct((rows, LANES), f32),
        ),
        in_specs=[SMEM, SMEM, SMEM, VMEM, VMEM, VMEM, VMEM],
        out_specs=(VMEM, VMEM, VMEM),
        name="finish",
    )(
        a,
        b,
        s,
        parts.reshape(N_COL, RC_DEV // N_COL, 2 * B),
        stress,
        state.reshape(rows, LANES),
        fault.reshape(rows, LANES),
    )
    return (new_stress, new_rate.reshape(-1), new_state.reshape(-1))


def body(
    slip_rate,
    source_cluster,
    near_kernel,
    near_pattern,
    far_left,
    far_right,
    far_pattern,
    stress,
    state,
    fault_of_row,
    direct_effect,
    evolution_effect,
    normal_stress,
):
    near, left, right = near_kernel[0, 0], far_left[0, 0], far_right[0, 0]
    near_index, far_index = near_pattern[0, 0], far_pattern[0, 0]
    slip = jnp.transpose(slip_rate.reshape(2, CLU_DEV, B), (1, 0, 2))
    row = lax.axis_index("row")
    payload = jnp.concatenate(
        [source_cluster, near_index[1], far_index[1], jnp.zeros((LANES - BLOCKS,), i32)]
    )
    gathered = lax.all_to_all(
        jnp.broadcast_to(payload[None, :], (N_ROW, CLU_DEV + LANES)), "row", 0, 0, tiled=True
    )

    def fetch(rnd):
        info = jnp.stack([row, rnd]).astype(i32)
        req, pos = make_index(info, gathered)
        asked = lax.all_to_all(req, "col", 0, 0, tiled=True)
        reply, over = gather_rows(asked, slip)
        return lax.all_to_all(reply, ("row", "col"), 0, 0, tiled=True), pos, over, info

    x, pos, over, info = fetch(jnp.int32(-1))
    fast = block_sums(info, pos, near_index, far_index, x, near, left, right)

    def more(carry):
        return carry[0] < jnp.where(over[0] > 0, ROUNDS, 0)

    def one_round(carry):
        rnd, total = carry
        x, pos, _, info = fetch(rnd)
        n = jnp.arange(LANES, dtype=i32)
        own = lax.dynamic_slice_in_dim(pos, row, 1, 0)[0]
        rows = jnp.where(active_in(n, rnd)[:, None, None], x[own], 0.0)
        places = jnp.broadcast_to(n[None, :], (N_ROW, LANES))
        part = block_sums(info, places, near_index, far_index, rows, near, left, right)
        return rnd + 1, jnp.where(rnd == 0, 0.0, total) + part

    _, summed = lax.while_loop(more, one_round, (jnp.int32(0), fast))
    parts = lax.all_to_all(summed, "col", 0, 0, tiled=True)
    return finish(
        direct_effect, evolution_effect, normal_stress, parts, stress, state, fault_of_row
    )


def solution(mesh):
    return jax.shard_map(
        body,
        mesh=mesh,
        in_specs=(
            P(None, ("row", "col")),
            P(("row", "col")),
            P("row", "col", None, None, None),
            P("row", "col", None, None),
            P("row", "col", None, None, None),
            P("row", "col", None, None, None),
            P("row", "col", None, None),
            P(None, ("row", "col")),
            P(("row", "col")),
            P(("row", "col")),
            P(),
            P(),
            P(),
        ),
        out_specs=(P(None, ("row", "col")), P(("row", "col")), P(("row", "col"))),
        check_vma=False,
    )
```

time: 273 us -> 95.6 us (0.35)
  waiting for transfers between devices: 156 us -> 34.5 us
  local copies, waits for them, and re-layouts: 38.8 us -> 2.02 us
  matrix products: 22.2 us -> 0 us
  Pallas kernels: 0 us -> 18.6 us
  between operations: 14.5 us -> 0.71 us
  other arithmetic: 15.1 us -> 1.33 us
  blocking collectives: 20.4 us -> 28.2 us
  starting transfers between devices: 6.05 us -> 9.05 us
    psum x1 -> x0, waiting for transfers between devices: 84.7 us -> none  [body(): summed_all = lax.psum(partial_value, 'col')]
    all_gather x1 -> x0, waiting for transfers between devices: 44.6 us -> none  [body(): arrived = lax.all_gather(own_piece, 'row', axis=1, tiled=True)]
    gather x6 -> x0, local copies, waits for them, and re-layouts: 29.7 us -> none  [the longest x1 10.1 us: body(): jnp.take(local_slip, lax.all_to_all(requests.reshape(senders, capacity),...]
    dot_general x6 -> x0, matrix products: 22.2 us -> none  [the longest x1 17.2 us: block_sums(): jnp.einsum('nij,nj->ni', kernel_rows, sources, precision=highest)]
    pallas_call x0 -> x4, Pallas kernels: none -> 18.6 us  [the longest x1 10.9 us: block_sums(): pl.pallas_call(blocks_kernel, grid=(N_ROW,), out_shape=jax.ShapeDtypeStru...]
    select_n x11 -> x0, other arithmetic: 8.38 us -> none  [the longest x2 5.21 us: body(): jnp.take(local_slip, lax.all_to_all(requests.reshape(senders, capacity),...]
    all_to_all x1 -> x2, waiting for transfers between devices: 26.4 us -> 34.5 us  [the longest x1 29.7 us: fetch(): lax.all_to_all(reply, ('row', 'col'), 0, 0, tiled=True)]
    all_to_all x1 -> x2, blocking collectives: 20.4 us -> 28.2 us  [the longest x1 15.5 us: fetch(): asked = lax.all_to_all(req, 'col', 0, 0, tiled=True)]
  transfers between devices with their start and end apart: 3 -> 2, of which waited for: 3 -> 2; matrix products, arithmetic and copies ran while one was open for 1% -> 1% of each run, Pallas kernels for 0% -> 0%
where the time goes in v1:
time: 95.6 us; the launch traced here: 95 us
  waiting for transfers between devices  34.5 us (36%)
  blocking collectives  28.2 us (29%)
  Pallas kernels  18.6 us (19%)
  starting transfers between devices  9.05 us (9%)
  local copies, waits for them, and re-layouts  2.02 us (2%)
  other arithmetic  1.33 us (1%)
    all_to_all x1, waiting for transfers between devices, fetch(): lax.all_to_all(reply, ('row', 'col'), 0, 0, tiled=True)  29.7 us
    all_to_all x1, blocking collectives, fetch(): asked = lax.all_to_all(req, 'col', 0, 0, tiled=True)  15.5 us
    all_to_all x1, blocking collectives, body(): parts = lax.all_to_all(summed, 'col', 0, 0, tiled=True)  12.7 us
    pallas_call x1, Pallas kernels, block_sums(): pl.pallas_call(blocks_kernel, grid=(N_ROW,), out_shape=jax.ShapeDtypeStru...  10.9 us
    all_to_all x1, waiting for transfers between devices, body(): lax.all_to_all(jnp.broadcast_to(payload[None, :], (N_ROW, CLU_DEV + LANES...  4.81 us
    all_to_all x1, starting transfers between devices, fetch(): lax.all_to_all(reply, ('row', 'col'), 0, 0, tiled=True)  4.67 us
    all_to_all x1, starting transfers between devices, body(): lax.all_to_all(jnp.broadcast_to(payload[None, :], (N_ROW, CLU_DEV + LANES...  4.38 us
    pallas_call x1, Pallas kernels, gather_rows(): pl.pallas_call(gather_kernel, out_shape=(jax.ShapeDtypeStruct((N_ROW * N_...  3.76 us
  transfers between devices with their start and end apart: 2, of which 2 were waited for; matrix products, arithmetic and copies ran while one was open for 1% of the time, Pallas kernels for 0%

profile of v1, /device:TPU:0, one launch (start us, length us, event | category | flops | bytes accessed | tf_op | source)
XLA Modules:
  0.0 95.0 jit_solution(12801715021129531384)
XLA Ops:
  0.6 0.7 slice_bitcast_fusion
  1.3 0.7 slice_bitcast_fusion.1
  2.0 0.8 pad_add_fusion.1
  2.8 0.6 broadcast_in_dim.49
  3.4 4.4 %all-to-all-start.2 = ((s32[8,1,640]{2,1,0:T(1,128)}), s32[8,1,640]{2,1,0:T(1,128)S(1)}, u32[]{:S(2)}, u32[]{:S(2)}) async-start(s32[8,1,640]{2,1,0:T(1,128)} %broadcast_in_dim.49), calls=%async_computation.2 | async-start | bytes 40960 | tf_op jit(solution)/shard_map/all_to_all | solution.py:287
  7.8 0.6 pad_add_fusion.2.info_ref
  8.3 4.8 %all-to-all-done.2 = s32[8,1,640]{2,1,0:T(1,128)S(1)} async-done(((s32[8,1,640]{2,1,0:T(1,128)}), s32[8,1,640]{2,1,0:T(1,128)S(1)}, u32[]{:S(2)}, u32[]{:S(2)}) %all-to-all-start.2) | async-done | bytes 20512 | tf_op jit(solution)/shard_map/all_to_all | solution.py:287
  13.2 2.2 %index.8 = (s32[16,128]{1,0:T(8,128)}, s32[8,128]{1,0:T(8,128)}) custom-call(s32[2]{0:T(128)} %pad_add_fusion.2.info_ref, s32[8,640]{1,0:T(8,128)S(1)} %bitcast.56), custom_call_target="tpu_custom_call" | custom-call | tf_op jit(solution)/shard_map/index/pallas_call | solution.py:104
  15.4 15.5 %all_to_all.55 = s32[16,1,128]{2,1,0:T(1,128)} all-to-all(s32[16,1,128]{2,1,0:T(1,128)} %bitcast.67), channel_id=1, replica_groups=mesh['row'=8,'col'=16] {'col'}, dimensions={0} | all-to-all | bytes 16384 | tf_op jit(solution)/shard_map/all_to_all | solution.py:294
  30.9 3.8 %gather.21 = (f32[1024,2,256]{2,1,0:T(2,128)}, s32[1]{0:T(128)}) custom-call(s32[16,128]{1,0:T(8,128)} %bitcast.64, f32[512,2,256]{2,1,0:T(2,128)} %bitcast.18.slip_ref), custom_call_target="tpu_custom_call" | custom-call | tf_op jit(solution)/shard_map/gather/pallas_call | solution.py:128
  34.6 0.0 copy-start.1
  34.6 0.0 copy-start.2
  34.7 0.0 copy-start.6
  34.7 0.0 copy-start.7
  34.7 4.7 %all-to-all-start.4 = ((f32[1024,2,256]{2,1,0:T(2,128)}), f32[1024,2,256]{2,1,0:T(2,128)S(1)}, u32[]{:S(2)}, u32[]{:S(2)}) async-start(f32[1024,2,256]{2,1,0:T(2,128)} %get-tuple-element.245), calls=%async_computation.4 | async-start | bytes 4194304 | tf_op jit(solution)/shard_map/all_to_all | solution.py:296
  39.3 29.7 %all-to-all-done.4.x_ref = f32[1024,2,256]{2,1,0:T(2,128)S(1)} async-done(((f32[1024,2,256]{2,1,0:T(2,128)}), f32[1024,2,256]{2,1,0:T(2,128)S(1)}, u32[]{:S(2)}, u32[]{:S(2)}) %all-to-all-start.4) | async-done | bytes 2097184 | tf_op jit(solution)/shard_map/all_to_all | solution.py:296
  69.1 0.0 copy-done.1
  69.1 0.0 copy-done.2
  69.1 0.0 copy-done.6
  69.1 0.0 copy-done.7
  69.1 10.9 %blocks.8 = f32[128,512]{1,0:T(8,128)} custom-call(s32[2]{0:T(128)S(1)} %copy-done.2, s32[8,128]{1,0:T(8,128)S(1)} %copy-done.1, s32[2,16]{1,0:T(2,128)S(1)} %bitcast.62, s32[2,96]{1,0:T(2,128)S(1)} %bitcast.60, f32[1024,2,256]{2,1,0:T(2,128)S(1)} %all-to-all-done.4.x_ref, f32[16,512,512]{2,1,0:T(8,128)} %bitcast.49, bf16[96,32,512]{2,1,0:T(8,128)(2,1)} %bitcast.51, ...), custom_call_target="tpu_custom_call" | custom-call | tf_op jit(solution)/shard_map/blocks/pallas_call | solution.py:181
  80.0 0.6 while.14
  80.6 12.7 %all_to_all.56.parts_ref = f32[16,8,512]{2,1,0:T(8,128)} all-to-all(f32[16,8,512]{2,1,0:T(8,128)} %bitcast.55), channel_id=1, replica_groups=mesh['row'=8,'col'=16] {'col'}, dimensions={0} | all-to-all | bytes 524288 | tf_op jit(solution)/shard_map/all_to_all | solution.py:315
  93.3 1.7 %finish.1 = (f32[2,2048]{1,0:T(2,128)}, f32[16,128]{1,0:T(8,128)}, f32[16,128]{1,0:T(8,128)}) custom-call(f32[40]{0:T(128)} %a_ref.1, f32[40]{0:T(128)} %b_ref.1, f32[40]{0:T(128)} %s_ref.1, f32[16,8,512]{2,1,0:T(8,128)} %all_to_all.56.parts_ref, f32[2,2048]{1,0:T(2,128)} %stress_ref.1, f32[16,128]{1,0:T(8,128)} %bitcast.65, s32[16,128]{1,0:T(8,128)} %bitcast.66), custom_call_target="tpu_custom_call" | custom-call | tf_op jit(solution)/shard_map/finish/pallas_call | solution.py:243
  (2 shorter events, 0.0 us)
Async XLA Ops:
  3.4 9.8 %all-to-all-start.2 = ((s32[8,1,640]{2,1,0:T(1,128)}), s32[8,1,640]{2,1,0:T(1,128)S(1)}, u32[]{:S(2)}, u32[]{:S(2)}) async-start(s32[8,1,640]{2,1,0:T(1,128)} %broadcast_in_dim.49), calls=%async_computation.2 | async-start | bytes 40960 | tf_op jit(solution)/shard_map/all_to_all | solution.py:287
  34.6 34.4 %copy-start.1 = (s32[8,128]{1,0:T(8,128)S(1)}, s32[8,128]{1,0:T(8,128)}, u32[]{:S(2)}) copy-start(s32[8,128]{1,0:T(8,128)} %get-tuple-element.243.pos_ref) | copy-start | bytes 12292
  34.6 34.4 %copy-start.2 = (s32[2]{0:T(128)S(1)}, s32[2]{0:T(128)}, u32[]{:S(2)}) copy-start(s32[2]{0:T(128)} %pad_add_fusion.2.info_ref) | copy-start | bytes 28
  34.7 34.4 %copy-start.6 = (s32[1,1,2,96]{3,2,1,0:T(2,128)S(1)}, s32[1,1,2,96]{3,2,1,0:T(2,128)}, u32[]{:S(2)}) copy-start(s32[1,1,2,96]{3,2,1,0:T(2,128)} %param.21) | copy-start | bytes 2308
  34.7 34.4 %copy-start.7 = (s32[1,1,2,16]{3,2,1,0:T(2,128)S(1)}, s32[1,1,2,16]{3,2,1,0:T(2,128)}, u32[]{:S(2)}) copy-start(s32[1,1,2,16]{3,2,1,0:T(2,128)} %param.18) | copy-start | bytes 388
  34.7 34.4 %all-to-all-start.4 = ((f32[1024,2,256]{2,1,0:T(2,128)}), f32[1024,2,256]{2,1,0:T(2,128)S(1)}, u32[]{:S(2)}, u32[]{:S(2)}) async-start(f32[1024,2,256]{2,1,0:T(2,128)} %get-tuple-element.245), calls=%async_computation.4 | async-start | bytes 4194304 | tf_op jit(solution)/shard_map/all_to_all | solution.py:296

commit v2 on v1

v2 whole, which is shorter than its diff:
```python
import functools

import functools

import jax
import jax.numpy as jnp
from jax import lax
from jax.experimental import pallas as pl
from jax.experimental.pallas import tpu as pltpu
from jax.sharding import PartitionSpec as P

B = 256
R = 32
CLU_DEV = 512
RC_DEV = 128
NP = 2
FP = 12
N_ROW = 8
N_COL = 16
NEAR = N_ROW * NP
FAR = N_ROW * FP
BLOCKS = NEAR + FAR
LANES = 128
CAP_COL = 24
CAP_ROW = 32
ROUNDS = 56
PIECE_ROWS = 8
FAULTS = 40
STEP_SIZE = 0.25

VMEM = pl.BlockSpec(memory_space=pltpu.VMEM)
SMEM = pl.BlockSpec(memory_space=pltpu.SMEM)
f32 = jnp.float32
bf16 = jnp.bfloat16
i32 = jnp.int32
NT = (((1,), (1,)), ((), ()))
SMALL = pltpu.CompilerParams(vmem_limit_bytes=6 * 1024 * 1024)


def iota(shape, dim):
    return lax.broadcasted_iota(i32, shape, dim)


def exact(x):
    return x.astype(f32).astype(bf16)


def split(x):
    return jnp.concatenate([x >> 8, x & 255], axis=0)


def piece_of(n):
    return jnp.where(n < NEAR, n >> 1, ((n - NEAR) * 43) >> 9)


def active_in(n, rnd):
    if rnd is None:
        return n < BLOCKS
    piece = piece_of(n)
    within = jnp.where(n < NEAR, n & 1, NP + (n - NEAR) - FP * piece)
    of = (rnd * 37) >> 8
    return (n < BLOCKS) & (piece == of) & ((within >> 1) == rnd - 7 * of)


def payload_kernel(table_ref, near_ref, far_ref, out_ref):
    out_ref[...] = jnp.zeros_like(out_ref)
    for r in range(N_ROW):
        out_ref[r, 0:4, :] = table_ref[...]
        out_ref[r, 4:5, 0:NEAR] = near_ref[1:2, :]
        out_ref[r, 5:6, 0:FAR] = far_ref[1:2, :]
        out_ref[r, 6:7, :] = jnp.full((1, LANES), r, i32)


def make_payload(source_cluster, near_index, far_index):
    return pl.pallas_call(
        payload_kernel,
        out_shape=jax.ShapeDtypeStruct((N_ROW, PIECE_ROWS, LANES), i32),
        in_specs=[VMEM, VMEM, VMEM],
        out_specs=VMEM,
        compiler_params=SMALL,
        name="payload",
    )(source_cluster.reshape(4, LANES), near_index, far_index)


def index_kernel(g_ref, *refs):
    req_ref, snd_ref, pos_ref = refs[-3:]
    rnd = refs[0][1] if len(refs) > 3 else None
    rho = g_ref[0, 6:7, :]
    tables = jnp.concatenate([g_ref[:, q, :] for q in range(4)], axis=1)
    n = iota((N_ROW, LANES), 1)
    m = jnp.where(n < NEAR, g_ref[:, 4, :], pltpu.roll(g_ref[:, 5, :], NEAR, 1))
    active = active_in(n, rnd)
    tab = exact(split(tables))
    piece_mask = (iota((N_ROW, LANES), 0) == piece_of(n)).astype(f32)
    place = iota((CLU_DEV, LANES), 0)
    rows = []
    for r in range(N_ROW):
        onehot = exact(place == m[r : r + 1, :])
        found = jnp.dot(tab, onehot, preferred_element_type=f32)
        value = found[0:N_ROW] * 256.0 + found[N_ROW : 2 * N_ROW]
        rows.append(jnp.sum(value * piece_mask, axis=0, keepdims=True))
    gid = jnp.concatenate(rows, axis=0).astype(i32)
    owner = jnp.where(active, gid >> 9, -1)
    owner_row = owner >> 4
    local = gid & (CLU_DEV - 1)
    every = iota((LANES, LANES), 0)
    counts = jnp.zeros((LANES, LANES), f32)
    for r in range(N_ROW):
        counts = counts + (every == owner[r : r + 1, :]).astype(f32)
    most = jnp.max(jnp.sum(counts, axis=1, keepdims=True))
    col_label = iota((N_COL, LANES), 0) + rho * N_COL
    row_label = iota((N_ROW, LANES), 0)
    to_col = jnp.concatenate([(col_label == owner[r : r + 1, :]).astype(f32) for r in range(N_ROW)], axis=0)
    to_row = jnp.concatenate([(row_label == owner_row[r : r + 1, :]).astype(f32) for r in range(N_ROW)], axis=0)
    sub, lane = iota((LANES, LANES), 0), iota((LANES, LANES), 1)
    scan = jnp.concatenate([exact(sub < lane), jnp.ones((LANES, LANES), bf16)], axis=1)
    ahead = jnp.dot(to_col.astype(bf16), scan, preferred_element_type=f32)
    earlier = exact(((sub & (N_COL - 1)) == (lane & (N_COL - 1))) & (sub > lane))
    offset = jnp.dot(earlier, ahead[:, LANES:].astype(bf16), preferred_element_type=f32)
    first = to_col * (ahead[:, :LANES] + offset)
    second = to_row * jnp.dot(to_row.astype(bf16), scan[:, :LANES], preferred_element_type=f32)
    slot1 = jnp.concatenate(
        [jnp.sum(first[r * N_COL : (r + 1) * N_COL], axis=0, keepdims=True) for r in range(N_ROW)], axis=0
    ).astype(i32)
    slot2 = jnp.concatenate(
        [jnp.sum(second[r * N_ROW : (r + 1) * N_ROW], axis=0, keepdims=True) for r in range(N_ROW)], axis=0
    ).astype(i32)
    deepest = jnp.max(jnp.where(active, slot2, 0).astype(f32))
    over = jnp.where((most > CAP_COL) | (deepest >= CAP_ROW), 1, 0)
    pos = jnp.clip(owner_row * CAP_ROW + slot2, 0, N_ROW * CAP_ROW - 1)
    pos_ref[...] = jnp.sum(jnp.where(row_label == rho, pos, 0).astype(f32), axis=0, keepdims=True).astype(i32)
    mine = owner_row == rho
    pos1 = jnp.clip((owner & (N_COL - 1)) * CAP_COL + slot1, 0, N_COL * CAP_COL - 1)
    req = jnp.zeros((2 * N_COL, LANES), f32)
    snd = jnp.zeros((2 * N_ROW, LANES), f32)
    for r in range(N_ROW):
        sel = to_col[r * N_COL : (r + 1) * N_COL] > 0.5
        value = split(jnp.where(sel, local[r : r + 1, :], 0))
        put = exact(sub == jnp.where(slot1[r : r + 1, :] < CAP_COL, slot1[r : r + 1, :], -1))
        req = req + lax.dot_general(exact(value), put, NT, preferred_element_type=f32)
        value = split(jnp.where((row_label == r) & mine[r : r + 1, :], pos1[r : r + 1, :], 0))
        put = exact(sub == jnp.where(slot2[r : r + 1, :] < CAP_ROW, slot2[r : r + 1, :], -1))
        snd = snd + lax.dot_general(exact(value), put, NT, preferred_element_type=f32)
    req = (req[0:N_COL] * 256.0 + req[N_COL : 2 * N_COL]).astype(i32)
    req_ref[...] = jnp.where(iota((N_COL, LANES), 1) == LANES - 1, over, req)
    snd_ref[...] = (snd[0:N_ROW] * 256.0 + snd[N_ROW : 2 * N_ROW]).astype(i32)


def make_index(gathered, ctl):
    return pl.pallas_call(
        index_kernel,
        out_shape=(
            jax.ShapeDtypeStruct((N_COL, LANES), i32),
            jax.ShapeDtypeStruct((N_ROW, LANES), i32),
            jax.ShapeDtypeStruct((1, LANES), i32),
        ),
        in_specs=[VMEM] + [SMEM] * len(ctl),
        out_specs=(VMEM, VMEM, VMEM),
        compiler_params=SMALL,
        name="index",
    )(gathered, *ctl)


def gather_kernel(idx_ref, slip_ref, out_ref, ctl_ref):
    def one_col(c, over):
        for k in range(CAP_COL):
            out_ref[c * CAP_COL + k] = slip_ref[idx_ref[c, k]]
        return jnp.maximum(over, idx_ref[c, LANES - 1])

    ctl_ref[0] = ROUNDS * lax.fori_loop(0, N_COL, one_col, jnp.int32(0))
    ctl_ref[1] = 0


def gather_rows(idx, slip):
    return pl.pallas_call(
        gather_kernel,
        out_shape=(
            jax.ShapeDtypeStruct((N_COL * CAP_COL, 2, B), f32),
            jax.ShapeDtypeStruct((2,), i32),
        ),
        in_specs=[SMEM, VMEM],
        out_specs=(VMEM, SMEM),
        compiler_params=SMALL,
        name="gather",
    )(idx, slip)


def forward_kernel(idx_ref, got_ref, out_ref):
    def one_row(r, _):
        for k in range(CAP_ROW):
            out_ref[r * CAP_ROW + k] = got_ref[idx_ref[r, k]]
        return 0

    lax.fori_loop(0, N_ROW, one_row, 0)


def forward_rows(idx, got):
    return pl.pallas_call(
        forward_kernel,
        out_shape=jax.ShapeDtypeStruct((N_ROW * CAP_ROW, 2, B), f32),
        in_specs=[SMEM, VMEM],
        out_specs=VMEM,
        compiler_params=SMALL,
        name="forward",
    )(idx, got)


def blocks_kernel(
    steps, pos_ref, near_row_ref, far_row_ref, x_ref, near_ref, left_ref, right_ref, out_ref, acc_ref
):
    step = pl.program_id(0) if steps > 1 else 0
    near_here, pieces_here = NEAR // steps, N_ROW // steps

    @pl.when(step == 0)
    def _():
        out_ref[...] = jnp.zeros_like(out_ref)
        acc_ref[...] = jnp.zeros_like(acc_ref)

    chunk = 64
    lane = iota((chunk, LANES), 1)

    def one_near(t, _):
        n = step * near_here + t
        x = x_ref[pos_ref[0, n]]
        x0, x1 = x[0:1, :], x[1:2, :]
        here = lane == near_row_ref[0, n]
        for s in range(0, 2 * B, chunk):
            rows = pl.ds(s, chunk)
            prod = near_ref[t, rows, 0:B] * x0 + near_ref[t, rows, B : 2 * B] * x1
            total = jnp.sum(prod[:, 0:LANES] + prod[:, LANES:B], axis=1, keepdims=True)
            old = acc_ref[rows, :]
            acc_ref[rows, :] = jnp.where(here, old + total, old)
        return 0

    lax.fori_loop(0, near_here, one_near, 0)

    def some_far(p, _):
        for t in range(FP):
            at = p * FP + t
            n = step * pieces_here * FP + at
            x = x_ref[pos_ref[0, NEAR + n]].astype(bf16).astype(f32)
            right = right_ref[at].astype(f32)
            prod = right[:, 0:B] * x[0:1, :] + right[:, B : 2 * B] * x[1:2, :]
            coef = jnp.sum(prod[:, 0:LANES] + prod[:, LANES:B], axis=1, keepdims=True)
            coef = coef.astype(bf16).astype(f32)
            far = jnp.sum(left_ref[at].astype(f32) * coef, axis=0, keepdims=True)
            row = pl.ds(far_row_ref[0, n], 1)
            out_ref[row, :] = out_ref[row, :] + far
        return 0

    lax.fori_loop(0, pieces_here, some_far, 0)

    @pl.when(step == steps - 1)
    def _():
        out_ref[...] = out_ref[...] + acc_ref[...].T


def block_sums(steps, pos, near_index, far_index, x, near, left, right):
    specs = [SMEM, SMEM, SMEM, VMEM, VMEM, VMEM, VMEM]
    out_spec, extra = VMEM, {}
    if steps > 1:
        specs[4:] = [
            pl.BlockSpec((one.shape[0] // steps,) + one.shape[1:], lambda p: (p, 0, 0))
            for one in (near, left, right)
        ]
        specs[3] = pl.BlockSpec(x.shape, lambda p: (0, 0, 0))
        out_spec = pl.BlockSpec((RC_DEV, 2 * B), lambda p: (0, 0))
        extra = {"grid": (steps,)}
    return pl.pallas_call(
        functools.partial(blocks_kernel, steps),
        out_shape=jax.ShapeDtypeStruct((RC_DEV, 2 * B), f32),
        in_specs=specs,
        out_specs=out_spec,
        scratch_shapes=[pltpu.VMEM((2 * B, LANES), f32)],
        compiler_params=pltpu.CompilerParams(vmem_limit_bytes=26 * 1024 * 1024),
        cost_estimate=pl.CostEstimate(
            flops=2 * (near.size + left.size + right.size),
            transcendentals=0,
            bytes_accessed=4 * (near.size + x.size) + 2 * (left.size + right.size),
        ),
        name="blocks" if steps == 1 else "blocks_streamed",
        **extra,
    )(pos, near_index, far_index, x, near, left, right)


def final_kernel(
    a_ref, b_ref, s_ref, parts_ref, stress_ref, state_ref, fault_ref, out_stress, out_rate, out_state
):
    total = parts_ref[0]
    for c in range(1, N_COL):
        total = total + parts_ref[c]
    groups = RC_DEV // N_COL
    for h in range(2):
        every = pl.ds(h, groups, stride=2)
        state = state_ref[every, :]
        fault = fault_ref[every, :]
        a = jnp.zeros_like(state)
        b = jnp.zeros_like(state)
        sigma = jnp.zeros_like(state)
        for f in range(FAULTS):
            here = fault == f
            a = jnp.where(here, a_ref[f], a)
            b = jnp.where(here, b_ref[f], b)
            sigma = jnp.where(here, s_ref[f], sigma)
        square = jnp.ones_like(state)
        for k in range(2):
            old = jnp.concatenate(
                [
                    stress_ref[k : k + 1, g * B + h * LANES : g * B + (h + 1) * LANES]
                    for g in range(groups)
                ],
                axis=0,
            )
            new = old + STEP_SIZE * total[:, k * B + h * LANES : k * B + (h + 1) * LANES]
            for g in range(groups):
                out_stress[k : k + 1, g * B + h * LANES : g * B + (h + 1) * LANES] = new[g : g + 1, :]
            square = square + new * new
        z = jnp.sqrt(square) / (a * sigma)
        u = state / a
        rate = jnp.exp(z - u) - jnp.exp(-z - u)
        out_rate[every, :] = rate
        out_state[every, :] = state + STEP_SIZE * b * (jnp.exp(-state / b) - rate)


def finish(a, b, s, parts, stress, state, fault):
    rows = stress.shape[1] // LANES
    new_stress, new_rate, new_state = pl.pallas_call(
        final_kernel,
        out_shape=(
            jax.ShapeDtypeStruct(stress.shape, f32),
            jax.ShapeDtypeStruct((rows, LANES), f32),
            jax.ShapeDtypeStruct((rows, LANES), f32),
        ),
        in_specs=[SMEM, SMEM, SMEM, VMEM, VMEM, VMEM, VMEM],
        out_specs=(VMEM, VMEM, VMEM),
        compiler_params=SMALL,
        name="finish",
    )(
        a,
        b,
        s,
        parts.reshape(N_COL, RC_DEV // N_COL, 2 * B),
        stress,
        state.reshape(rows, LANES),
        fault.reshape(rows, LANES),
    )
    return (new_stress, new_rate.reshape(-1), new_state.reshape(-1))


def body(
    slip_rate,
    source_cluster,
    near_kernel,
    near_pattern,
    far_left,
    far_right,
    far_pattern,
    stress,
    state,
    fault_of_row,
    direct_effect,
    evolution_effect,
    normal_stress,
):
    near, left, right = near_kernel[0, 0], far_left[0, 0], far_right[0, 0]
    near_index, far_index = near_pattern[0, 0], far_pattern[0, 0]
    slip = jnp.transpose(slip_rate.reshape(2, CLU_DEV, B), (1, 0, 2))
    gathered = lax.all_to_all(
        make_payload(source_cluster, near_index, far_index), "row", 0, 0, tiled=True
    )

    def fetch(*ctl):
        req, snd, pos = make_index(gathered, ctl)
        asked = lax.all_to_all(req, "col", 0, 0, tiled=True)
        reply, now = gather_rows(asked, slip)
        got = lax.all_to_all(reply, "col", 0, 0, tiled=True)
        return lax.all_to_all(forward_rows(snd, got), "row", 0, 0, tiled=True), pos, now

    x, pos, ctl = fetch()
    fast = block_sums(1, pos, near_index, far_index, x, near, left, right)

    def more(carry):
        return carry[0][1] < carry[0][0]

    def one_round(carry):
        ctl, total = carry
        x, pos, _ = fetch(ctl)
        n = jnp.arange(LANES, dtype=i32)
        rows = jnp.where(active_in(n, ctl[1])[:, None, None], x[pos[0]], 0.0)
        rows = jnp.concatenate([rows, jnp.zeros_like(rows)], axis=0)
        part = block_sums(N_ROW, n[None, :], near_index, far_index, rows, near, left, right)
        return ctl + jnp.arange(2, dtype=i32), jnp.where(ctl[1] == 0, 0.0, total) + part

    _, summed = lax.while_loop(more, one_round, (ctl, fast))
    parts = lax.all_to_all(summed, "col", 0, 0, tiled=True)
    return finish(
        direct_effect, evolution_effect, normal_stress, parts, stress, state, fault_of_row
    )


def solution(mesh):
    return jax.shard_map(
        body,
        mesh=mesh,
        in_specs=(
            P(None, ("row", "col")),
            P(("row", "col")),
            P("row", "col", None, None, None),
            P("row", "col", None, None),
            P("row", "col", None, None, None),
            P("row", "col", None, None, None),
            P("row", "col", None, None),
            P(None, ("row", "col")),
            P(("row", "col")),
            P(("row", "col")),
            P(),
            P(),
            P(),
        ),
        out_specs=(P(None, ("row", "col")), P(("row", "col")), P(("row", "col"))),
        check_vma=False,
    )
```

time: 95.6 us -> 88.4 us (0.925)
  blocking collectives: 28.2 us -> 65.8 us
  waiting for transfers between devices: 34.5 us -> 0 us
  starting transfers between devices: 9.05 us -> 0 us
  other arithmetic: 1.33 us -> 0 us
    all_to_all x0 -> x3, blocking collectives: none -> 38.2 us  [the longest x1 15.6 us: fetch(): got = lax.all_to_all(reply, 'col', 0, 0, tiled=True)]
    all_to_all x2 -> x0, waiting for transfers between devices: 34.5 us -> none  [the longest x1 29.7 us: fetch(): lax.all_to_all(reply, ('row', 'col'), 0, 0, tiled=True)]
    all_to_all x2 -> x0, starting transfers between devices: 9.05 us -> none  [the longest x1 4.67 us: fetch(): lax.all_to_all(reply, ('row', 'col'), 0, 0, tiled=True)]
    squeeze x2 -> x0, local copies, waits for them, and re-layouts: 1.37 us -> none  [the longest x1 0.68 us: body(): far_index[1]]
    slice x0 -> x1, local copies, waits for them, and re-layouts: none -> 1.31 us  [more(): return carry[0][1] < carry[0][0]]
    pallas_call x1, Pallas kernels: 2.22 us -> 1.06 us  [make_index(): pl.pallas_call(index_kernel, out_shape=(jax.ShapeDtypeStruct((N_COL, LANE...]
    pallas_call x2 -> x4, Pallas kernels: 14.7 us -> 15.7 us  [the longest x1 11.8 us: block_sums(): pl.pallas_call(functools.partial(blocks_kernel, steps), out_shape=jax.Sha...]
  transfers between devices with their start and end apart: 2 -> 0, of which waited for: 2 -> 0; matrix products, arithmetic and copies ran while one was open for 1% -> 0% of each run, Pallas kernels for 0% -> 0%
where the time goes in v2:
time: 88.4 us; the launch traced here: 87.9 us
  blocking collectives  65.8 us (74%)
  Pallas kernels  18.1 us (20%)
  local copies, waits for them, and re-layouts  2.04 us (2%)
  loops' own time  1.31 us (1%)
    all_to_all x1, blocking collectives, fetch(): got = lax.all_to_all(reply, 'col', 0, 0, tiled=True)  15.6 us
    all_to_all x1, blocking collectives, fetch(): asked = lax.all_to_all(req, 'col', 0, 0, tiled=True)  15.4 us
    all_to_all x1, blocking collectives, fetch(): lax.all_to_all(forward_rows(snd, got), 'row', 0, 0, tiled=True)  12.8 us
    all_to_all x1, blocking collectives, body(): parts = lax.all_to_all(summed, 'col', 0, 0, tiled=True)  12.2 us
    pallas_call x1, Pallas kernels, block_sums(): pl.pallas_call(functools.partial(blocks_kernel, steps), out_shape=jax.Sha...  11.8 us
    all_to_all x1, blocking collectives, body(): lax.all_to_all(make_payload(source_cluster, near_index, far_index), 'row'...  9.76 us
    pallas_call x1, Pallas kernels, gather_rows(): pl.pallas_call(gather_kernel, out_shape=(jax.ShapeDtypeStruct((N_COL * CA...  2.24 us

profile of v2, /device:TPU:0, one launch (start us, length us, event | category | flops | bytes accessed | tf_op | source)
XLA Modules:
  0.0 87.9 jit_solution(6397175437452365288)
XLA Ops:
  0.6 0.0 copy-start.11
  0.6 0.0 copy-start.10
  0.7 0.0 copy-start.3
  0.7 0.7 copy-done.3
  1.3 0.9 payload.1
  2.2 9.8 %all_to_all.63.g_ref = s32[8,8,128]{2,1,0:T(8,128)S(1)} all-to-all(s32[8,8,128]{2,1,0:T(8,128)S(1)} %payload.1), channel_id=1, replica_groups=mesh['row'=8,'col'=16] {'row'}, dimensions={0} | all-to-all | bytes 65536 | tf_op jit(solution)/shard_map/all_to_all | solution.py:368
  12.0 1.1 %index.8 = (s32[16,128]{1,0:T(8,128)S(1)}, s32[8,128]{1,0:T(8,128)S(1)}, s32[1,128]{1,0:T(1,128)S(1)}) custom-call(s32[8,8,128]{2,1,0:T(8,128)S(1)} %all_to_all.63.g_ref), custom_call_target="tpu_custom_call" | custom-call | tf_op jit(solution)/shard_map/index/pallas_call | solution.py:150
  13.0 15.4 %all_to_all.64 = s32[16,1,128]{2,1,0:T(1,128)S(1)} all-to-all(s32[16,1,128]{2,1,0:T(1,128)S(1)} %bitcast.44), channel_id=1, replica_groups=mesh['row'=8,'col'=16] {'col'}, dimensions={0} | all-to-all | bytes 16384 | tf_op jit(solution)/shard_map/all_to_all | solution.py:374
  28.4 2.2 %gather.21 = (f32[384,2,256]{2,1,0:T(2,128)S(1)}, s32[2]{0:T(128)}) custom-call(s32[16,128]{1,0:T(8,128)S(1)} %bitcast.41, f32[512,2,256]{2,1,0:T(2,128)} %bitcast.15.slip_ref), custom_call_target="tpu_custom_call" | custom-call | tf_op jit(solution)/shard_map/gather/pallas_call | solution.py:175
  30.7 15.6 %all_to_all.65.got_ref = f32[384,2,256]{2,1,0:T(2,128)S(1)} all-to-all(f32[384,2,256]{2,1,0:T(2,128)S(1)} %get-tuple-element.189), channel_id=1, replica_groups=mesh['row'=8,'col'=16] {'col'}, dimensions={0} | all-to-all | bytes 1572864 | tf_op jit(solution)/shard_map/all_to_all | solution.py:376
  46.3 0.9 %forward.8 = f32[256,2,256]{2,1,0:T(2,128)S(1)} custom-call(s32[8,128]{1,0:T(8,128)S(1)} %get-tuple-element.188.idx_ref, f32[384,2,256]{2,1,0:T(2,128)S(1)} %all_to_all.65.got_ref), custom_call_target="tpu_custom_call" | custom-call | tf_op jit(solution)/shard_map/forward/pallas_call | solution.py:198
  47.2 12.8 %all_to_all.66.x_ref = f32[256,2,256]{2,1,0:T(2,128)S(1)} all-to-all(f32[256,2,256]{2,1,0:T(2,128)S(1)} %forward.8), channel_id=1, replica_groups=mesh['row'=8,'col'=16] {'row'}, dimensions={0} | all-to-all | bytes 1048576 | tf_op jit(solution)/shard_map/all_to_all | solution.py:377
  60.0 0.0 copy-done.11
  60.0 0.0 copy-done.10
  60.0 0.0 copy-done.7
  60.0 11.8 %blocks.1 = f32[128,512]{1,0:T(8,128)} custom-call(s32[1,128]{1,0:T(1,128)S(1)} %get-tuple-element.187.pos_ref, s32[2,16]{1,0:T(2,128)S(1)} %bitcast.54, s32[2,96]{1,0:T(2,128)S(1)} %bitcast.57, f32[256,2,256]{2,1,0:T(2,128)S(1)} %all_to_all.66.x_ref, f32[16,512,512]{2,1,0:T(8,128)} %bitcast.46, bf16[96,32,512]{2,1,0:T(8,128)(2,1)S(1)} %bitcast.48, ...), custom_call_target="tpu_custom_call" | custom-call | flops 14680064 | bytes 23592960 | tf_op jit(solution)/shard_map/blocks/pallas_call | solution.py:269
  71.8 0.0 copy-start.4
  71.8 0.0 copy-start.5
  71.8 0.0 copy-start.6
  71.8 2.6 %while.14 = (s32[2]{0:T(128)}, f32[128,512]{1,0:T(8,128)}, s32[8,8,128]{2,1,0:T(8,128)S(1)}, f32[512,2,256]{2,1,0:T(2,128)}, s32[2,16]{1,0:T(2,128)S(1)}, /*inde...) while((s32[2]{0:T(128)}, f32[128,512]{1,0:T(8,128)}, ...), condition=%wide.region_1.2_spmd, body=%wide.region_0.1_spmd.sunk | while | flops 14880264 | bytes 31480892 | solution.py:394
  71.8 1.3 %fusion.6 = (s32[1]{0:T(128)}, s32[1]{0:T(128)}) fusion(s32[2]{0:T(128)} %get-tuple-element.223), kind=kLoop, calls=%fused_computation.18.clone | loop fusion | bytes 16 | tf_op jit(solution)/shard_map/while/cond/slice | solution.py:383
  74.5 12.2 %all_to_all.67.parts_ref = f32[16,8,512]{2,1,0:T(8,128)S(1)} all-to-all(f32[16,8,512]{2,1,0:T(8,128)} %bitcast.52), channel_id=1, replica_groups=mesh['row'=8,'col'=16] {'col'}, dimensions={0} | all-to-all | bytes 524288 | tf_op jit(solution)/shard_map/all_to_all | solution.py:395
  86.6 0.0 copy-done.1
  86.7 1.3 %finish.1 = (f32[2,2048]{1,0:T(2,128)}, f32[16,128]{1,0:T(8,128)}, f32[16,128]{1,0:T(8,128)}) custom-call(f32[40]{0:T(128)S(1)} %copy-done.4, f32[40]{0:T(128)S(1)} %copy-done.5, f32[40]{0:T(128)S(1)} %copy-done.6, f32[16,8,512]{2,1,0:T(8,128)S(1)} %all_to_all.67.parts_ref, f32[2,2048]{1,0:T(2,128)S(1)} %copy-done, f32[16,128]{1,0:T(8,128)S(1)} %bitcast.42, ...), custom_call_target="tpu_custom_call" | custom-call | tf_op jit(solution)/shard_map/finish/pallas_call | solution.py:327
  (9 shorter events, 0.0 us)
Async XLA Ops:
  0.6 59.4 %copy-start.11 = (s32[1,1,2,96]{3,2,1,0:T(2,128)S(1)}, s32[1,1,2,96]{3,2,1,0:T(2,128)}, u32[]{:S(2)}) copy-start(s32[1,1,2,96]{3,2,1,0:T(2,128)} %param.21) | copy-start | bytes 2308
  0.6 59.4 %copy-start.10 = (s32[1,1,2,16]{3,2,1,0:T(2,128)S(1)}, s32[1,1,2,16]{3,2,1,0:T(2,128)}, u32[]{:S(2)}) copy-start(s32[1,1,2,16]{3,2,1,0:T(2,128)} %param.18) | copy-start | bytes 388
  0.7 0.7 copy-start.3
  1.3 58.7 %copy-start.7 = (bf16[1,1,96,32,512]{4,3,2,1,0:T(8,128)(2,1)S(1)}, bf16[1,1,96,32,512]{4,3,2,1,0:T(8,128)(2,1)}, u32[]{:S(2)}) copy-start(bf16[1,1,96,32,512]{4,3,2,1,0:T(8,128)(2,1)} %param.19) | copy-start | bytes 9437188
  71.8 14.8 %copy-start = (f32[2,2048]{1,0:T(2,128)S(1)}, f32[2,2048]{1,0:T(2,128)}, u32[]{:S(2)}) copy-start(f32[2,2048]{1,0:T(2,128)} %stress_ref.1) | copy-start | bytes 49156
  71.8 14.8 %copy-start.1 = (f32[2048]{0:T(1024)S(1)}, f32[2048]{0:T(1024)}, u32[]{:S(2)}) copy-start(f32[2048]{0:T(1024)} %param.23) | copy-start | bytes 24580
  71.8 14.8 %copy-start.2 = (s32[2048]{0:T(1024)S(1)}, s32[2048]{0:T(1024)}, u32[]{:S(2)}) copy-start(s32[2048]{0:T(1024)} %param.24) | copy-start | bytes 24580
  71.8 14.8 %copy-start.4 = (f32[40]{0:T(128)S(1)}, f32[40]{0:T(128)}, u32[]{:S(2)}) copy-start(f32[40]{0:T(128)} %a_ref.1) | copy-start | bytes 484
  71.8 14.8 %copy-start.5 = (f32[40]{0:T(128)S(1)}, f32[40]{0:T(128)}, u32[]{:S(2)}) copy-start(f32[40]{0:T(128)} %b_ref.1) | copy-start | bytes 484
  71.8 14.8 %copy-start.6 = (f32[40]{0:T(128)S(1)}, f32[40]{0:T(128)}, u32[]{:S(2)}) copy-start(f32[40]{0:T(128)} %s_ref.1) | copy-start | bytes 484

commit v3 on v2

--- a/solution.py
+++ b/solution.py
@@ -23,6 +23,9 @@
 LANES = 128
 CAP_COL = 24
 CAP_ROW = 32
+HELD_A = 4
+HELD_B = 2
+GROUP = 2
 ROUNDS = 56
 PIECE_ROWS = 8
 FAULTS = 40
@@ -30,11 +33,45 @@
 
 VMEM = pl.BlockSpec(memory_space=pltpu.VMEM)
 SMEM = pl.BlockSpec(memory_space=pltpu.SMEM)
+HBM = pl.BlockSpec(memory_space=pltpu.HBM)
 f32 = jnp.float32
 bf16 = jnp.bfloat16
 i32 = jnp.int32
 NT = (((1,), (1,)), ((), ()))
 SMALL = pltpu.CompilerParams(vmem_limit_bytes=6 * 1024 * 1024)
+
+
+def in_hbm(x):
+    return pltpu.with_memory_space_constraint(x, pltpu.HBM)
+
+
+def call(kernel, ins, specs, outs, out_specs, name, staged=()):
+    count, given, made = len(staged), len(ins), len(outs)
+
+    def run(*refs):
+        held = refs[given + count + made : given + 2 * count + made]
+        copies = [
+            pltpu.make_async_copy(one.at[pl.ds(first, size)], to, done)
+            for one, to, done, (_, first, size) in zip(
+                refs[given : given + count], held, refs[given + 2 * count + made :], staged
+            )
+        ]
+        for copy in copies:
+            copy.start()
+        kernel(*refs[:given], *refs[given + count : given + count + made])
+        for copy in copies:
+            copy.wait()
+
+    return pl.pallas_call(
+        run,
+        out_shape=tuple(outs)
+        + tuple(pltpu.VMEM((size,) + one.shape[1:], one.dtype) for one, _, size in staged),
+        in_specs=list(specs) + [HBM] * count,
+        out_specs=tuple(out_specs) + (VMEM,) * count,
+        scratch_shapes=[pltpu.SemaphoreType.DMA] * count,
+        compiler_params=SMALL,
+        name=name,
+    )(*ins, *(in_hbm(one) for one, _, _ in staged))
 
 
 def iota(shape, dim):
@@ -71,20 +108,21 @@
         out_ref[r, 6:7, :] = jnp.full((1, LANES), r, i32)
 
 
-def make_payload(source_cluster, near_index, far_index):
-    return pl.pallas_call(
+def make_payload(source_cluster, near_index, far_index, staged):
+    return call(
         payload_kernel,
-        out_shape=jax.ShapeDtypeStruct((N_ROW, PIECE_ROWS, LANES), i32),
-        in_specs=[VMEM, VMEM, VMEM],
-        out_specs=VMEM,
-        compiler_params=SMALL,
-        name="payload",
-    )(source_cluster.reshape(4, LANES), near_index, far_index)
+        (source_cluster.reshape(4, LANES), near_index, far_index),
+        [VMEM, VMEM, VMEM],
+        (jax.ShapeDtypeStruct((N_ROW, PIECE_ROWS, LANES), i32),),
+        (VMEM,),
+        "payload",
+        staged,
+    )
 
 
 def index_kernel(g_ref, *refs):
     req_ref, snd_ref, pos_ref = refs[-3:]
-    rnd = refs[0][1] if len(refs) > 3 else None
+    rnd = refs[0][0] if len(refs) > 3 else None
     rho = g_ref[0, 6:7, :]
     tables = jnp.concatenate([g_ref[:, q, :] for q in range(4)], axis=1)
     n = iota((N_ROW, LANES), 1)
@@ -146,43 +184,40 @@
     snd_ref[...] = (snd[0:N_ROW] * 256.0 + snd[N_ROW : 2 * N_ROW]).astype(i32)
 
 
-def make_index(gathered, ctl):
-    return pl.pallas_call(
+def make_index(gathered, done, staged=()):
+    square = jax.ShapeDtypeStruct((N_ROW, LANES), i32)
+    return call(
         index_kernel,
-        out_shape=(
-            jax.ShapeDtypeStruct((N_COL, LANES), i32),
-            jax.ShapeDtypeStruct((N_ROW, LANES), i32),
-            jax.ShapeDtypeStruct((1, LANES), i32),
-        ),
-        in_specs=[VMEM] + [SMEM] * len(ctl),
-        out_specs=(VMEM, VMEM, VMEM),
-        compiler_params=SMALL,
-        name="index",
-    )(gathered, *ctl)
-
-
-def gather_kernel(idx_ref, slip_ref, out_ref, ctl_ref):
+        (gathered, *done),
+        [VMEM] + [SMEM] * len(done),
+        (jax.ShapeDtypeStruct((N_COL, LANES), i32), square, jax.ShapeDtypeStruct((1, LANES), i32)),
+        (VMEM, VMEM, VMEM),
+        "index",
+        staged,
+    )
+
+
+def gather_kernel(idx_ref, slip_ref, out_ref, rounds_ref, done_ref):
     def one_col(c, over):
         for k in range(CAP_COL):
             out_ref[c * CAP_COL + k] = slip_ref[idx_ref[c, k]]
         return jnp.maximum(over, idx_ref[c, LANES - 1])
 
-    ctl_ref[0] = ROUNDS * lax.fori_loop(0, N_COL, one_col, jnp.int32(0))
-    ctl_ref[1] = 0
-
-
-def gather_rows(idx, slip):
-    return pl.pallas_call(
+    rounds_ref[0] = ROUNDS * lax.fori_loop(0, N_COL, one_col, jnp.int32(0))
+    done_ref[0] = 0
+
+
+def gather_rows(idx, slip, staged=()):
+    one = jax.ShapeDtypeStruct((1,), i32)
+    return call(
         gather_kernel,
-        out_shape=(
-            jax.ShapeDtypeStruct((N_COL * CAP_COL, 2, B), f32),
-            jax.ShapeDtypeStruct((2,), i32),
-        ),
-        in_specs=[SMEM, VMEM],
-        out_specs=(VMEM, SMEM),
-        compiler_params=SMALL,
-        name="gather",
-    )(idx, slip)
+        (idx, slip),
+        [SMEM, VMEM],
+        (jax.ShapeDtypeStruct((N_COL * CAP_COL, 2, B), f32), one, one),
+        (VMEM, SMEM, SMEM),
+        "gather",
+        staged,
+    )
 
 
 def forward_kernel(idx_ref, got_ref, out_ref):
@@ -194,93 +229,139 @@
     lax.fori_loop(0, N_ROW, one_row, 0)
 
 
-def forward_rows(idx, got):
+def forward_rows(idx, got, staged=()):
+    return call(
+        forward_kernel,
+        (idx, got),
+        [SMEM, VMEM],
+        (jax.ShapeDtypeStruct((N_ROW * CAP_ROW, 2, B), f32),),
+        (VMEM,),
+        "forward",
+        staged,
+    )
+
+
+CHUNK = 64
+
+
+def add_near(acc_ref, near_ref, at, x, row):
+    x0, x1 = x[0:1, :], x[1:2, :]
+    here = iota((CHUNK, LANES), 1) == row
+    for s in range(0, 2 * B, CHUNK):
+        rows = pl.ds(s, CHUNK)
+        prod = near_ref[at, rows, 0:B] * x0 + near_ref[at, rows, B : 2 * B] * x1
+        total = jnp.sum(prod[:, 0:LANES] + prod[:, LANES:B], axis=1, keepdims=True)
+        old = acc_ref[rows, :]
+        acc_ref[rows, :] = jnp.where(here, old + total, old)
+
+
+def add_far(out_ref, left_ref, right_ref, at, x, row):
+    x = x.astype(bf16).astype(f32)
+    right = right_ref[at].astype(f32)
+    prod = right[:, 0:B] * x[0:1, :] + right[:, B : 2 * B] * x[1:2, :]
+    coef = jnp.sum(prod[:, 0:LANES] + prod[:, LANES:B], axis=1, keepdims=True)
+    coef = coef.astype(bf16).astype(f32)
+    far = jnp.sum(left_ref[at].astype(f32) * coef, axis=0, keepdims=True)
+    rows = pl.ds(row, 1)
+    out_ref[rows, :] = out_ref[rows, :] + far
+
+
+def blocks_kernel(
+    pos_ref, near_row_ref, far_row_ref, x_ref, held_a, held_b, left_ref, right_ref, near_ref,
+    out_ref, acc_ref, rest_ref, sems,
+):
+    first = HELD_A + HELD_B
+    copies = [
+        pltpu.make_async_copy(
+            near_ref.at[pl.ds(first + g * GROUP, GROUP)], rest_ref.at[pl.ds(g * GROUP, GROUP)], sems.at[g]
+        )
+        for g in range((NEAR - first) // GROUP)
+    ]
+    for copy in copies:
+        copy.start()
+    out_ref[...] = jnp.zeros_like(out_ref)
+    acc_ref[...] = jnp.zeros_like(acc_ref)
+
+    def some_far(p, _):
+        for t in range(FP):
+            n = p * FP + t
+            add_far(out_ref, left_ref, right_ref, n, x_ref[pos_ref[0, NEAR + n]], far_row_ref[0, n])
+        return 0
+
+    lax.fori_loop(0, N_ROW, some_far, 0)
+
+    def near_from(ref, base, start, size):
+        def pair(q, _):
+            for t in range(2):
+                at = start + 2 * q + t
+                n = base + at
+                add_near(acc_ref, ref, at, x_ref[pos_ref[0, n]], near_row_ref[0, n])
+            return 0
+
+        lax.fori_loop(0, size // 2, pair, 0)
+
+    near_from(held_a, 0, 0, HELD_A)
+    near_from(held_b, HELD_A, 0, HELD_B)
+    for g, copy in enumerate(copies):
+        copy.wait()
+        near_from(rest_ref, first, g * GROUP, GROUP)
+    out_ref[...] = out_ref[...] + acc_ref[...].T
+
+
+def block_sums(pos, near_index, far_index, x, held_a, held_b, left, right, near):
+    rest = NEAR - HELD_A - HELD_B
     return pl.pallas_call(
-        forward_kernel,
-        out_shape=jax.ShapeDtypeStruct((N_ROW * CAP_ROW, 2, B), f32),
-        in_specs=[SMEM, VMEM],
+        blocks_kernel,
+        out_shape=jax.ShapeDtypeStruct((RC_DEV, 2 * B), f32),
+        in_specs=[SMEM, SMEM, SMEM, VMEM, VMEM, VMEM, VMEM, VMEM, HBM],
         out_specs=VMEM,
-        compiler_params=SMALL,
-        name="forward",
-    )(idx, got)
-
-
-def blocks_kernel(
-    steps, pos_ref, near_row_ref, far_row_ref, x_ref, near_ref, left_ref, right_ref, out_ref, acc_ref
+        scratch_shapes=[
+            pltpu.VMEM((2 * B, LANES), f32),
+            pltpu.VMEM((rest, 2 * B, 2 * B), f32),
+            pltpu.SemaphoreType.DMA((rest // GROUP,)),
+        ],
+        compiler_params=pltpu.CompilerParams(vmem_limit_bytes=24 * 1024 * 1024),
+        name="blocks",
+    )(pos, near_index, far_index, x, held_a, held_b, left, right, in_hbm(near))
+
+
+def round_kernel(
+    pos_ref, near_row_ref, far_row_ref, x_ref, near_ref, left_ref, right_ref, out_ref, acc_ref
 ):
-    step = pl.program_id(0) if steps > 1 else 0
-    near_here, pieces_here = NEAR // steps, N_ROW // steps
-
-    @pl.when(step == 0)
+    p = pl.program_id(0)
+
+    @pl.when(p == 0)
     def _():
         out_ref[...] = jnp.zeros_like(out_ref)
         acc_ref[...] = jnp.zeros_like(acc_ref)
 
-    chunk = 64
-    lane = iota((chunk, LANES), 1)
-
-    def one_near(t, _):
-        n = step * near_here + t
-        x = x_ref[pos_ref[0, n]]
-        x0, x1 = x[0:1, :], x[1:2, :]
-        here = lane == near_row_ref[0, n]
-        for s in range(0, 2 * B, chunk):
-            rows = pl.ds(s, chunk)
-            prod = near_ref[t, rows, 0:B] * x0 + near_ref[t, rows, B : 2 * B] * x1
-            total = jnp.sum(prod[:, 0:LANES] + prod[:, LANES:B], axis=1, keepdims=True)
-            old = acc_ref[rows, :]
-            acc_ref[rows, :] = jnp.where(here, old + total, old)
-        return 0
-
-    lax.fori_loop(0, near_here, one_near, 0)
-
-    def some_far(p, _):
-        for t in range(FP):
-            at = p * FP + t
-            n = step * pieces_here * FP + at
-            x = x_ref[pos_ref[0, NEAR + n]].astype(bf16).astype(f32)
-            right = right_ref[at].astype(f32)
-            prod = right[:, 0:B] * x[0:1, :] + right[:, B : 2 * B] * x[1:2, :]
-            coef = jnp.sum(prod[:, 0:LANES] + prod[:, LANES:B], axis=1, keepdims=True)
-            coef = coef.astype(bf16).astype(f32)
-            far = jnp.sum(left_ref[at].astype(f32) * coef, axis=0, keepdims=True)
-            row = pl.ds(far_row_ref[0, n], 1)
-            out_ref[row, :] = out_ref[row, :] + far
-        return 0
-
-    lax.fori_loop(0, pieces_here, some_far, 0)
-
-    @pl.when(step == steps - 1)
+    for t in range(NP):
+        n = p * NP + t
+        add_near(acc_ref, near_ref, t, x_ref[pos_ref[0, n]], near_row_ref[0, n])
+    for t in range(FP):
+        n = p * FP + t
+        add_far(out_ref, left_ref, right_ref, t, x_ref[pos_ref[0, NEAR + n]], far_row_ref[0, n])
+
+    @pl.when(p == N_ROW - 1)
     def _():
         out_ref[...] = out_ref[...] + acc_ref[...].T
 
 
-def block_sums(steps, pos, near_index, far_index, x, near, left, right):
-    specs = [SMEM, SMEM, SMEM, VMEM, VMEM, VMEM, VMEM]
-    out_spec, extra = VMEM, {}
-    if steps > 1:
-        specs[4:] = [
-            pl.BlockSpec((one.shape[0] // steps,) + one.shape[1:], lambda p: (p, 0, 0))
+def round_sums(pos, near_index, far_index, x, near, left, right):
+    return pl.pallas_call(
+        round_kernel,
+        grid=(N_ROW,),
+        out_shape=jax.ShapeDtypeStruct((RC_DEV, 2 * B), f32),
+        in_specs=[SMEM, SMEM, SMEM, pl.BlockSpec(x.shape, lambda p: (0, 0, 0))]
+        + [
+            pl.BlockSpec((one.shape[0] // N_ROW,) + one.shape[1:], lambda p: (p, 0, 0))
             for one in (near, left, right)
-        ]
-        specs[3] = pl.BlockSpec(x.shape, lambda p: (0, 0, 0))
-        out_spec = pl.BlockSpec((RC_DEV, 2 * B), lambda p: (0, 0))
-        extra = {"grid": (steps,)}
-    return pl.pallas_call(
-        functools.partial(blocks_kernel, steps),
-        out_shape=jax.ShapeDtypeStruct((RC_DEV, 2 * B), f32),
-        in_specs=specs,
-        out_specs=out_spec,
+        ],
+        out_specs=pl.BlockSpec((RC_DEV, 2 * B), lambda p: (0, 0)),
         scratch_shapes=[pltpu.VMEM((2 * B, LANES), f32)],
-        compiler_params=pltpu.CompilerParams(vmem_limit_bytes=26 * 1024 * 1024),
-        cost_estimate=pl.CostEstimate(
-            flops=2 * (near.size + left.size + right.size),
-            transcendentals=0,
-            bytes_accessed=4 * (near.size + x.size) + 2 * (left.size + right.size),
-        ),
-        name="blocks" if steps == 1 else "blocks_streamed",
-        **extra,
-    )(pos, near_index, far_index, x, near, left, right)
+        compiler_params=pltpu.CompilerParams(vmem_limit_bytes=10 * 1024 * 1024),
+        name="round",
+    )(pos, near_index, far_index, x, in_hbm(near), in_hbm(left), in_hbm(right))
 
 
 def final_kernel(
@@ -365,33 +446,39 @@
     near, left, right = near_kernel[0, 0], far_left[0, 0], far_right[0, 0]
     near_index, far_index = near_pattern[0, 0], far_pattern[0, 0]
     slip = jnp.transpose(slip_rate.reshape(2, CLU_DEV, B), (1, 0, 2))
-    gathered = lax.all_to_all(
-        make_payload(source_cluster, near_index, far_index), "row", 0, 0, tiled=True
-    )
-
-    def fetch(*ctl):
-        req, snd, pos = make_index(gathered, ctl)
+    payload, left_held = make_payload(source_cluster, near_index, far_index, ((left, 0, FAR),))
+    gathered = lax.all_to_all(payload, "row", 0, 0, tiled=True)
+
+    def exchange(req, snd, source, staged):
         asked = lax.all_to_all(req, "col", 0, 0, tiled=True)
-        reply, now = gather_rows(asked, slip)
+        reply, rounds, done, *held = gather_rows(asked, source, staged[0])
         got = lax.all_to_all(reply, "col", 0, 0, tiled=True)
-        return lax.all_to_all(forward_rows(snd, got), "row", 0, 0, tiled=True), pos, now
-
-    x, pos, ctl = fetch()
-    fast = block_sums(1, pos, near_index, far_index, x, near, left, right)
+        ready, *more_held = forward_rows(snd, got, staged[1])
+        return lax.all_to_all(ready, "row", 0, 0, tiled=True), rounds, done, *held, *more_held
+
+    req, snd, pos, slip_held, right_held = make_index(
+        gathered, (), ((slip, 0, CLU_DEV), (right, 0, FAR))
+    )
+    x, rounds, done, held_a, held_b = exchange(
+        req, snd, slip_held, (((near, 0, HELD_A),), ((near, HELD_A, HELD_B),))
+    )
+    fast = block_sums(pos, near_index, far_index, x, held_a, held_b, left_held, right_held, near)
+
+    limit = rounds.reshape(())
 
     def more(carry):
-        return carry[0][1] < carry[0][0]
+        return carry[0] < limit
 
     def one_round(carry):
-        ctl, total = carry
-        x, pos, _ = fetch(ctl)
+        k, total = carry
+        req, snd, pos, slip_now = make_index(gathered, (k.reshape(1),), ((slip, 0, CLU_DEV),))
+        x, _, _ = exchange(req, snd, slip_now, ((), ()))
         n = jnp.arange(LANES, dtype=i32)
-        rows = jnp.where(active_in(n, ctl[1])[:, None, None], x[pos[0]], 0.0)
-        rows = jnp.concatenate([rows, jnp.zeros_like(rows)], axis=0)
-        part = block_sums(N_ROW, n[None, :], near_index, far_index, rows, near, left, right)
-        return ctl + jnp.arange(2, dtype=i32), jnp.where(ctl[1] == 0, 0.0, total) + part
-
-    _, summed = lax.while_loop(more, one_round, (ctl, fast))
+        rows = jnp.where(active_in(n, k)[:, None, None], x[pos[0]], 0.0)
+        part = round_sums(n[None, :], near_index, far_index, rows, near, left, right)
+        return k + 1, jnp.where(k == 0, 0.0, total) + part
+
+    _, summed = lax.while_loop(more, one_round, (done.reshape(()), fast))
     parts = lax.all_to_all(summed, "col", 0, 0, tiled=True)
     return finish(
         direct_effect, evolution_effect, normal_stress, parts, stress, state, fault_of_row

time: 88.4 us -> 85.4 us (0.966)
  Pallas kernels: 18.1 us -> 16.7 us
  local copies, waits for them, and re-layouts: 2.04 us -> 0.72 us
    pallas_call x5, Pallas kernels: 16.8 us -> 15.4 us  [the longest x4 10.4 us: call(): pl.pallas_call(run, out_shape=tuple(outs) + tuple((pltpu.VMEM((size,) + o...]
    slice x1 -> x0, local copies, waits for them, and re-layouts: 1.31 us -> none  [more(): return carry[0][1] < carry[0][0]]
where the time goes in v3:
time: 85.4 us; the launch traced here: 84.9 us
  blocking collectives  65.4 us (77%)
  Pallas kernels  16.7 us (20%)
  loops' own time  1.32 us (2%)
    all_to_all x1, blocking collectives, exchange(): got = lax.all_to_all(reply, 'col', 0, 0, tiled=True)  15.6 us
    all_to_all x1, blocking collectives, exchange(): asked = lax.all_to_all(req, 'col', 0, 0, tiled=True)  15.4 us
    all_to_all x1, blocking collectives, exchange(): lax.all_to_all(ready, 'row', 0, 0, tiled=True)  12.8 us
    all_to_all x1, blocking collectives, body(): parts = lax.all_to_all(summed, 'col', 0, 0, tiled=True)  11.9 us
    pallas_call x4, Pallas kernels, call(): pl.pallas_call(run, out_shape=tuple(outs) + tuple((pltpu.VMEM((size,) + o...  10.4 us
    all_to_all x1, blocking collectives, body(): gathered = lax.all_to_all(payload, 'row', 0, 0, tiled=True)  9.63 us
    pallas_call x1, Pallas kernels, block_sums(): pl.pallas_call(blocks_kernel, out_shape=jax.ShapeDtypeStruct((RC_DEV, 2 *...  4.98 us

profile of v3, /device:TPU:0, one launch (start us, length us, event | category | flops | bytes accessed | tf_op | source)
XLA Modules:
  0.0 84.9 jit_solution(14446262646924499532)
XLA Ops:
  0.6 0.0 copy-start.3
  0.6 0.7 copy-done.3
  1.3 2.6 %payload.1 = (s32[8,8,128]{2,1,0:T(8,128)S(1)}, bf16[96,32,512]{2,1,0:T(8,128)(2,1)S(1)}) custom-call(s32[4,128]{1,0:T(4,128)S(1)} %bitcast.45, s32[2,16]{1,0:T(2,128)} %bitcast.57, s32[2,96]{1,0:T(2,128)} %bitcast.60, bf16[96,32,512]{2,1,0:T(8,128)(2,1)} %bitcast.50), custom_call_target="tpu_custom_call" | custom-call | tf_op jit(solution)/shard_map/payload/pallas_call | solution.py:65
  3.9 9.6 %all_to_all.63.refs_0_ = s32[8,8,128]{2,1,0:T(8,128)S(1)} all-to-all(s32[8,8,128]{2,1,0:T(8,128)S(1)} %get-tuple-element.220), channel_id=1, replica_groups=mesh['row'=8,'col'=16] {'row'}, dimensions={0} | all-to-all | bytes 65536 | tf_op jit(solution)/shard_map/all_to_all | solution.py:450
  13.5 2.2 %index.8 = (s32[16,128]{1,0:T(8,128)S(1)}, s32[8,128]{1,0:T(8,128)S(1)}, s32[1,128]{1,0:T(1,128)S(1)}, f32[512,2,256]{2,1,0:T(2,128)S(1)}, bf16[96,32,512]{2,1,0:T(8,128)(2,1)S(1)}) custom-call(s32[8,8,128]{2,1,0:T(8,128)S(1)} %all_to_all.63.refs_0_, f32[512,2,256]{2,1,0:T(2,128)} %bitcast.54, bf16[96,32,512]{2,1,0:T(8,128)(2,1)} %bitcast.52), custom_call_target="tpu_custom_call" | custom-call | tf_op jit(solution)/shard_map/index/pallas_call | solution.py:65
  15.8 15.4 %all_to_all.64 = s32[16,1,128]{2,1,0:T(1,128)S(1)} all-to-all(s32[16,1,128]{2,1,0:T(1,128)S(1)} %bitcast.44), channel_id=1, replica_groups=mesh['row'=8,'col'=16] {'col'}, dimensions={0} | all-to-all | bytes 16384 | tf_op jit(solution)/shard_map/all_to_all | solution.py:453
  31.2 3.4 %gather.21 = (f32[384,2,256]{2,1,0:T(2,128)S(1)}, s32[1]{0:T(128)}, s32[1]{0:T(128)}, f32[4,512,512]{2,1,0:T(8,128)S(1)}) custom-call(s32[16,128]{1,0:T(8,128)S(1)} %bitcast.41, f32[512,2,256]{2,1,0:T(2,128)S(1)} %get-tuple-element.222.refs_1_, f32[16,512,512]{2,1,0:T(8,128)} %bitcast.46), custom_call_target="tpu_custom_call" | custom-call | tf_op jit(solution)/shard_map/gather/pallas_call | solution.py:65
  34.6 15.6 %all_to_all.65.refs_1_ = f32[384,2,256]{2,1,0:T(2,128)S(1)} all-to-all(f32[384,2,256]{2,1,0:T(2,128)S(1)} %get-tuple-element.226), channel_id=1, replica_groups=mesh['row'=8,'col'=16] {'col'}, dimensions={0} | all-to-all | bytes 1572864 | tf_op jit(solution)/shard_map/all_to_all | solution.py:455
  50.2 2.2 %forward.8 = (f32[256,2,256]{2,1,0:T(2,128)S(1)}, f32[2,512,512]{2,1,0:T(8,128)S(1)}) custom-call(s32[8,128]{1,0:T(8,128)S(1)} %get-tuple-element.225.refs_0_, f32[384,2,256]{2,1,0:T(2,128)S(1)} %all_to_all.65.refs_1_, f32[16,512,512]{2,1,0:T(8,128)} %bitcast.47), custom_call_target="tpu_custom_call" | custom-call | tf_op jit(solution)/shard_map/forward/pallas_call | solution.py:65
  52.4 12.8 %all_to_all.66.x_ref = f32[256,2,256]{2,1,0:T(2,128)S(1)} all-to-all(f32[256,2,256]{2,1,0:T(2,128)S(1)} %get-tuple-element.227), channel_id=1, replica_groups=mesh['row'=8,'col'=16] {'row'}, dimensions={0} | all-to-all | bytes 1048576 | tf_op jit(solution)/shard_map/all_to_all | solution.py:457
  65.2 0.0 copy-done.7
  65.2 0.0 copy-done.8
  65.2 5.0 %blocks.1 = f32[128,512]{1,0:T(8,128)S(1)} custom-call(s32[1,128]{1,0:T(1,128)S(1)} %get-tuple-element.224.pos_ref, s32[2,16]{1,0:T(2,128)S(1)} %bitcast.58, s32[2,96]{1,0:T(2,128)S(1)} %bitcast.61, f32[256,2,256]{2,1,0:T(2,128)S(1)} %all_to_all.66.x_ref, f32[4,512,512]{2,1,0:T(8,128)S(1)} %get-tuple-element.228.held_a, ...), custom_call_target="tpu_custom_call" | custom-call | tf_op jit(solution)/shard_map/blocks/pallas_call | solution.py:313
  70.2 0.0 copy-start
  70.2 0.0 copy-start.1
  70.3 0.0 copy-start.2
  70.3 0.0 copy-start.4
  70.3 0.0 copy-start.5
  70.3 0.0 copy-start.6
  70.3 1.3 %while.14 = (s32[]{:T(128)}, f32[128,512]{1,0:T(8,128)S(1)}, s32[]{:T(128)}, s32[8,8,128]{2,1,0:T(8,128)S(1)}, f32[512,2,256]{2,1,0:T(2,128)}, /*index=5*/s32[2,...) while((s32[]{:T(128)}, f32[128,512]{1,0:T(8,128)S(1)}, ...), condition=%wide.region_1.2_spmd, body=%wide.region_0.1_spmd.sunk | while | flops 200199 | bytes 5004279 | solution.py:481
  71.6 11.9 %all_to_all.67.parts_ref = f32[16,8,512]{2,1,0:T(8,128)S(1)} all-to-all(f32[16,8,512]{2,1,0:T(8,128)S(1)} %bitcast.56), channel_id=1, replica_groups=mesh['row'=8,'col'=16] {'col'}, dimensions={0} | all-to-all | bytes 524288 | tf_op jit(solution)/shard_map/all_to_all | solution.py:482
  83.6 0.0 copy-done
  83.6 0.0 copy-done.1
  83.6 1.3 %finish.1 = (f32[2,2048]{1,0:T(2,128)}, f32[16,128]{1,0:T(8,128)}, f32[16,128]{1,0:T(8,128)}) custom-call(f32[40]{0:T(128)S(1)} %copy-done.4, f32[40]{0:T(128)S(1)} %copy-done.5, f32[40]{0:T(128)S(1)} %copy-done.6, f32[16,8,512]{2,1,0:T(8,128)S(1)} %all_to_all.67.parts_ref, f32[2,2048]{1,0:T(2,128)S(1)} %copy-done, f32[16,128]{1,0:T(8,128)S(1)} %bitcast.42, ...), custom_call_target="tpu_custom_call" | custom-call | tf_op jit(solution)/shard_map/finish/pallas_call | solution.py:408
  (6 shorter events, 0.0 us)
Async XLA Ops:
  0.6 0.7 copy-start.3
  50.2 15.0 %copy-start.7 = (s32[1,1,2,16]{3,2,1,0:T(2,128)S(1)}, s32[1,1,2,16]{3,2,1,0:T(2,128)}, u32[]{:S(2)}) copy-start(s32[1,1,2,16]{3,2,1,0:T(2,128)} %param.18) | copy-start | bytes 388
  50.2 15.0 %copy-start.8 = (s32[1,1,2,96]{3,2,1,0:T(2,128)S(1)}, s32[1,1,2,96]{3,2,1,0:T(2,128)}, u32[]{:S(2)}) copy-start(s32[1,1,2,96]{3,2,1,0:T(2,128)} %param.21) | copy-start | bytes 2308
  70.2 13.3 %copy-start = (f32[2,2048]{1,0:T(2,128)S(1)}, f32[2,2048]{1,0:T(2,128)}, u32[]{:S(2)}) copy-start(f32[2,2048]{1,0:T(2,128)} %stress_ref.1) | copy-start | bytes 49156
  70.2 13.3 %copy-start.1 = (f32[2048]{0:T(1024)S(1)}, f32[2048]{0:T(1024)}, u32[]{:S(2)}) copy-start(f32[2048]{0:T(1024)} %param.23) | copy-start | bytes 24580
  70.3 13.3 %copy-start.2 = (s32[2048]{0:T(1024)S(1)}, s32[2048]{0:T(1024)}, u32[]{:S(2)}) copy-start(s32[2048]{0:T(1024)} %param.24) | copy-start | bytes 24580
  70.3 13.3 %copy-start.4 = (f32[40]{0:T(128)S(1)}, f32[40]{0:T(128)}, u32[]{:S(2)}) copy-start(f32[40]{0:T(128)} %a_ref.1) | copy-start | bytes 484
  70.3 13.3 %copy-start.5 = (f32[40]{0:T(128)S(1)}, f32[40]{0:T(128)}, u32[]{:S(2)}) copy-start(f32[40]{0:T(128)} %b_ref.1) | copy-start | bytes 484
  70.3 13.3 %copy-start.6 = (f32[40]{0:T(128)S(1)}, f32[40]{0:T(128)}, u32[]{:S(2)}) copy-start(f32[40]{0:T(128)} %s_ref.1) | copy-start | bytes 484

commit v4 on v3

--- a/solution.py
+++ b/solution.py
@@ -23,9 +23,8 @@
 LANES = 128
 CAP_COL = 24
 CAP_ROW = 32
-HELD_A = 4
-HELD_B = 2
 GROUP = 2
+HALVES = 2
 ROUNDS = 56
 PIECE_ROWS = 8
 FAULTS = 40
@@ -90,13 +89,15 @@
     return jnp.where(n < NEAR, n >> 1, ((n - NEAR) * 43) >> 9)
 
 
-def active_in(n, rnd):
-    if rnd is None:
+def active_in(n, ctl=None):
+    if ctl is None:
         return n < BLOCKS
+    rnd, rounds = ctl
     piece = piece_of(n)
     within = jnp.where(n < NEAR, n & 1, NP + (n - NEAR) - FP * piece)
     of = (rnd * 37) >> 8
-    return (n < BLOCKS) & (piece == of) & ((within >> 1) == rnd - 7 * of)
+    pair = (piece == of) & ((within >> 1) == rnd - 7 * of)
+    return (n < BLOCKS) & (((rounds == HALVES) & ((piece >> 2) == rnd)) | ((rounds != HALVES) & pair))
 
 
 def payload_kernel(table_ref, near_ref, far_ref, out_ref):
@@ -108,26 +109,25 @@
         out_ref[r, 6:7, :] = jnp.full((1, LANES), r, i32)
 
 
-def make_payload(source_cluster, near_index, far_index, staged):
+def make_payload(source_cluster, near_index, far_index):
     return call(
         payload_kernel,
-        (source_cluster.reshape(4, LANES), near_index, far_index),
+        [in_hbm(one) for one in (source_cluster.reshape(4, LANES), near_index, far_index)],
         [VMEM, VMEM, VMEM],
         (jax.ShapeDtypeStruct((N_ROW, PIECE_ROWS, LANES), i32),),
         (VMEM,),
         "payload",
-        staged,
-    )
+    )[0]
 
 
 def index_kernel(g_ref, *refs):
     req_ref, snd_ref, pos_ref = refs[-3:]
-    rnd = refs[0][0] if len(refs) > 3 else None
+    ctl = (refs[0][0] - 1, refs[1][0]) if len(refs) > 3 else None
     rho = g_ref[0, 6:7, :]
     tables = jnp.concatenate([g_ref[:, q, :] for q in range(4)], axis=1)
     n = iota((N_ROW, LANES), 1)
     m = jnp.where(n < NEAR, g_ref[:, 4, :], pltpu.roll(g_ref[:, 5, :], NEAR, 1))
-    active = active_in(n, rnd)
+    active = active_in(n, ctl)
     tab = exact(split(tables))
     piece_mask = (iota((N_ROW, LANES), 0) == piece_of(n)).astype(f32)
     place = iota((CLU_DEV, LANES), 0)
@@ -145,7 +145,7 @@
     counts = jnp.zeros((LANES, LANES), f32)
     for r in range(N_ROW):
         counts = counts + (every == owner[r : r + 1, :]).astype(f32)
-    most = jnp.max(jnp.sum(counts, axis=1, keepdims=True))
+    early = (piece_of(iota((1, LANES), 1)) < N_ROW // 2).astype(f32)
     col_label = iota((N_COL, LANES), 0) + rho * N_COL
     row_label = iota((N_ROW, LANES), 0)
     to_col = jnp.concatenate([(col_label == owner[r : r + 1, :]).astype(f32) for r in range(N_ROW)], axis=0)
@@ -163,8 +163,12 @@
     slot2 = jnp.concatenate(
         [jnp.sum(second[r * N_ROW : (r + 1) * N_ROW], axis=0, keepdims=True) for r in range(N_ROW)], axis=0
     ).astype(i32)
-    deepest = jnp.max(jnp.where(active, slot2, 0).astype(f32))
-    over = jnp.where((most > CAP_COL) | (deepest >= CAP_ROW), 1, 0)
+    fits = [
+        (jnp.max(jnp.sum(counts * part, axis=1, keepdims=True)) <= CAP_COL)
+        & (jnp.max(jnp.sum(to_row * part, axis=1, keepdims=True)) <= CAP_ROW)
+        for part in (jnp.ones((1, LANES), f32), early, 1.0 - early)
+    ]
+    over = jnp.where(fits[0], 0, jnp.where(fits[1] & fits[2], 1, 2))
     pos = jnp.clip(owner_row * CAP_ROW + slot2, 0, N_ROW * CAP_ROW - 1)
     pos_ref[...] = jnp.sum(jnp.where(row_label == rho, pos, 0).astype(f32), axis=0, keepdims=True).astype(i32)
     mine = owner_row == rho
@@ -184,30 +188,32 @@
     snd_ref[...] = (snd[0:N_ROW] * 256.0 + snd[N_ROW : 2 * N_ROW]).astype(i32)
 
 
-def make_index(gathered, done, staged=()):
+def make_index(gathered, slip, ctl=()):
     square = jax.ShapeDtypeStruct((N_ROW, LANES), i32)
     return call(
         index_kernel,
-        (gathered, *done),
-        [VMEM] + [SMEM] * len(done),
+        (gathered, *ctl),
+        [VMEM] + [SMEM] * len(ctl),
         (jax.ShapeDtypeStruct((N_COL, LANES), i32), square, jax.ShapeDtypeStruct((1, LANES), i32)),
         (VMEM, VMEM, VMEM),
         "index",
-        staged,
+        ((slip, 0, CLU_DEV),),
     )
 
 
-def gather_kernel(idx_ref, slip_ref, out_ref, rounds_ref, done_ref):
+def gather_kernel(idx_ref, slip_ref, out_ref, rounds_ref, to_do_ref):
     def one_col(c, over):
         for k in range(CAP_COL):
             out_ref[c * CAP_COL + k] = slip_ref[idx_ref[c, k]]
         return jnp.maximum(over, idx_ref[c, LANES - 1])
 
-    rounds_ref[0] = ROUNDS * lax.fori_loop(0, N_COL, one_col, jnp.int32(0))
-    done_ref[0] = 0
-
-
-def gather_rows(idx, slip, staged=()):
+    over = lax.fori_loop(0, N_COL, one_col, jnp.int32(0))
+    rounds = jnp.where(over == 0, 0, jnp.where(over == 1, HALVES, ROUNDS))
+    rounds_ref[0] = rounds
+    to_do_ref[0] = rounds
+
+
+def gather_rows(idx, slip):
     one = jax.ShapeDtypeStruct((1,), i32)
     return call(
         gather_kernel,
@@ -216,7 +222,6 @@
         (jax.ShapeDtypeStruct((N_COL * CAP_COL, 2, B), f32), one, one),
         (VMEM, SMEM, SMEM),
         "gather",
-        staged,
     )
 
 
@@ -229,7 +234,7 @@
     lax.fori_loop(0, N_ROW, one_row, 0)
 
 
-def forward_rows(idx, got, staged=()):
+def forward_rows(idx, got):
     return call(
         forward_kernel,
         (idx, got),
@@ -237,8 +242,7 @@
         (jax.ShapeDtypeStruct((N_ROW * CAP_ROW, 2, B), f32),),
         (VMEM,),
         "forward",
-        staged,
-    )
+    )[0]
 
 
 CHUNK = 64
@@ -267,17 +271,23 @@
 
 
 def blocks_kernel(
-    pos_ref, near_row_ref, far_row_ref, x_ref, held_a, held_b, left_ref, right_ref, near_ref,
-    out_ref, acc_ref, rest_ref, sems,
+    pos_ref, near_row_ref, far_row_ref, x_ref, left_ref, right_hbm, near_hbm,
+    out_ref, acc_ref, right_ref, near_ref, right_sems, near_sems,
 ):
-    first = HELD_A + HELD_B
-    copies = [
+    half = FAR // 2
+    right_copies = [
         pltpu.make_async_copy(
-            near_ref.at[pl.ds(first + g * GROUP, GROUP)], rest_ref.at[pl.ds(g * GROUP, GROUP)], sems.at[g]
+            right_hbm.at[pl.ds(g * half, half)], right_ref.at[pl.ds(g * half, half)], right_sems.at[g]
         )
-        for g in range((NEAR - first) // GROUP)
+        for g in range(2)
     ]
-    for copy in copies:
+    near_copies = [
+        pltpu.make_async_copy(
+            near_hbm.at[pl.ds(g * GROUP, GROUP)], near_ref.at[pl.ds(g * GROUP, GROUP)], near_sems.at[g]
+        )
+        for g in range(NEAR // GROUP)
+    ]
+    for copy in right_copies + near_copies:
         copy.start()
     out_ref[...] = jnp.zeros_like(out_ref)
     acc_ref[...] = jnp.zeros_like(acc_ref)
@@ -288,41 +298,53 @@
             add_far(out_ref, left_ref, right_ref, n, x_ref[pos_ref[0, NEAR + n]], far_row_ref[0, n])
         return 0
 
-    lax.fori_loop(0, N_ROW, some_far, 0)
-
-    def near_from(ref, base, start, size):
-        def pair(q, _):
-            for t in range(2):
-                at = start + 2 * q + t
-                n = base + at
-                add_near(acc_ref, ref, at, x_ref[pos_ref[0, n]], near_row_ref[0, n])
-            return 0
-
-        lax.fori_loop(0, size // 2, pair, 0)
-
-    near_from(held_a, 0, 0, HELD_A)
-    near_from(held_b, HELD_A, 0, HELD_B)
-    for g, copy in enumerate(copies):
+    for g, copy in enumerate(right_copies):
         copy.wait()
-        near_from(rest_ref, first, g * GROUP, GROUP)
+        lax.fori_loop(g * N_ROW // 2, (g + 1) * N_ROW // 2, some_far, 0)
+    for g, copy in enumerate(near_copies):
+        copy.wait()
+        for n in range(g * GROUP, (g + 1) * GROUP):
+            add_near(acc_ref, near_ref, n, x_ref[pos_ref[0, n]], near_row_ref[0, n])
     out_ref[...] = out_ref[...] + acc_ref[...].T
 
 
-def block_sums(pos, near_index, far_index, x, held_a, held_b, left, right, near):
-    rest = NEAR - HELD_A - HELD_B
+def block_sums(pos, near_index, far_index, x, left, right, near):
     return pl.pallas_call(
         blocks_kernel,
         out_shape=jax.ShapeDtypeStruct((RC_DEV, 2 * B), f32),
-        in_specs=[SMEM, SMEM, SMEM, VMEM, VMEM, VMEM, VMEM, VMEM, HBM],
+        in_specs=[SMEM, SMEM, SMEM, VMEM, VMEM, HBM, HBM],
         out_specs=VMEM,
         scratch_shapes=[
             pltpu.VMEM((2 * B, LANES), f32),
-            pltpu.VMEM((rest, 2 * B, 2 * B), f32),
-            pltpu.SemaphoreType.DMA((rest // GROUP,)),
+            pltpu.VMEM(right.shape, bf16),
+            pltpu.VMEM(near.shape, f32),
+            pltpu.SemaphoreType.DMA((2,)),
+            pltpu.SemaphoreType.DMA((NEAR // GROUP,)),
         ],
-        compiler_params=pltpu.CompilerParams(vmem_limit_bytes=24 * 1024 * 1024),
+        compiler_params=pltpu.CompilerParams(vmem_limit_bytes=28 * 1024 * 1024),
         name="blocks",
-    )(pos, near_index, far_index, x, held_a, held_b, left, right, in_hbm(near))
+    )(pos, near_index, far_index, x, left, in_hbm(right), in_hbm(near))
+
+
+def pick_kernel(to_do_ref, rounds_ref, pos_ref, x_ref, out_ref):
+    def one(n, _):
+        taken = active_in(n, (to_do_ref[0] - 1, rounds_ref[0]))
+        x = x_ref[pos_ref[0, n]]
+        out_ref[n] = jnp.where(taken, x, jnp.zeros_like(x))
+        return 0
+
+    lax.fori_loop(0, LANES, one, 0)
+
+
+def pick_rows(to_do, rounds, pos, x):
+    return call(
+        pick_kernel,
+        (to_do, rounds, pos, x),
+        [SMEM, SMEM, SMEM, VMEM],
+        (jax.ShapeDtypeStruct((LANES, 2, B), f32),),
+        (VMEM,),
+        "pick",
+    )[0]
 
 
 def round_kernel(
@@ -446,39 +468,30 @@
     near, left, right = near_kernel[0, 0], far_left[0, 0], far_right[0, 0]
     near_index, far_index = near_pattern[0, 0], far_pattern[0, 0]
     slip = jnp.transpose(slip_rate.reshape(2, CLU_DEV, B), (1, 0, 2))
-    payload, left_held = make_payload(source_cluster, near_index, far_index, ((left, 0, FAR),))
-    gathered = lax.all_to_all(payload, "row", 0, 0, tiled=True)
-
-    def exchange(req, snd, source, staged):
+    gathered = lax.all_to_all(
+        make_payload(source_cluster, near_index, far_index), "row", 0, 0, tiled=True
+    )
+
+    def fetch(*ctl):
+        req, snd, pos, slip_held = make_index(gathered, slip, ctl)
         asked = lax.all_to_all(req, "col", 0, 0, tiled=True)
-        reply, rounds, done, *held = gather_rows(asked, source, staged[0])
+        reply, rounds, to_do = gather_rows(asked, slip_held)
         got = lax.all_to_all(reply, "col", 0, 0, tiled=True)
-        ready, *more_held = forward_rows(snd, got, staged[1])
-        return lax.all_to_all(ready, "row", 0, 0, tiled=True), rounds, done, *held, *more_held
-
-    req, snd, pos, slip_held, right_held = make_index(
-        gathered, (), ((slip, 0, CLU_DEV), (right, 0, FAR))
-    )
-    x, rounds, done, held_a, held_b = exchange(
-        req, snd, slip_held, (((near, 0, HELD_A),), ((near, HELD_A, HELD_B),))
-    )
-    fast = block_sums(pos, near_index, far_index, x, held_a, held_b, left_held, right_held, near)
-
-    limit = rounds.reshape(())
-
-    def more(carry):
-        return carry[0] < limit
+        return lax.all_to_all(forward_rows(snd, got), "row", 0, 0, tiled=True), pos, rounds, to_do
+
+    x, pos, rounds, to_do = fetch()
+    fast = block_sums(pos, near_index, far_index, x, left, right, near)
 
     def one_round(carry):
-        k, total = carry
-        req, snd, pos, slip_now = make_index(gathered, (k.reshape(1),), ((slip, 0, CLU_DEV),))
-        x, _, _ = exchange(req, snd, slip_now, ((), ()))
-        n = jnp.arange(LANES, dtype=i32)
-        rows = jnp.where(active_in(n, k)[:, None, None], x[pos[0]], 0.0)
-        part = round_sums(n[None, :], near_index, far_index, rows, near, left, right)
-        return k + 1, jnp.where(k == 0, 0.0, total) + part
-
-    _, summed = lax.while_loop(more, one_round, (done.reshape(()), fast))
+        to_do, total = carry
+        now = to_do.reshape(1)
+        x, pos, _, _ = fetch(now, rounds)
+        rows = pick_rows(now, rounds, pos, x)
+        n = jnp.arange(LANES, dtype=i32)[None, :]
+        part = round_sums(n, near_index, far_index, rows, near, left, right)
+        return to_do - 1, jnp.where(to_do == rounds[0], 0.0, total) + part
+
+    _, summed = lax.while_loop(lambda carry: carry[0] > 0, one_round, (to_do.reshape(()), fast))
     parts = lax.all_to_all(summed, "col", 0, 0, tiled=True)
     return finish(
         direct_effect, evolution_effect, normal_stress, parts, stress, state, fault_of_row

time: 85.4 us -> 82.9 us (0.971)
  Pallas kernels: 16.7 us -> 15.5 us
    pallas_call x4, Pallas kernels: 10.4 us -> 4.7 us  [call(): pl.pallas_call(run, out_shape=tuple(outs) + tuple((pltpu.VMEM((size,) + o...]
    pallas_call x1, Pallas kernels: 4.98 us -> 9.53 us  [block_sums(): pl.pallas_call(blocks_kernel, out_shape=jax.ShapeDtypeStruct((RC_DEV, 2 *...]
where the time goes in v4:
time: 82.9 us; the launch traced here: 82.6 us
  blocking collectives  65.5 us (79%)
  Pallas kernels  15.5 us (19%)
    all_to_all x1, blocking collectives, fetch(): got = lax.all_to_all(reply, 'col', 0, 0, tiled=True)  15.6 us
    all_to_all x1, blocking collectives, fetch(): asked = lax.all_to_all(req, 'col', 0, 0, tiled=True)  15.4 us
    all_to_all x1, blocking collectives, fetch(): lax.all_to_all(forward_rows(snd, got), 'row', 0, 0, tiled=True)  12.8 us
    all_to_all x1, blocking collectives, body(): parts = lax.all_to_all(summed, 'col', 0, 0, tiled=True)  11.9 us
    all_to_all x1, blocking collectives, body(): lax.all_to_all(make_payload(source_cluster, near_index, far_index), 'row'...  9.76 us
    pallas_call x1, Pallas kernels, block_sums(): pl.pallas_call(blocks_kernel, out_shape=jax.ShapeDtypeStruct((RC_DEV, 2 *...  9.53 us
    pallas_call x4, Pallas kernels, call(): pl.pallas_call(run, out_shape=tuple(outs) + tuple((pltpu.VMEM((size,) + o...  4.7 us

profile of v4, /device:TPU:0, one launch (start us, length us, event | category | flops | bytes accessed | tf_op | source)
XLA Modules:
  0.0 82.6 jit_solution(15271854669034410116)
XLA Ops:
  0.6 0.0 copy-start.7
  0.6 0.0 copy-start.8
  0.7 0.0 copy-start.6
  0.7 0.9 %payload.1 = s32[8,8,128]{2,1,0:T(8,128)S(1)} custom-call(s32[4,128]{1,0:T(4,128)} %bitcast.54, s32[2,16]{1,0:T(2,128)} %bitcast.48, s32[2,96]{1,0:T(2,128)} %bitcast.51), custom_call_target="tpu_custom_call" | custom-call | tf_op jit(solution)/shard_map/payload/pallas_call | solution.py:64
  1.5 9.8 %all_to_all.57.refs_0_ = s32[8,8,128]{2,1,0:T(8,128)S(1)} all-to-all(s32[8,8,128]{2,1,0:T(8,128)S(1)} %payload.1), channel_id=1, replica_groups=mesh['row'=8,'col'=16] {'row'}, dimensions={0} | all-to-all | bytes 65536 | tf_op jit(solution)/shard_map/all_to_all | solution.py:471
  11.3 1.2 %index.5 = (s32[16,128]{1,0:T(8,128)S(1)}, s32[8,128]{1,0:T(8,128)S(1)}, s32[1,128]{1,0:T(1,128)S(1)}, f32[512,2,256]{2,1,0:T(2,128)S(1)}) custom-call(s32[8,8,128]{2,1,0:T(8,128)S(1)} %all_to_all.57.refs_0_, f32[512,2,256]{2,1,0:T(2,128)} %bitcast.45), custom_call_target="tpu_custom_call" | custom-call | tf_op jit(solution)/shard_map/index/pallas_call | solution.py:64
  12.6 15.4 %all_to_all.58 = s32[16,1,128]{2,1,0:T(1,128)S(1)} all-to-all(s32[16,1,128]{2,1,0:T(1,128)S(1)} %bitcast.38), channel_id=1, replica_groups=mesh['row'=8,'col'=16] {'col'}, dimensions={0} | all-to-all | bytes 16384 | tf_op jit(solution)/shard_map/all_to_all | solution.py:477
  28.0 1.7 %gather.5 = (f32[384,2,256]{2,1,0:T(2,128)S(1)}, s32[1]{0:T(128)}, s32[1]{0:T(128)}) custom-call(s32[16,128]{1,0:T(8,128)S(1)} %bitcast.35, f32[512,2,256]{2,1,0:T(2,128)S(1)} %get-tuple-element.136.refs_1_), custom_call_target="tpu_custom_call" | custom-call | tf_op jit(solution)/shard_map/gather/pallas_call | solution.py:64
  29.7 15.6 %all_to_all.59.refs_1_ = f32[384,2,256]{2,1,0:T(2,128)S(1)} all-to-all(f32[384,2,256]{2,1,0:T(2,128)S(1)} %get-tuple-element.140), channel_id=1, replica_groups=mesh['row'=8,'col'=16] {'col'}, dimensions={0} | all-to-all | bytes 1572864 | tf_op jit(solution)/shard_map/all_to_all | solution.py:479
  45.3 0.9 %forward.5 = f32[256,2,256]{2,1,0:T(2,128)S(1)} custom-call(s32[8,128]{1,0:T(8,128)S(1)} %get-tuple-element.139.refs_0_, f32[384,2,256]{2,1,0:T(2,128)S(1)} %all_to_all.59.refs_1_), custom_call_target="tpu_custom_call" | custom-call | tf_op jit(solution)/shard_map/forward/pallas_call | solution.py:64
  46.2 12.8 %all_to_all.60.x_ref = f32[256,2,256]{2,1,0:T(2,128)S(1)} all-to-all(f32[256,2,256]{2,1,0:T(2,128)S(1)} %forward.5), channel_id=1, replica_groups=mesh['row'=8,'col'=16] {'row'}, dimensions={0} | all-to-all | bytes 1048576 | tf_op jit(solution)/shard_map/all_to_all | solution.py:480
  59.0 0.0 copy-done.7
  59.0 0.0 copy-done.6
  59.0 9.5 %blocks.1 = f32[128,512]{1,0:T(8,128)S(1)} custom-call(s32[1,128]{1,0:T(1,128)S(1)} %get-tuple-element.138.pos_ref, s32[2,16]{1,0:T(2,128)S(1)} %bitcast.49, s32[2,96]{1,0:T(2,128)S(1)} %bitcast.52, f32[256,2,256]{2,1,0:T(2,128)S(1)} %all_to_all.60.x_ref, bf16[96,32,512]{2,1,0:T(8,128)(2,1)S(1)} %bitcast.42, bf16[96,32,512]{2,1,0:T(8,128)(2,1)} %bitcast.43, ...), custom_call_target="tpu_custom_call" | custom-call | tf_op jit(solution)/shard_map/blocks/pallas_call | solution.py:312
  68.5 0.0 copy-start
  68.5 0.0 copy-start.1
  68.6 0.0 copy-start.2
  68.6 0.0 copy-start.3
  68.6 0.0 copy-start.4
  68.6 0.0 copy-start.5
  68.6 0.7 while.12
  69.3 11.9 %all_to_all.61.parts_ref = f32[16,8,512]{2,1,0:T(8,128)S(1)} all-to-all(f32[16,8,512]{2,1,0:T(8,128)S(1)} %bitcast.47), channel_id=1, replica_groups=mesh['row'=8,'col'=16] {'col'}, dimensions={0} | all-to-all | bytes 524288 | tf_op jit(solution)/shard_map/all_to_all | solution.py:495
  81.2 0.0 copy-done
  81.3 1.3 %finish.1 = (f32[2,2048]{1,0:T(2,128)}, f32[16,128]{1,0:T(8,128)}, f32[16,128]{1,0:T(8,128)}) custom-call(f32[40]{0:T(128)S(1)} %copy-done.3, f32[40]{0:T(128)S(1)} %copy-done.4, f32[40]{0:T(128)S(1)} %copy-done.5, f32[16,8,512]{2,1,0:T(8,128)S(1)} %all_to_all.61.parts_ref, f32[2,2048]{1,0:T(2,128)S(1)} %copy-done, f32[16,128]{1,0:T(8,128)S(1)} %bitcast.36, ...), custom_call_target="tpu_custom_call" | custom-call | tf_op jit(solution)/shard_map/finish/pallas_call | solution.py:430
  (6 shorter events, 0.0 us)
Async XLA Ops:
  0.6 58.4 %copy-start.7 = (s32[1,1,2,16]{3,2,1,0:T(2,128)S(1)}, s32[1,1,2,16]{3,2,1,0:T(2,128)}, u32[]{:S(2)}) copy-start(s32[1,1,2,16]{3,2,1,0:T(2,128)} %param.18) | copy-start | bytes 388
  0.6 58.4 %copy-start.8 = (s32[1,1,2,96]{3,2,1,0:T(2,128)S(1)}, s32[1,1,2,96]{3,2,1,0:T(2,128)}, u32[]{:S(2)}) copy-start(s32[1,1,2,96]{3,2,1,0:T(2,128)} %param.21) | copy-start | bytes 2308
  0.7 58.3 %copy-start.6 = (bf16[1,1,96,32,512]{4,3,2,1,0:T(8,128)(2,1)S(1)}, bf16[1,1,96,32,512]{4,3,2,1,0:T(8,128)(2,1)}, u32[]{:S(2)}) copy-start(bf16[1,1,96,32,512]{4,3,2,1,0:T(8,128)(2,1)} %param.19) | copy-start | bytes 9437188
  68.5 12.7 %copy-start = (f32[2,2048]{1,0:T(2,128)S(1)}, f32[2,2048]{1,0:T(2,128)}, u32[]{:S(2)}) copy-start(f32[2,2048]{1,0:T(2,128)} %stress_ref.1) | copy-start | bytes 49156
  68.5 12.7 %copy-start.1 = (f32[2048]{0:T(1024)S(1)}, f32[2048]{0:T(1024)}, u32[]{:S(2)}) copy-start(f32[2048]{0:T(1024)} %param.23) | copy-start | bytes 24580
  68.6 12.7 %copy-start.2 = (s32[2048]{0:T(1024)S(1)}, s32[2048]{0:T(1024)}, u32[]{:S(2)}) copy-start(s32[2048]{0:T(1024)} %param.24) | copy-start | bytes 24580
  68.6 12.7 %copy-start.3 = (f32[40]{0:T(128)S(1)}, f32[40]{0:T(128)}, u32[]{:S(2)}) copy-start(f32[40]{0:T(128)} %a_ref.1) | copy-start | bytes 484
  68.6 12.7 %copy-start.4 = (f32[40]{0:T(128)S(1)}, f32[40]{0:T(128)}, u32[]{:S(2)}) copy-start(f32[40]{0:T(128)} %b_ref.1) | copy-start | bytes 484
  68.6 12.7 %copy-start.5 = (f32[40]{0:T(128)S(1)}, f32[40]{0:T(128)}, u32[]{:S(2)}) copy-start(f32[40]{0:T(128)} %s_ref.1) | copy-start | bytes 484

commit v5 on v4

--- a/solution.py
+++ b/solution.py
@@ -24,6 +24,8 @@
 CAP_COL = 24
 CAP_ROW = 32
 GROUP = 2
+RIGHTS = 4
+AHEAD = 8
 HALVES = 2
 ROUNDS = 56
 PIECE_ROWS = 8
@@ -33,6 +35,7 @@
 VMEM = pl.BlockSpec(memory_space=pltpu.VMEM)
 SMEM = pl.BlockSpec(memory_space=pltpu.SMEM)
 HBM = pl.BlockSpec(memory_space=pltpu.HBM)
+ANY = pl.BlockSpec(memory_space=pl.ANY)
 f32 = jnp.float32
 bf16 = jnp.bfloat16
 i32 = jnp.int32
@@ -201,28 +204,24 @@
     )
 
 
-def gather_kernel(idx_ref, slip_ref, out_ref, rounds_ref, to_do_ref):
-    def one_col(c, over):
+def gather_kernel(idx_ref, slip_ref, out_ref):
+    def one_col(c, _):
         for k in range(CAP_COL):
             out_ref[c * CAP_COL + k] = slip_ref[idx_ref[c, k]]
-        return jnp.maximum(over, idx_ref[c, LANES - 1])
-
-    over = lax.fori_loop(0, N_COL, one_col, jnp.int32(0))
-    rounds = jnp.where(over == 0, 0, jnp.where(over == 1, HALVES, ROUNDS))
-    rounds_ref[0] = rounds
-    to_do_ref[0] = rounds
+        return 0
+
+    lax.fori_loop(0, N_COL, one_col, 0)
 
 
 def gather_rows(idx, slip):
-    one = jax.ShapeDtypeStruct((1,), i32)
     return call(
         gather_kernel,
         (idx, slip),
         [SMEM, VMEM],
-        (jax.ShapeDtypeStruct((N_COL * CAP_COL, 2, B), f32), one, one),
-        (VMEM, SMEM, SMEM),
+        (jax.ShapeDtypeStruct((N_COL * CAP_COL, 2, B), f32),),
+        (VMEM,),
         "gather",
-    )
+    )[0]
 
 
 def forward_kernel(idx_ref, got_ref, out_ref):
@@ -271,26 +270,64 @@
 
 
 def blocks_kernel(
-    pos_ref, near_row_ref, far_row_ref, x_ref, left_ref, right_hbm, near_hbm,
-    out_ref, acc_ref, right_ref, near_ref, right_sems, near_sems,
+    pos_hbm, asked_hbm, near_row_hbm, far_row_hbm, a_hbm, b_hbm, s_hbm, fault_ref, x_ref, left_ref,
+    right_hbm, near_hbm,
+    out_ref, param_ref, rounds_out, to_do_out,
+    acc_ref, right_ref, near_ref, pos_ref, asked_ref, near_row_ref, far_row_ref, a_ref, b_ref, s_ref,
+    rounds_ref, sems, small_sems, out_sems,
 ):
-    half = FAR // 2
-    right_copies = [
-        pltpu.make_async_copy(
-            right_hbm.at[pl.ds(g * half, half)], right_ref.at[pl.ds(g * half, half)], right_sems.at[g]
+    copies = [
+        pltpu.make_async_copy(from_ref.at[pl.ds(at, size)], to_ref.at[pl.ds(at, size)], sems.at[k])
+        for k, (from_ref, to_ref, at, size) in enumerate(
+            [(right_hbm, right_ref, at, FAR // RIGHTS) for at in range(0, FAR, FAR // RIGHTS)]
+            + [(near_hbm, near_ref, at, GROUP) for at in range(0, NEAR, GROUP)]
         )
-        for g in range(2)
     ]
-    near_copies = [
-        pltpu.make_async_copy(
-            near_hbm.at[pl.ds(g * GROUP, GROUP)], near_ref.at[pl.ds(g * GROUP, GROUP)], near_sems.at[g]
+    small = [
+        pltpu.make_async_copy(one, to, small_sems.at[k])
+        for k, (one, to) in enumerate(
+            [
+                (pos_hbm, pos_ref),
+                (far_row_hbm, far_row_ref),
+                (near_row_hbm, near_row_ref),
+                (asked_hbm, asked_ref),
+                (a_hbm, a_ref),
+                (b_hbm, b_ref),
+                (s_hbm, s_ref),
+            ]
         )
-        for g in range(NEAR // GROUP)
     ]
-    for copy in right_copies + near_copies:
+    for copy in small:
         copy.start()
+    for copy in copies[:AHEAD]:
+        copy.start()
+
+    def arrive(k):
+        copies[k].wait()
+        if k + AHEAD < len(copies):
+            copies[k + AHEAD].start()
+
     out_ref[...] = jnp.zeros_like(out_ref)
     acc_ref[...] = jnp.zeros_like(acc_ref)
+    for copy in small:
+        copy.wait()
+    over = asked_ref[0, LANES - 1]
+    for c in range(1, N_COL):
+        over = jnp.maximum(over, asked_ref[c, LANES - 1])
+    rounds_ref[0] = jnp.where(over == 0, 0, jnp.where(over == 1, HALVES, ROUNDS))
+    told = [
+        pltpu.make_async_copy(rounds_ref, to, out_sems.at[k])
+        for k, to in enumerate((rounds_out, to_do_out))
+    ]
+    for copy in told:
+        copy.start()
+    fault = fault_ref[...]
+    found = [jnp.zeros(fault.shape, f32) for _ in range(3)]
+    for f in range(FAULTS):
+        here = fault == f
+        found = [jnp.where(here, one[f], old) for one, old in zip((a_ref, b_ref, s_ref), found)]
+    for k in range(3):
+        param_ref[k] = found[k]
 
     def some_far(p, _):
         for t in range(FP):
@@ -298,32 +335,44 @@
             add_far(out_ref, left_ref, right_ref, n, x_ref[pos_ref[0, NEAR + n]], far_row_ref[0, n])
         return 0
 
-    for g, copy in enumerate(right_copies):
-        copy.wait()
-        lax.fori_loop(g * N_ROW // 2, (g + 1) * N_ROW // 2, some_far, 0)
-    for g, copy in enumerate(near_copies):
-        copy.wait()
+    for g in range(RIGHTS):
+        arrive(g)
+        lax.fori_loop(g * N_ROW // RIGHTS, (g + 1) * N_ROW // RIGHTS, some_far, 0)
+    for g in range(NEAR // GROUP):
+        arrive(RIGHTS + g)
         for n in range(g * GROUP, (g + 1) * GROUP):
             add_near(acc_ref, near_ref, n, x_ref[pos_ref[0, n]], near_row_ref[0, n])
     out_ref[...] = out_ref[...] + acc_ref[...].T
-
-
-def block_sums(pos, near_index, far_index, x, left, right, near):
+    for copy in told:
+        copy.wait()
+
+
+def block_sums(pos, asked, near_index, far_index, params, fault, x, left, right, near):
+    one = jax.ShapeDtypeStruct((1,), i32)
+    small = (pos, asked, near_index, far_index, *params)
     return pl.pallas_call(
         blocks_kernel,
-        out_shape=jax.ShapeDtypeStruct((RC_DEV, 2 * B), f32),
-        in_specs=[SMEM, SMEM, SMEM, VMEM, VMEM, HBM, HBM],
-        out_specs=VMEM,
+        out_shape=(
+            jax.ShapeDtypeStruct((RC_DEV, 2 * B), f32),
+            jax.ShapeDtypeStruct((3,) + fault.shape, f32),
+            one,
+            one,
+        ),
+        in_specs=[ANY] * len(small) + [VMEM, VMEM, VMEM, HBM, HBM],
+        out_specs=(VMEM, VMEM, ANY, ANY),
         scratch_shapes=[
             pltpu.VMEM((2 * B, LANES), f32),
             pltpu.VMEM(right.shape, bf16),
             pltpu.VMEM(near.shape, f32),
+            *(pltpu.SMEM(x.shape, x.dtype) for x in small),
+            pltpu.SMEM((1,), i32),
+            pltpu.SemaphoreType.DMA((RIGHTS + NEAR // GROUP,)),
+            pltpu.SemaphoreType.DMA((len(small),)),
             pltpu.SemaphoreType.DMA((2,)),
-            pltpu.SemaphoreType.DMA((NEAR // GROUP,)),
         ],
         compiler_params=pltpu.CompilerParams(vmem_limit_bytes=28 * 1024 * 1024),
         name="blocks",
-    )(pos, near_index, far_index, x, left, in_hbm(right), in_hbm(near))
+    )(*small, fault, x, left, in_hbm(right), in_hbm(near))
 
 
 def pick_kernel(to_do_ref, rounds_ref, pos_ref, x_ref, out_ref):
@@ -386,9 +435,7 @@
     )(pos, near_index, far_index, x, in_hbm(near), in_hbm(left), in_hbm(right))
 
 
-def final_kernel(
-    a_ref, b_ref, s_ref, parts_ref, stress_ref, state_ref, fault_ref, out_stress, out_rate, out_state
-):
+def final_kernel(param_ref, parts_ref, stress_ref, state_ref, out_stress, out_rate, out_state):
     total = parts_ref[0]
     for c in range(1, N_COL):
         total = total + parts_ref[c]
@@ -396,15 +443,7 @@
     for h in range(2):
         every = pl.ds(h, groups, stride=2)
         state = state_ref[every, :]
-        fault = fault_ref[every, :]
-        a = jnp.zeros_like(state)
-        b = jnp.zeros_like(state)
-        sigma = jnp.zeros_like(state)
-        for f in range(FAULTS):
-            here = fault == f
-            a = jnp.where(here, a_ref[f], a)
-            b = jnp.where(here, b_ref[f], b)
-            sigma = jnp.where(here, s_ref[f], sigma)
+        a, b, sigma = (param_ref[k, every, :] for k in range(3))
         square = jnp.ones_like(state)
         for k in range(2):
             old = jnp.concatenate(
@@ -425,27 +464,19 @@
         out_state[every, :] = state + STEP_SIZE * b * (jnp.exp(-state / b) - rate)
 
 
-def finish(a, b, s, parts, stress, state, fault):
+def finish(params, parts, stress, state):
     rows = stress.shape[1] // LANES
-    new_stress, new_rate, new_state = pl.pallas_call(
+    new_stress, new_rate, new_state = call(
         final_kernel,
-        out_shape=(
+        (params, parts.reshape(N_COL, RC_DEV // N_COL, 2 * B), stress, state.reshape(rows, LANES)),
+        [VMEM] * 4,
+        (
             jax.ShapeDtypeStruct(stress.shape, f32),
             jax.ShapeDtypeStruct((rows, LANES), f32),
             jax.ShapeDtypeStruct((rows, LANES), f32),
         ),
-        in_specs=[SMEM, SMEM, SMEM, VMEM, VMEM, VMEM, VMEM],
-        out_specs=(VMEM, VMEM, VMEM),
-        compiler_params=SMALL,
-        name="finish",
-    )(
-        a,
-        b,
-        s,
-        parts.reshape(N_COL, RC_DEV // N_COL, 2 * B),
-        stress,
-        state.reshape(rows, LANES),
-        fault.reshape(rows, LANES),
+        (VMEM,) * 3,
+        "finish",
     )
     return (new_stress, new_rate.reshape(-1), new_state.reshape(-1))
 
@@ -475,17 +506,20 @@
     def fetch(*ctl):
         req, snd, pos, slip_held = make_index(gathered, slip, ctl)
         asked = lax.all_to_all(req, "col", 0, 0, tiled=True)
-        reply, rounds, to_do = gather_rows(asked, slip_held)
-        got = lax.all_to_all(reply, "col", 0, 0, tiled=True)
-        return lax.all_to_all(forward_rows(snd, got), "row", 0, 0, tiled=True), pos, rounds, to_do
-
-    x, pos, rounds, to_do = fetch()
-    fast = block_sums(pos, near_index, far_index, x, left, right, near)
+        got = lax.all_to_all(gather_rows(asked, slip_held), "col", 0, 0, tiled=True)
+        return lax.all_to_all(forward_rows(snd, got), "row", 0, 0, tiled=True), pos, asked
+
+    x, pos, asked = fetch()
+    faults = (direct_effect, evolution_effect, normal_stress)
+    fault = fault_of_row.reshape(-1, LANES)
+    fast, params, rounds, to_do = block_sums(
+        pos, asked, near_index, far_index, faults, fault, x, left, right, near
+    )
 
     def one_round(carry):
         to_do, total = carry
         now = to_do.reshape(1)
-        x, pos, _, _ = fetch(now, rounds)
+        x, pos, _ = fetch(now, rounds)
         rows = pick_rows(now, rounds, pos, x)
         n = jnp.arange(LANES, dtype=i32)[None, :]
         part = round_sums(n, near_index, far_index, rows, near, left, right)
@@ -493,9 +527,7 @@
 
     _, summed = lax.while_loop(lambda carry: carry[0] > 0, one_round, (to_do.reshape(()), fast))
     parts = lax.all_to_all(summed, "col", 0, 0, tiled=True)
-    return finish(
-        direct_effect, evolution_effect, normal_stress, parts, stress, state, fault_of_row
-    )
+    return finish(params, parts, stress, state)
 
 
 def solution(mesh):

time: 82.9 us -> 79.7 us (0.961)
  Pallas kernels: 15.5 us -> 12.2 us
    pallas_call x2 -> x1, Pallas kernels: 10.8 us -> 7.49 us  [block_sums(): pl.pallas_call(blocks_kernel, out_shape=(jax.ShapeDtypeStruct((RC_DEV, 2...]
    pallas_call x4 -> x5, Pallas kernels: 4.7 us -> 4.67 us  [call(): pl.pallas_call(run, out_shape=tuple(outs) + tuple((pltpu.VMEM((size,) + o...]
where the time goes in v5:
time: 79.7 us; the launch traced here: 79.3 us
  blocking collectives  65.7 us (82%)
  Pallas kernels  12.2 us (15%)
    all_to_all x1, blocking collectives, fetch(): asked = lax.all_to_all(req, 'col', 0, 0, tiled=True)  15.7 us
    all_to_all x1, blocking collectives, fetch(): got = lax.all_to_all(gather_rows(asked, slip_held), 'col', 0, 0, tiled=True)  15.6 us
    all_to_all x1, blocking collectives, fetch(): lax.all_to_all(forward_rows(snd, got), 'row', 0, 0, tiled=True)  12.8 us
    all_to_all x1, blocking collectives, body(): parts = lax.all_to_all(summed, 'col', 0, 0, tiled=True)  11.9 us
    all_to_all x1, blocking collectives, body(): lax.all_to_all(make_payload(source_cluster, near_index, far_index), 'row'...  9.63 us
    pallas_call x1, Pallas kernels, block_sums(): pl.pallas_call(blocks_kernel, out_shape=(jax.ShapeDtypeStruct((RC_DEV, 2...  7.49 us
    pallas_call x5, Pallas kernels, call(): pl.pallas_call(run, out_shape=tuple(outs) + tuple((pltpu.VMEM((size,) + o...  4.67 us

profile of v5, /device:TPU:0, one launch (start us, length us, event | category | flops | bytes accessed | tf_op | source)
XLA Modules:
  0.0 79.3 jit_solution(293308454496933436)
XLA Ops:
  0.6 0.7 payload.1
  1.4 9.6 %all_to_all.57.refs_0_ = s32[8,8,128]{2,1,0:T(8,128)S(1)} all-to-all(s32[8,8,128]{2,1,0:T(8,128)S(1)} %payload.1), channel_id=1, replica_groups=mesh['row'=8,'col'=16] {'row'}, dimensions={0} | all-to-all | bytes 65536 | tf_op jit(solution)/shard_map/all_to_all | solution.py:502
  11.0 1.2 %index.5 = (s32[16,128]{1,0:T(8,128)S(1)}, s32[8,128]{1,0:T(8,128)S(1)}, s32[1,128]{1,0:T(1,128)S(1)}, f32[512,2,256]{2,1,0:T(2,128)S(1)}) custom-call(s32[8,8,128]{2,1,0:T(8,128)S(1)} %all_to_all.57.refs_0_, f32[512,2,256]{2,1,0:T(2,128)} %bitcast.46), custom_call_target="tpu_custom_call" | custom-call | tf_op jit(solution)/shard_map/index/pallas_call | solution.py:67
  12.2 0.0 copy-start.1
  12.3 0.0 copy-start.3
  12.3 0.0 copy-start.4
  12.3 0.0 copy-start.5
  12.3 0.0 copy-start.6
  12.3 0.0 copy-start.7
  12.3 0.0 copy-start.8
  12.3 15.7 %all_to_all.58 = s32[16,1,128]{2,1,0:T(1,128)S(1)} all-to-all(s32[16,1,128]{2,1,0:T(1,128)S(1)} %bitcast.39), channel_id=1, replica_groups=mesh['row'=8,'col'=16] {'col'}, dimensions={0} | all-to-all | bytes 16384 | tf_op jit(solution)/shard_map/all_to_all | solution.py:508
  28.0 1.1 %gather.5 = f32[384,2,256]{2,1,0:T(2,128)S(1)} custom-call(s32[16,128]{1,0:T(8,128)S(1)} %bitcast.35, f32[512,2,256]{2,1,0:T(2,128)S(1)} %get-tuple-element.138.refs_1_), custom_call_target="tpu_custom_call" | custom-call | tf_op jit(solution)/shard_map/gather/pallas_call | solution.py:67
  29.1 15.6 %all_to_all.59.refs_1_ = f32[384,2,256]{2,1,0:T(2,128)S(1)} all-to-all(f32[384,2,256]{2,1,0:T(2,128)S(1)} %gather.5), channel_id=1, replica_groups=mesh['row'=8,'col'=16] {'col'}, dimensions={0} | all-to-all | bytes 1572864 | tf_op jit(solution)/shard_map/all_to_all | solution.py:509
  44.8 0.9 %forward.5 = f32[256,2,256]{2,1,0:T(2,128)S(1)} custom-call(s32[8,128]{1,0:T(8,128)S(1)} %get-tuple-element.137.refs_0_, f32[384,2,256]{2,1,0:T(2,128)S(1)} %all_to_all.59.refs_1_), custom_call_target="tpu_custom_call" | custom-call | tf_op jit(solution)/shard_map/forward/pallas_call | solution.py:67
  45.7 12.8 %all_to_all.60.x_ref = f32[256,2,256]{2,1,0:T(2,128)S(1)} all-to-all(f32[256,2,256]{2,1,0:T(2,128)S(1)} %forward.5), channel_id=1, replica_groups=mesh['row'=8,'col'=16] {'row'}, dimensions={0} | all-to-all | bytes 1048576 | tf_op jit(solution)/shard_map/all_to_all | solution.py:510
  58.5 0.0 copy-done.1
  58.5 0.0 copy-done.3
  58.5 7.5 %blocks.1 = (f32[128,512]{1,0:T(8,128)S(1)}, f32[3,16,128]{2,1,0:T(8,128)S(1)}, s32[1]{0:T(128)}, s32[1]{0:T(128)}) custom-call(s32[1,128]{1,0:T(1,128)S(1)} %get-tuple-element.135.pos_hbm, s32[16,128]{1,0:T(8,128)S(1)} %bitcast.36, s32[2,16]{1,0:T(2,128)S(1)} %bitcast.50, s32[2,96]{1,0:T(2,128)S(1)} %bitcast.53, f32[40]{0:T(128)S(1)} %copy-done.3, ...), custom_call_target="tpu_custom_call" | custom-call | tf_op jit(solution)/shard_map/blocks/pallas_call | solution.py:353
  66.0 0.0 copy-start
  66.0 0.0 copy-start.2
  66.1 0.7 while.12
  66.7 11.9 %all_to_all.61.refs_1_ = f32[16,8,512]{2,1,0:T(8,128)S(1)} all-to-all(f32[16,8,512]{2,1,0:T(8,128)S(1)} %bitcast.48), channel_id=1, replica_groups=mesh['row'=8,'col'=16] {'col'}, dimensions={0} | all-to-all | bytes 524288 | tf_op jit(solution)/shard_map/all_to_all | solution.py:529
  78.7 0.0 copy-done
  78.7 0.7 finish.1
  (6 shorter events, 0.0 us)
Async XLA Ops:
  12.2 46.2 %copy-start.1 = (s32[2048]{0:T(1024)S(1)}, s32[2048]{0:T(1024)}, u32[]{:S(2)}) copy-start(s32[2048]{0:T(1024)} %param.24) | copy-start | bytes 24580
  12.3 46.2 %copy-start.3 = (f32[40]{0:T(128)S(1)}, f32[40]{0:T(128)}, u32[]{:S(2)}) copy-start(f32[40]{0:T(128)} %a_hbm.1) | copy-start | bytes 484
  12.3 46.2 %copy-start.4 = (f32[40]{0:T(128)S(1)}, f32[40]{0:T(128)}, u32[]{:S(2)}) copy-start(f32[40]{0:T(128)} %b_hbm.1) | copy-start | bytes 484
  12.3 46.2 %copy-start.5 = (f32[40]{0:T(128)S(1)}, f32[40]{0:T(128)}, u32[]{:S(2)}) copy-start(f32[40]{0:T(128)} %s_hbm.1) | copy-start | bytes 484
  12.3 46.2 %copy-start.6 = (bf16[1,1,96,32,512]{4,3,2,1,0:T(8,128)(2,1)S(1)}, bf16[1,1,96,32,512]{4,3,2,1,0:T(8,128)(2,1)}, u32[]{:S(2)}) copy-start(bf16[1,1,96,32,512]{4,3,2,1,0:T(8,128)(2,1)} %param.19) | copy-start | bytes 9437188
  12.3 46.2 %copy-start.7 = (s32[1,1,2,16]{3,2,1,0:T(2,128)S(1)}, s32[1,1,2,16]{3,2,1,0:T(2,128)}, u32[]{:S(2)}) copy-start(s32[1,1,2,16]{3,2,1,0:T(2,128)} %param.18) | copy-start | bytes 388
  12.3 46.2 %copy-start.8 = (s32[1,1,2,96]{3,2,1,0:T(2,128)S(1)}, s32[1,1,2,96]{3,2,1,0:T(2,128)}, u32[]{:S(2)}) copy-start(s32[1,1,2,96]{3,2,1,0:T(2,128)} %param.21) | copy-start | bytes 2308
  66.0 12.6 %copy-start = (f32[2,2048]{1,0:T(2,128)S(1)}, f32[2,2048]{1,0:T(2,128)}, u32[]{:S(2)}) copy-start(f32[2,2048]{1,0:T(2,128)} %refs_2_.1) | copy-start | bytes 49156
  66.0 12.6 %copy-start.2 = (f32[2048]{0:T(1024)S(1)}, f32[2048]{0:T(1024)}, u32[]{:S(2)}) copy-start(f32[2048]{0:T(1024)} %param.23) | copy-start | bytes 24580

commit v6 on v5

--- a/solution.py
+++ b/solution.py
@@ -23,10 +23,8 @@
 LANES = 128
 CAP_COL = 24
 CAP_ROW = 32
-GROUP = 2
-RIGHTS = 4
-AHEAD = 8
 HALVES = 2
+SPAN = 15 * 10**9
 ROUNDS = 56
 PIECE_ROWS = 8
 FAULTS = 40
@@ -47,7 +45,7 @@
     return pltpu.with_memory_space_constraint(x, pltpu.HBM)
 
 
-def call(kernel, ins, specs, outs, out_specs, name, staged=()):
+def call(kernel, ins, specs, outs, out_specs, name, staged=(), span=0):
     count, given, made = len(staged), len(ins), len(outs)
 
     def run(*refs):
@@ -72,6 +70,7 @@
         out_specs=tuple(out_specs) + (VMEM,) * count,
         scratch_shapes=[pltpu.SemaphoreType.DMA] * count,
         compiler_params=SMALL,
+        cost_estimate=pl.CostEstimate(flops=span, transcendentals=0, bytes_accessed=0) if span else None,
         name=name,
     )(*ins, *(in_hbm(one) for one, _, _ in staged))
 
@@ -241,6 +240,7 @@
         (jax.ShapeDtypeStruct((N_ROW * CAP_ROW, 2, B), f32),),
         (VMEM,),
         "forward",
+        span=SPAN,
     )[0]
 
 
@@ -271,18 +271,11 @@
 
 def blocks_kernel(
     pos_hbm, asked_hbm, near_row_hbm, far_row_hbm, a_hbm, b_hbm, s_hbm, fault_ref, x_ref, left_ref,
-    right_hbm, near_hbm,
+    right_ref, near_ref,
     out_ref, param_ref, rounds_out, to_do_out,
-    acc_ref, right_ref, near_ref, pos_ref, asked_ref, near_row_ref, far_row_ref, a_ref, b_ref, s_ref,
-    rounds_ref, sems, small_sems, out_sems,
+    acc_ref, pos_ref, asked_ref, near_row_ref, far_row_ref, a_ref, b_ref, s_ref,
+    rounds_ref, small_sems, out_sems,
 ):
-    copies = [
-        pltpu.make_async_copy(from_ref.at[pl.ds(at, size)], to_ref.at[pl.ds(at, size)], sems.at[k])
-        for k, (from_ref, to_ref, at, size) in enumerate(
-            [(right_hbm, right_ref, at, FAR // RIGHTS) for at in range(0, FAR, FAR // RIGHTS)]
-            + [(near_hbm, near_ref, at, GROUP) for at in range(0, NEAR, GROUP)]
-        )
-    ]
     small = [
         pltpu.make_async_copy(one, to, small_sems.at[k])
         for k, (one, to) in enumerate(
@@ -299,14 +292,6 @@
     ]
     for copy in small:
         copy.start()
-    for copy in copies[:AHEAD]:
-        copy.start()
-
-    def arrive(k):
-        copies[k].wait()
-        if k + AHEAD < len(copies):
-            copies[k + AHEAD].start()
-
     out_ref[...] = jnp.zeros_like(out_ref)
     acc_ref[...] = jnp.zeros_like(acc_ref)
     for copy in small:
@@ -335,13 +320,14 @@
             add_far(out_ref, left_ref, right_ref, n, x_ref[pos_ref[0, NEAR + n]], far_row_ref[0, n])
         return 0
 
-    for g in range(RIGHTS):
-        arrive(g)
-        lax.fori_loop(g * N_ROW // RIGHTS, (g + 1) * N_ROW // RIGHTS, some_far, 0)
-    for g in range(NEAR // GROUP):
-        arrive(RIGHTS + g)
-        for n in range(g * GROUP, (g + 1) * GROUP):
+    lax.fori_loop(0, N_ROW, some_far, 0)
+    def two_near(q, _):
+        for t in range(2):
+            n = 2 * q + t
             add_near(acc_ref, near_ref, n, x_ref[pos_ref[0, n]], near_row_ref[0, n])
+        return 0
+
+    lax.fori_loop(0, NEAR // 2, two_near, 0)
     out_ref[...] = out_ref[...] + acc_ref[...].T
     for copy in told:
         copy.wait()
@@ -358,21 +344,18 @@
             one,
             one,
         ),
-        in_specs=[ANY] * len(small) + [VMEM, VMEM, VMEM, HBM, HBM],
+        in_specs=[ANY] * len(small) + [VMEM, VMEM, VMEM, VMEM, VMEM],
         out_specs=(VMEM, VMEM, ANY, ANY),
         scratch_shapes=[
             pltpu.VMEM((2 * B, LANES), f32),
-            pltpu.VMEM(right.shape, bf16),
-            pltpu.VMEM(near.shape, f32),
             *(pltpu.SMEM(x.shape, x.dtype) for x in small),
             pltpu.SMEM((1,), i32),
-            pltpu.SemaphoreType.DMA((RIGHTS + NEAR // GROUP,)),
             pltpu.SemaphoreType.DMA((len(small),)),
             pltpu.SemaphoreType.DMA((2,)),
         ],
         compiler_params=pltpu.CompilerParams(vmem_limit_bytes=28 * 1024 * 1024),
         name="blocks",
-    )(*small, fault, x, left, in_hbm(right), in_hbm(near))
+    )(*small, fault, x, left, right, near)
 
 
 def pick_kernel(to_do_ref, rounds_ref, pos_ref, x_ref, out_ref):

time: 79.7 us -> 77.2 us (0.969)
  Pallas kernels: 12.2 us -> 9.36 us
    pallas_call x1, Pallas kernels: 7.49 us -> 4.68 us  [block_sums(): pl.pallas_call(blocks_kernel, out_shape=(jax.ShapeDtypeStruct((RC_DEV, 2...]
where the time goes in v6:
time: 77.2 us; the launch traced here: 76.9 us
  blocking collectives  65.9 us (85%)
  Pallas kernels  9.36 us (12%)
  between operations  0.84 us (1%)
    all_to_all x1, blocking collectives, fetch(): got = lax.all_to_all(gather_rows(asked, slip_held), 'col', 0, 0, tiled=True)  15.6 us
    all_to_all x1, blocking collectives, fetch(): asked = lax.all_to_all(req, 'col', 0, 0, tiled=True)  15.4 us
    all_to_all x1, blocking collectives, fetch(): lax.all_to_all(forward_rows(snd, got), 'row', 0, 0, tiled=True)  13.3 us
    all_to_all x1, blocking collectives, body(): parts = lax.all_to_all(summed, 'col', 0, 0, tiled=True)  11.9 us
    all_to_all x1, blocking collectives, body(): lax.all_to_all(make_payload(source_cluster, near_index, far_index), 'row'...  9.63 us
    pallas_call x1, Pallas kernels, block_sums(): pl.pallas_call(blocks_kernel, out_shape=(jax.ShapeDtypeStruct((RC_DEV, 2...  4.68 us
    pallas_call x5, Pallas kernels, call(): pl.pallas_call(run, out_shape=tuple(outs) + tuple((pltpu.VMEM((size,) + o...  4.67 us

profile of v6, /device:TPU:0, one launch (start us, length us, event | category | flops | bytes accessed | tf_op | source)
XLA Modules:
  0.0 76.9 jit_solution(7259396322899548314)
XLA Ops:
  0.6 0.7 payload.1
  1.4 9.6 %all_to_all.57.refs_0_ = s32[8,8,128]{2,1,0:T(8,128)S(1)} all-to-all(s32[8,8,128]{2,1,0:T(8,128)S(1)} %payload.1), channel_id=1, replica_groups=mesh['row'=8,'col'=16] {'row'}, dimensions={0} | all-to-all | bytes 65536 | tf_op jit(solution)/shard_map/all_to_all | solution.py:485
  11.0 1.2 %index.5 = (s32[16,128]{1,0:T(8,128)S(1)}, s32[8,128]{1,0:T(8,128)S(1)}, s32[1,128]{1,0:T(1,128)S(1)}, f32[512,2,256]{2,1,0:T(2,128)S(1)}) custom-call(s32[8,8,128]{2,1,0:T(8,128)S(1)} %all_to_all.57.refs_0_, f32[512,2,256]{2,1,0:T(2,128)} %bitcast.48), custom_call_target="tpu_custom_call" | custom-call | tf_op jit(solution)/shard_map/index/pallas_call | solution.py:65
  12.2 15.4 %all_to_all.58 = s32[16,1,128]{2,1,0:T(1,128)S(1)} all-to-all(s32[16,1,128]{2,1,0:T(1,128)S(1)} %bitcast.39), channel_id=1, replica_groups=mesh['row'=8,'col'=16] {'col'}, dimensions={0} | all-to-all | bytes 16384 | tf_op jit(solution)/shard_map/all_to_all | solution.py:491
  27.7 1.1 %gather.5 = f32[384,2,256]{2,1,0:T(2,128)S(1)} custom-call(s32[16,128]{1,0:T(8,128)S(1)} %bitcast.35, f32[512,2,256]{2,1,0:T(2,128)S(1)} %get-tuple-element.138.refs_1_), custom_call_target="tpu_custom_call" | custom-call | tf_op jit(solution)/shard_map/gather/pallas_call | solution.py:65
  28.8 15.6 %all_to_all.59.refs_1_ = f32[384,2,256]{2,1,0:T(2,128)S(1)} all-to-all(f32[384,2,256]{2,1,0:T(2,128)S(1)} %gather.5), channel_id=1, replica_groups=mesh['row'=8,'col'=16] {'col'}, dimensions={0} | all-to-all | bytes 1572864 | tf_op jit(solution)/shard_map/all_to_all | solution.py:492
  44.4 0.0 copy-start.5
  44.4 0.0 slice-start.1
  44.5 0.0 slice-start.2
  44.5 0.0 slice-start.3
  44.5 0.0 copy-start.6
  44.5 0.0 copy-start.7
  44.5 0.0 copy-start.8
  44.5 0.0 copy-start.9
  44.5 0.9 %forward.5 = f32[256,2,256]{2,1,0:T(2,128)S(1)} custom-call(s32[8,128]{1,0:T(8,128)S(1)} %get-tuple-element.137.refs_0_, f32[384,2,256]{2,1,0:T(2,128)S(1)} %all_to_all.59.refs_1_), custom_call_target="tpu_custom_call" | custom-call | flops 15000000512 | tf_op jit(solution)/shard_map/forward/pallas_call | solution.py:65
  45.4 13.3 %all_to_all.60.x_ref = f32[256,2,256]{2,1,0:T(2,128)S(1)} all-to-all(f32[256,2,256]{2,1,0:T(2,128)S(1)} %forward.5), channel_id=1, replica_groups=mesh['row'=8,'col'=16] {'row'}, dimensions={0} | all-to-all | bytes 1048576 | tf_op jit(solution)/shard_map/all_to_all | solution.py:493
  58.8 0.0 slice-done
  58.9 4.7 %blocks.1 = (f32[128,512]{1,0:T(8,128)S(1)}, f32[3,16,128]{2,1,0:T(8,128)S(1)}, s32[1]{0:T(128)}, s32[1]{0:T(128)}) custom-call(s32[1,128]{1,0:T(1,128)S(1)} %get-tuple-element.135.pos_hbm, s32[16,128]{1,0:T(8,128)S(1)} %bitcast.36, s32[2,16]{1,0:T(2,128)S(1)} %bitcast.52, s32[2,96]{1,0:T(2,128)S(1)} %bitcast.55, f32[40]{0:T(128)S(1)} %copy-done.3, ...), custom_call_target="tpu_custom_call" | custom-call | tf_op jit(solution)/shard_map/blocks/pallas_call | solution.py:339
  63.6 0.0 copy-start
  63.6 0.0 copy-start.2
  63.6 0.7 while.12
  64.3 11.9 %all_to_all.61.refs_1_ = f32[16,8,512]{2,1,0:T(8,128)S(1)} all-to-all(f32[16,8,512]{2,1,0:T(8,128)S(1)} %bitcast.50), channel_id=1, replica_groups=mesh['row'=8,'col'=16] {'col'}, dimensions={0} | all-to-all | bytes 524288 | tf_op jit(solution)/shard_map/all_to_all | solution.py:512
  76.2 0.0 copy-done.2
  76.2 0.7 finish.1
  (17 shorter events, 0.0 us)
Async XLA Ops:
  44.4 14.3 %slice-start = ((s8[16777216]{0:T(1024)(128)(4,1)}), s8[4194304]{0:T(1024)(128)(4,1)S(1)}, s32[]{:S(2)}) async-start(s8[16777216]{0:T(1024)(128)(4,1)} %bitcast.41), calls=%async_computation.8 | async-start | bytes 8388608
  44.4 14.3 %copy-start.1 = (s32[2048]{0:T(1024)S(1)}, s32[2048]{0:T(1024)}, u32[]{:S(2)}) copy-start(s32[2048]{0:T(1024)} %param.24) | copy-start | bytes 24580
  44.4 14.3 %copy-start.3 = (f32[40]{0:T(128)S(1)}, f32[40]{0:T(128)}, u32[]{:S(2)}) copy-start(f32[40]{0:T(128)} %a_hbm.1) | copy-start | bytes 484
  44.4 14.3 %copy-start.4 = (f32[40]{0:T(128)S(1)}, f32[40]{0:T(128)}, u32[]{:S(2)}) copy-start(f32[40]{0:T(128)} %b_hbm.1) | copy-start | bytes 484
  44.4 14.4 %copy-start.5 = (f32[40]{0:T(128)S(1)}, f32[40]{0:T(128)}, u32[]{:S(2)}) copy-start(f32[40]{0:T(128)} %s_hbm.1) | copy-start | bytes 484
  44.4 14.4 %slice-start.1 = ((s8[16777216]{0:T(1024)(128)(4,1)}), s8[4194304]{0:T(1024)(128)(4,1)S(1)}, s32[]{:S(2)}) async-start(s8[16777216]{0:T(1024)(128)(4,1)} %bitcast.41), calls=%async_computation.9 | async-start | bytes 8388608
  44.5 14.3 %slice-start.2 = ((s8[16777216]{0:T(1024)(128)(4,1)}), s8[4194304]{0:T(1024)(128)(4,1)S(1)}, s32[]{:S(2)}) async-start(s8[16777216]{0:T(1024)(128)(4,1)} %bitcast.41), calls=%async_computation.10 | async-start | bytes 8388608
  44.5 14.3 %slice-start.3 = ((s8[16777216]{0:T(1024)(128)(4,1)}), s8[4194304]{0:T(1024)(128)(4,1)S(1)}, s32[]{:S(2)}) async-start(s8[16777216]{0:T(1024)(128)(4,1)} %bitcast.41), calls=%async_computation.11 | async-start | bytes 8388608
  44.5 14.3 %copy-start.6 = (bf16[1,1,96,32,512]{4,3,2,1,0:T(8,128)(2,1)S(1)}, bf16[1,1,96,32,512]{4,3,2,1,0:T(8,128)(2,1)}, u32[]{:S(2)}) copy-start(bf16[1,1,96,32,512]{4,3,2,1,0:T(8,128)(2,1)} %param.19) | copy-start | bytes 9437188
  44.5 14.3 %copy-start.7 = (bf16[1,1,96,32,512]{4,3,2,1,0:T(8,128)(2,1)S(1)}, bf16[1,1,96,32,512]{4,3,2,1,0:T(8,128)(2,1)}, u32[]{:S(2)}) copy-start(bf16[1,1,96,32,512]{4,3,2,1,0:T(8,128)(2,1)} %param.20) | copy-start | bytes 9437188
  44.5 14.3 %copy-start.8 = (s32[1,1,2,16]{3,2,1,0:T(2,128)S(1)}, s32[1,1,2,16]{3,2,1,0:T(2,128)}, u32[]{:S(2)}) copy-start(s32[1,1,2,16]{3,2,1,0:T(2,128)} %param.18) | copy-start | bytes 388
  44.5 14.3 %copy-start.9 = (s32[1,1,2,96]{3,2,1,0:T(2,128)S(1)}, s32[1,1,2,96]{3,2,1,0:T(2,128)}, u32[]{:S(2)}) copy-start(s32[1,1,2,96]{3,2,1,0:T(2,128)} %param.21) | copy-start | bytes 2308
  63.6 12.6 %copy-start = (f32[2,2048]{1,0:T(2,128)S(1)}, f32[2,2048]{1,0:T(2,128)}, u32[]{:S(2)}) copy-start(f32[2,2048]{1,0:T(2,128)} %refs_2_.1) | copy-start | bytes 49156
  63.6 12.6 %copy-start.2 = (f32[2048]{0:T(1024)S(1)}, f32[2048]{0:T(1024)}, u32[]{:S(2)}) copy-start(f32[2048]{0:T(1024)} %param.23) | copy-start | bytes 24580

commit v7 on v6

--- a/solution.py
+++ b/solution.py
@@ -190,7 +190,7 @@
     snd_ref[...] = (snd[0:N_ROW] * 256.0 + snd[N_ROW : 2 * N_ROW]).astype(i32)
 
 
-def make_index(gathered, slip, ctl=()):
+def make_index(gathered, ctl=()):
     square = jax.ShapeDtypeStruct((N_ROW, LANES), i32)
     return call(
         index_kernel,
@@ -199,7 +199,7 @@
         (jax.ShapeDtypeStruct((N_COL, LANES), i32), square, jax.ShapeDtypeStruct((1, LANES), i32)),
         (VMEM, VMEM, VMEM),
         "index",
-        ((slip, 0, CLU_DEV),),
+        span=SPAN,
     )
 
 
@@ -240,22 +240,23 @@
         (jax.ShapeDtypeStruct((N_ROW * CAP_ROW, 2, B), f32),),
         (VMEM,),
         "forward",
-        span=SPAN,
     )[0]
 
 
-CHUNK = 64
+CHUNK = 128
+
+
+def near_sum(near_ref, at, rows, x):
+    prod = near_ref[at, rows, 0:B] * x[0:1, :] + near_ref[at, rows, B : 2 * B] * x[1:2, :]
+    return jnp.sum(prod[:, 0:LANES] + prod[:, LANES:B], axis=1, keepdims=True)
 
 
 def add_near(acc_ref, near_ref, at, x, row):
-    x0, x1 = x[0:1, :], x[1:2, :]
     here = iota((CHUNK, LANES), 1) == row
     for s in range(0, 2 * B, CHUNK):
         rows = pl.ds(s, CHUNK)
-        prod = near_ref[at, rows, 0:B] * x0 + near_ref[at, rows, B : 2 * B] * x1
-        total = jnp.sum(prod[:, 0:LANES] + prod[:, LANES:B], axis=1, keepdims=True)
         old = acc_ref[rows, :]
-        acc_ref[rows, :] = jnp.where(here, old + total, old)
+        acc_ref[rows, :] = jnp.where(here, old + near_sum(near_ref, at, rows, x), old)
 
 
 def add_far(out_ref, left_ref, right_ref, at, x, row):
@@ -293,7 +294,6 @@
     for copy in small:
         copy.start()
     out_ref[...] = jnp.zeros_like(out_ref)
-    acc_ref[...] = jnp.zeros_like(acc_ref)
     for copy in small:
         copy.wait()
     over = asked_ref[0, LANES - 1]
@@ -321,13 +321,18 @@
         return 0
 
     lax.fori_loop(0, N_ROW, some_far, 0)
-    def two_near(q, _):
-        for t in range(2):
-            n = 2 * q + t
-            add_near(acc_ref, near_ref, n, x_ref[pos_ref[0, n]], near_row_ref[0, n])
+    xs = [x_ref[pos_ref[0, n]] for n in range(NEAR)]
+    lane = iota((CHUNK, LANES), 1)
+
+    def some_rows(q, _):
+        rows = pl.ds(pl.multiple_of(q * CHUNK, CHUNK), CHUNK)
+        acc = jnp.zeros((CHUNK, LANES), f32)
+        for n in range(NEAR):
+            acc = jnp.where(lane == near_row_ref[0, n], acc + near_sum(near_ref, n, rows, xs[n]), acc)
+        acc_ref[rows, :] = acc
         return 0
 
-    lax.fori_loop(0, NEAR // 2, two_near, 0)
+    lax.fori_loop(0, 2 * B // CHUNK, some_rows, 0)
     out_ref[...] = out_ref[...] + acc_ref[...].T
     for copy in told:
         copy.wait()
@@ -487,9 +492,9 @@
     )
 
     def fetch(*ctl):
-        req, snd, pos, slip_held = make_index(gathered, slip, ctl)
+        req, snd, pos = make_index(gathered, ctl)
         asked = lax.all_to_all(req, "col", 0, 0, tiled=True)
-        got = lax.all_to_all(gather_rows(asked, slip_held), "col", 0, 0, tiled=True)
+        got = lax.all_to_all(gather_rows(asked, slip), "col", 0, 0, tiled=True)
         return lax.all_to_all(forward_rows(snd, got), "row", 0, 0, tiled=True), pos, asked
 
     x, pos, asked = fetch()

time: 77.2 us -> 76.7 us (level)
  no operation moved by 1% of the time
where the time goes in v7:
time: 76.7 us; the launch traced here: 76.4 us
  blocking collectives  65.9 us (86%)
  Pallas kernels  8.87 us (12%)
  between operations  0.85 us (1%)
    all_to_all x1, blocking collectives, fetch(): asked = lax.all_to_all(req, 'col', 0, 0, tiled=True)  15.7 us
    all_to_all x1, blocking collectives, fetch(): got = lax.all_to_all(gather_rows(asked, slip), 'col', 0, 0, tiled=True)  15.6 us
    all_to_all x1, blocking collectives, fetch(): lax.all_to_all(forward_rows(snd, got), 'row', 0, 0, tiled=True)  12.8 us
    all_to_all x1, blocking collectives, body(): parts = lax.all_to_all(summed, 'col', 0, 0, tiled=True)  11.9 us
    all_to_all x1, blocking collectives, body(): lax.all_to_all(make_payload(source_cluster, near_index, far_index), 'row'...  9.89 us
    pallas_call x5, Pallas kernels, call(): pl.pallas_call(run, out_shape=tuple(outs) + tuple((pltpu.VMEM((size,) + o...  4.47 us
    pallas_call x1, Pallas kernels, block_sums(): pl.pallas_call(blocks_kernel, out_shape=(jax.ShapeDtypeStruct((RC_DEV, 2...  4.4 us

profile of v7, /device:TPU:0, one launch (start us, length us, event | category | flops | bytes accessed | tf_op | source)
XLA Modules:
  0.0 76.4 jit_solution(1367359241070155228)
XLA Ops:
  0.6 0.7 payload.1
  1.4 0.0 slice-start
  1.4 9.9 %all_to_all.57.refs_0_ = s32[8,8,128]{2,1,0:T(8,128)S(1)} all-to-all(s32[8,8,128]{2,1,0:T(8,128)S(1)} %payload.1), channel_id=1, replica_groups=mesh['row'=8,'col'=16] {'row'}, dimensions={0} | all-to-all | bytes 65536 | tf_op jit(solution)/shard_map/all_to_all | solution.py:490
  11.3 0.0 copy-start.7
  11.3 1.0 %index.5 = (s32[16,128]{1,0:T(8,128)S(1)}, s32[8,128]{1,0:T(8,128)S(1)}, s32[1,128]{1,0:T(1,128)S(1)}) custom-call(s32[8,8,128]{2,1,0:T(8,128)S(1)} %all_to_all.57.refs_0_), custom_call_target="tpu_custom_call" | custom-call | flops 15000000512 | tf_op jit(solution)/shard_map/index/pallas_call | solution.py:65
  12.3 0.0 copy-start.1
  12.4 0.0 copy-start.3
  12.4 0.0 copy-start.4
  12.4 0.0 copy-start.5
  12.4 0.0 copy-start.6
  12.4 0.0 copy-start.9
  12.4 0.0 copy-start.10
  12.4 15.7 %all_to_all.58 = s32[16,1,128]{2,1,0:T(1,128)S(1)} all-to-all(s32[16,1,128]{2,1,0:T(1,128)S(1)} %bitcast.39), channel_id=1, replica_groups=mesh['row'=8,'col'=16] {'col'}, dimensions={0} | all-to-all | bytes 16384 | tf_op jit(solution)/shard_map/all_to_all | solution.py:496
  28.1 1.1 %gather.5 = f32[384,2,256]{2,1,0:T(2,128)S(1)} custom-call(s32[16,128]{1,0:T(8,128)S(1)} %bitcast.35, f32[512,2,256]{2,1,0:T(2,128)S(1)} %bitcast.48), custom_call_target="tpu_custom_call" | custom-call | tf_op jit(solution)/shard_map/gather/pallas_call | solution.py:65
  29.2 15.6 %all_to_all.59.refs_1_ = f32[384,2,256]{2,1,0:T(2,128)S(1)} all-to-all(f32[384,2,256]{2,1,0:T(2,128)S(1)} %gather.5), channel_id=1, replica_groups=mesh['row'=8,'col'=16] {'col'}, dimensions={0} | all-to-all | bytes 1572864 | tf_op jit(solution)/shard_map/all_to_all | solution.py:497
  44.9 0.9 %forward.5 = f32[256,2,256]{2,1,0:T(2,128)S(1)} custom-call(s32[8,128]{1,0:T(8,128)S(1)} %get-tuple-element.135.refs_0_, f32[384,2,256]{2,1,0:T(2,128)S(1)} %all_to_all.59.refs_1_), custom_call_target="tpu_custom_call" | custom-call | tf_op jit(solution)/shard_map/forward/pallas_call | solution.py:65
  45.8 12.8 %all_to_all.60.x_ref = f32[256,2,256]{2,1,0:T(2,128)S(1)} all-to-all(f32[256,2,256]{2,1,0:T(2,128)S(1)} %forward.5), channel_id=1, replica_groups=mesh['row'=8,'col'=16] {'row'}, dimensions={0} | all-to-all | bytes 1048576 | tf_op jit(solution)/shard_map/all_to_all | solution.py:498
  58.6 0.0 slice-done.1
  58.7 4.4 %blocks.1 = (f32[128,512]{1,0:T(8,128)S(1)}, f32[3,16,128]{2,1,0:T(8,128)S(1)}, s32[1]{0:T(128)}, s32[1]{0:T(128)}) custom-call(s32[1,128]{1,0:T(1,128)S(1)} %get-tuple-element.133.pos_hbm, s32[16,128]{1,0:T(8,128)S(1)} %bitcast.36, s32[2,16]{1,0:T(2,128)S(1)} %bitcast.52, s32[2,96]{1,0:T(2,128)S(1)} %bitcast.55, f32[40]{0:T(128)S(1)} %copy-done.3, ...), custom_call_target="tpu_custom_call" | custom-call | tf_op jit(solution)/shard_map/blocks/pallas_call | solution.py:344
  63.1 0.0 copy-start
  63.1 0.0 copy-start.2
  63.1 0.7 while.12
  63.8 11.9 %all_to_all.61.refs_1_ = f32[16,8,512]{2,1,0:T(8,128)S(1)} all-to-all(f32[16,8,512]{2,1,0:T(8,128)S(1)} %bitcast.50), channel_id=1, replica_groups=mesh['row'=8,'col'=16] {'col'}, dimensions={0} | all-to-all | bytes 524288 | tf_op jit(solution)/shard_map/all_to_all | solution.py:517
  75.7 0.7 finish.1
  (19 shorter events, 0.0 us)
Async XLA Ops:
  1.4 57.2 %slice-start = ((s8[16777216]{0:T(1024)(128)(4,1)}), s8[4194304]{0:T(1024)(128)(4,1)S(1)}, s32[]{:S(2)}) async-start(s8[16777216]{0:T(1024)(128)(4,1)} %bitcast.41), calls=%async_computation.8 | async-start | bytes 8388608
  11.3 16.8 %copy-start.8 = (f32[2,131072]{1,0:T(2,128)S(1)}, f32[2,131072]{1,0:T(2,128)}, u32[]{:S(2)}) copy-start(f32[2,131072]{1,0:T(2,128)} %param.15) | copy-start | bytes 3145732
  11.3 47.3 %slice-start.1 = ((s8[16777216]{0:T(1024)(128)(4,1)}), s8[4194304]{0:T(1024)(128)(4,1)S(1)}, s32[]{:S(2)}) async-start(s8[16777216]{0:T(1024)(128)(4,1)} %bitcast.41), calls=%async_computation.9 | async-start | bytes 8388608
  11.3 47.3 %slice-start.2 = ((s8[16777216]{0:T(1024)(128)(4,1)}), s8[4194304]{0:T(1024)(128)(4,1)S(1)}, s32[]{:S(2)}) async-start(s8[16777216]{0:T(1024)(128)(4,1)} %bitcast.41), calls=%async_computation.10 | async-start | bytes 8388608
  11.3 47.3 %slice-start.3 = ((s8[16777216]{0:T(1024)(128)(4,1)}), s8[4194304]{0:T(1024)(128)(4,1)S(1)}, s32[]{:S(2)}) async-start(s8[16777216]{0:T(1024)(128)(4,1)} %bitcast.41), calls=%async_computation.11 | async-start | bytes 8388608
  11.3 47.3 %copy-start.7 = (bf16[1,1,96,32,512]{4,3,2,1,0:T(8,128)(2,1)S(1)}, bf16[1,1,96,32,512]{4,3,2,1,0:T(8,128)(2,1)}, u32[]{:S(2)}) copy-start(bf16[1,1,96,32,512]{4,3,2,1,0:T(8,128)(2,1)} %param.20) | copy-start | bytes 9437188
  12.3 46.3 %copy-start.1 = (s32[2048]{0:T(1024)S(1)}, s32[2048]{0:T(1024)}, u32[]{:S(2)}) copy-start(s32[2048]{0:T(1024)} %param.24) | copy-start | bytes 24580
  12.4 46.3 %copy-start.3 = (f32[40]{0:T(128)S(1)}, f32[40]{0:T(128)}, u32[]{:S(2)}) copy-start(f32[40]{0:T(128)} %a_hbm.1) | copy-start | bytes 484
  12.4 46.3 %copy-start.4 = (f32[40]{0:T(128)S(1)}, f32[40]{0:T(128)}, u32[]{:S(2)}) copy-start(f32[40]{0:T(128)} %b_hbm.1) | copy-start | bytes 484
  12.4 46.3 %copy-start.5 = (f32[40]{0:T(128)S(1)}, f32[40]{0:T(128)}, u32[]{:S(2)}) copy-start(f32[40]{0:T(128)} %s_hbm.1) | copy-start | bytes 484
  12.4 46.3 %copy-start.6 = (bf16[1,1,96,32,512]{4,3,2,1,0:T(8,128)(2,1)S(1)}, bf16[1,1,96,32,512]{4,3,2,1,0:T(8,128)(2,1)}, u32[]{:S(2)}) copy-start(bf16[1,1,96,32,512]{4,3,2,1,0:T(8,128)(2,1)} %param.19) | copy-start | bytes 9437188
  12.4 46.3 %copy-start.9 = (s32[1,1,2,16]{3,2,1,0:T(2,128)S(1)}, s32[1,1,2,16]{3,2,1,0:T(2,128)}, u32[]{:S(2)}) copy-start(s32[1,1,2,16]{3,2,1,0:T(2,128)} %param.18) | copy-start | bytes 388
  12.4 46.3 %copy-start.10 = (s32[1,1,2,96]{3,2,1,0:T(2,128)S(1)}, s32[1,1,2,96]{3,2,1,0:T(2,128)}, u32[]{:S(2)}) copy-start(s32[1,1,2,96]{3,2,1,0:T(2,128)} %param.21) | copy-start | bytes 2308
  63.1 12.6 %copy-start = (f32[2,2048]{1,0:T(2,128)S(1)}, f32[2,2048]{1,0:T(2,128)}, u32[]{:S(2)}) copy-start(f32[2,2048]{1,0:T(2,128)} %refs_2_.1) | copy-start | bytes 49156
  63.1 12.6 %copy-start.2 = (f32[2048]{0:T(1024)S(1)}, f32[2048]{0:T(1024)}, u32[]{:S(2)}) copy-start(f32[2048]{0:T(1024)} %param.23) | copy-start | bytes 24580

commit v8 on v7

--- a/solution.py
+++ b/solution.py
@@ -45,34 +45,15 @@
     return pltpu.with_memory_space_constraint(x, pltpu.HBM)
 
 
-def call(kernel, ins, specs, outs, out_specs, name, staged=(), span=0):
-    count, given, made = len(staged), len(ins), len(outs)
-
-    def run(*refs):
-        held = refs[given + count + made : given + 2 * count + made]
-        copies = [
-            pltpu.make_async_copy(one.at[pl.ds(first, size)], to, done)
-            for one, to, done, (_, first, size) in zip(
-                refs[given : given + count], held, refs[given + 2 * count + made :], staged
-            )
-        ]
-        for copy in copies:
-            copy.start()
-        kernel(*refs[:given], *refs[given + count : given + count + made])
-        for copy in copies:
-            copy.wait()
-
+def call(kernel, ins, specs, outs, out_specs, name):
     return pl.pallas_call(
-        run,
-        out_shape=tuple(outs)
-        + tuple(pltpu.VMEM((size,) + one.shape[1:], one.dtype) for one, _, size in staged),
-        in_specs=list(specs) + [HBM] * count,
-        out_specs=tuple(out_specs) + (VMEM,) * count,
-        scratch_shapes=[pltpu.SemaphoreType.DMA] * count,
+        kernel,
+        out_shape=tuple(outs),
+        in_specs=list(specs),
+        out_specs=tuple(out_specs),
         compiler_params=SMALL,
-        cost_estimate=pl.CostEstimate(flops=span, transcendentals=0, bytes_accessed=0) if span else None,
         name=name,
-    )(*ins, *(in_hbm(one) for one, _, _ in staged))
+    )(*ins)
 
 
 def iota(shape, dim):
@@ -123,8 +104,19 @@
 
 
 def index_kernel(g_ref, *refs):
-    req_ref, snd_ref, pos_ref = refs[-3:]
-    ctl = (refs[0][0] - 1, refs[1][0]) if len(refs) > 3 else None
+    near_hbm, far_hbm = refs[0:2]
+    req_ref, snd_out, pos_out, near_out, far_out, snd_ref, pos_ref, sems = refs[-8:]
+    ctl = (refs[2][0] - 1, refs[3][0]) if len(refs) > 10 else None
+    clusters = [
+        pltpu.make_async_copy(near_hbm, near_out, sems.at[0]),
+        pltpu.make_async_copy(far_hbm, far_out, sems.at[1]),
+    ]
+    lists = [
+        pltpu.make_async_copy(pos_ref, pos_out, sems.at[2]),
+        pltpu.make_async_copy(snd_ref, snd_out, sems.at[3]),
+    ]
+    for copy in clusters:
+        copy.start()
     rho = g_ref[0, 6:7, :]
     tables = jnp.concatenate([g_ref[:, q, :] for q in range(4)], axis=1)
     n = iota((N_ROW, LANES), 1)
@@ -173,34 +165,44 @@
     over = jnp.where(fits[0], 0, jnp.where(fits[1] & fits[2], 1, 2))
     pos = jnp.clip(owner_row * CAP_ROW + slot2, 0, N_ROW * CAP_ROW - 1)
     pos_ref[...] = jnp.sum(jnp.where(row_label == rho, pos, 0).astype(f32), axis=0, keepdims=True).astype(i32)
+    lists[0].start()
     mine = owner_row == rho
     pos1 = jnp.clip((owner & (N_COL - 1)) * CAP_COL + slot1, 0, N_COL * CAP_COL - 1)
+    snd = jnp.zeros((2 * N_ROW, LANES), f32)
+    for r in range(N_ROW):
+        value = split(jnp.where((row_label == r) & mine[r : r + 1, :], pos1[r : r + 1, :], 0))
+        put = exact(sub == jnp.where(slot2[r : r + 1, :] < CAP_ROW, slot2[r : r + 1, :], -1))
+        snd = snd + lax.dot_general(exact(value), put, NT, preferred_element_type=f32)
+    snd_ref[...] = (snd[0:N_ROW] * 256.0 + snd[N_ROW : 2 * N_ROW]).astype(i32)
+    lists[1].start()
     req = jnp.zeros((2 * N_COL, LANES), f32)
-    snd = jnp.zeros((2 * N_ROW, LANES), f32)
     for r in range(N_ROW):
         sel = to_col[r * N_COL : (r + 1) * N_COL] > 0.5
         value = split(jnp.where(sel, local[r : r + 1, :], 0))
         put = exact(sub == jnp.where(slot1[r : r + 1, :] < CAP_COL, slot1[r : r + 1, :], -1))
         req = req + lax.dot_general(exact(value), put, NT, preferred_element_type=f32)
-        value = split(jnp.where((row_label == r) & mine[r : r + 1, :], pos1[r : r + 1, :], 0))
-        put = exact(sub == jnp.where(slot2[r : r + 1, :] < CAP_ROW, slot2[r : r + 1, :], -1))
-        snd = snd + lax.dot_general(exact(value), put, NT, preferred_element_type=f32)
     req = (req[0:N_COL] * 256.0 + req[N_COL : 2 * N_COL]).astype(i32)
     req_ref[...] = jnp.where(iota((N_COL, LANES), 1) == LANES - 1, over, req)
-    snd_ref[...] = (snd[0:N_ROW] * 256.0 + snd[N_ROW : 2 * N_ROW]).astype(i32)
-
-
-def make_index(gathered, ctl=()):
-    square = jax.ShapeDtypeStruct((N_ROW, LANES), i32)
-    return call(
+    for copy in clusters + lists:
+        copy.wait()
+
+
+def make_index(gathered, near_index, far_index, ctl=()):
+    scalars = ((N_ROW, LANES), (1, LANES), near_index.shape, far_index.shape)
+    return pl.pallas_call(
         index_kernel,
-        (gathered, *ctl),
-        [VMEM] + [SMEM] * len(ctl),
-        (jax.ShapeDtypeStruct((N_COL, LANES), i32), square, jax.ShapeDtypeStruct((1, LANES), i32)),
-        (VMEM, VMEM, VMEM),
-        "index",
-        span=SPAN,
-    )
+        out_shape=(jax.ShapeDtypeStruct((N_COL, LANES), i32), *(pltpu.SMEM(one, i32) for one in scalars)),
+        in_specs=[VMEM, HBM, HBM] + [SMEM] * len(ctl),
+        out_specs=(VMEM, SMEM, SMEM, SMEM, SMEM),
+        scratch_shapes=[
+            pltpu.VMEM((N_ROW, LANES), i32),
+            pltpu.VMEM((1, LANES), i32),
+            pltpu.SemaphoreType.DMA((4,)),
+        ],
+        compiler_params=SMALL,
+        cost_estimate=pl.CostEstimate(flops=SPAN, transcendentals=0, bytes_accessed=0),
+        name="index",
+    )(gathered, in_hbm(near_index), in_hbm(far_index), *ctl)
 
 
 def gather_kernel(idx_ref, slip_ref, out_ref):
@@ -271,29 +273,28 @@
 
 
 def blocks_kernel(
-    pos_hbm, asked_hbm, near_row_hbm, far_row_hbm, a_hbm, b_hbm, s_hbm, fault_ref, x_ref, left_ref,
+    pos_ref, near_row_ref, far_row_ref, asked_hbm, a_hbm, b_hbm, s_hbm, fault_ref, x_ref, left_ref,
     right_ref, near_ref,
     out_ref, param_ref, rounds_out, to_do_out,
-    acc_ref, pos_ref, asked_ref, near_row_ref, far_row_ref, a_ref, b_ref, s_ref,
-    rounds_ref, small_sems, out_sems,
+    acc_ref, asked_ref, a_ref, b_ref, s_ref, rounds_ref, small_sems, out_sems,
 ):
     small = [
         pltpu.make_async_copy(one, to, small_sems.at[k])
         for k, (one, to) in enumerate(
-            [
-                (pos_hbm, pos_ref),
-                (far_row_hbm, far_row_ref),
-                (near_row_hbm, near_row_ref),
-                (asked_hbm, asked_ref),
-                (a_hbm, a_ref),
-                (b_hbm, b_ref),
-                (s_hbm, s_ref),
-            ]
+            [(asked_hbm, asked_ref), (a_hbm, a_ref), (b_hbm, b_ref), (s_hbm, s_ref)]
         )
     ]
     for copy in small:
         copy.start()
     out_ref[...] = jnp.zeros_like(out_ref)
+
+    def some_far(p, _):
+        for t in range(FP):
+            n = p * FP + t
+            add_far(out_ref, left_ref, right_ref, n, x_ref[pos_ref[0, NEAR + n]], far_row_ref[0, n])
+        return 0
+
+    lax.fori_loop(0, N_ROW, some_far, 0)
     for copy in small:
         copy.wait()
     over = asked_ref[0, LANES - 1]
@@ -314,13 +315,6 @@
     for k in range(3):
         param_ref[k] = found[k]
 
-    def some_far(p, _):
-        for t in range(FP):
-            n = p * FP + t
-            add_far(out_ref, left_ref, right_ref, n, x_ref[pos_ref[0, NEAR + n]], far_row_ref[0, n])
-        return 0
-
-    lax.fori_loop(0, N_ROW, some_far, 0)
     xs = [x_ref[pos_ref[0, n]] for n in range(NEAR)]
     lane = iota((CHUNK, LANES), 1)
 
@@ -338,9 +332,9 @@
         copy.wait()
 
 
-def block_sums(pos, asked, near_index, far_index, params, fault, x, left, right, near):
+def block_sums(lists, asked, params, fault, x, left, right, near):
     one = jax.ShapeDtypeStruct((1,), i32)
-    small = (pos, asked, near_index, far_index, *params)
+    small = (asked, *params)
     return pl.pallas_call(
         blocks_kernel,
         out_shape=(
@@ -349,7 +343,7 @@
             one,
             one,
         ),
-        in_specs=[ANY] * len(small) + [VMEM, VMEM, VMEM, VMEM, VMEM],
+        in_specs=[SMEM] * 3 + [ANY] * len(small) + [VMEM] * 5,
         out_specs=(VMEM, VMEM, ANY, ANY),
         scratch_shapes=[
             pltpu.VMEM((2 * B, LANES), f32),
@@ -360,7 +354,7 @@
         ],
         compiler_params=pltpu.CompilerParams(vmem_limit_bytes=28 * 1024 * 1024),
         name="blocks",
-    )(*small, fault, x, left, right, near)
+    )(*lists, *small, fault, x, left, right, near)
 
 
 def pick_kernel(to_do_ref, rounds_ref, pos_ref, x_ref, out_ref):
@@ -492,23 +486,21 @@
     )
 
     def fetch(*ctl):
-        req, snd, pos = make_index(gathered, ctl)
+        req, snd, *lists = make_index(gathered, near_index, far_index, ctl)
         asked = lax.all_to_all(req, "col", 0, 0, tiled=True)
         got = lax.all_to_all(gather_rows(asked, slip), "col", 0, 0, tiled=True)
-        return lax.all_to_all(forward_rows(snd, got), "row", 0, 0, tiled=True), pos, asked
-
-    x, pos, asked = fetch()
+        return lax.all_to_all(forward_rows(snd, got), "row", 0, 0, tiled=True), lists, asked
+
+    x, lists, asked = fetch()
     faults = (direct_effect, evolution_effect, normal_stress)
     fault = fault_of_row.reshape(-1, LANES)
-    fast, params, rounds, to_do = block_sums(
-        pos, asked, near_index, far_index, faults, fault, x, left, right, near
-    )
+    fast, params, rounds, to_do = block_sums(lists, asked, faults, fault, x, left, right, near)
 
     def one_round(carry):
         to_do, total = carry
         now = to_do.reshape(1)
-        x, pos, _ = fetch(now, rounds)
-        rows = pick_rows(now, rounds, pos, x)
+        x, lists, _ = fetch(now, rounds)
+        rows = pick_rows(now, rounds, lists[0], x)
         n = jnp.arange(LANES, dtype=i32)[None, :]
         part = round_sums(n, near_index, far_index, rows, near, left, right)
         return to_do - 1, jnp.where(to_do == rounds[0], 0.0, total) + part

time: 76.7 us -> 76 us (level)
  no operation moved by 1% of the time
where the time goes in v8:
time: 76 us; the launch traced here: 75.7 us
  blocking collectives  65.9 us (87%)
  Pallas kernels  8.18 us (11%)
  between operations  0.85 us (1%)
    all_to_all x1, blocking collectives, fetch(): asked = lax.all_to_all(req, 'col', 0, 0, tiled=True)  15.7 us
    all_to_all x1, blocking collectives, fetch(): got = lax.all_to_all(gather_rows(asked, slip), 'col', 0, 0, tiled=True)  15.6 us
    all_to_all x1, blocking collectives, fetch(): lax.all_to_all(forward_rows(snd, got), 'row', 0, 0, tiled=True)  12.8 us
    all_to_all x1, blocking collectives, body(): parts = lax.all_to_all(summed, 'col', 0, 0, tiled=True)  11.9 us
    all_to_all x1, blocking collectives, body(): lax.all_to_all(make_payload(source_cluster, near_index, far_index), 'row'...  9.89 us
    pallas_call x1, Pallas kernels, block_sums(): pl.pallas_call(blocks_kernel, out_shape=(jax.ShapeDtypeStruct((RC_DEV, 2...  3.69 us
    pallas_call x4, Pallas kernels, call(): pl.pallas_call(kernel, out_shape=tuple(outs), in_specs=list(specs), out_s...  2.82 us
    pallas_call x1, Pallas kernels, make_index(): pl.pallas_call(index_kernel, out_shape=(jax.ShapeDtypeStruct((N_COL, LANE...  1.67 us

profile of v8, /device:TPU:0, one launch (start us, length us, event | category | flops | bytes accessed | tf_op | source)
XLA Modules:
  0.0 75.7 jit_solution(6187615486069992845)
XLA Ops:
  0.6 0.7 payload.1
  1.4 0.0 slice-start
  1.4 9.9 %all_to_all.57.g_ref = s32[8,8,128]{2,1,0:T(8,128)S(1)} all-to-all(s32[8,8,128]{2,1,0:T(8,128)S(1)} %payload.1), channel_id=1, replica_groups=mesh['row'=8,'col'=16] {'row'}, dimensions={0} | all-to-all | bytes 65536 | tf_op jit(solution)/shard_map/all_to_all | solution.py:484
  11.3 0.0 copy-start.7
  11.3 1.7 %index.5 = (s32[16,128]{1,0:T(8,128)S(1)}, s32[8,128]{1,0:T(8,128)S(4)}, s32[1,128]{1,0:T(1,128)S(4)}, s32[2,16]{1,0:T(2,128)S(4)}, s32[2,96]{1,0:T(2,128)S(4)}) custom-call(s32[8,8,128]{2,1,0:T(8,128)S(1)} %all_to_all.57.g_ref, s32[2,16]{1,0:T(2,128)} %bitcast.52, s32[2,96]{1,0:T(2,128)} %bitcast.58), custom_call_target="tpu_custom_call" | custom-call | flops 15000000512 | tf_op jit(solution)/shard_map/index/pallas_call | solution.py:192
  13.0 0.0 copy-start.1
  13.0 0.0 copy-start.3
  13.0 0.0 copy-start.4
  13.0 0.0 copy-start.5
  13.0 0.0 copy-start.6
  13.0 15.7 %all_to_all.58 = s32[16,1,128]{2,1,0:T(1,128)S(1)} all-to-all(s32[16,1,128]{2,1,0:T(1,128)S(1)} %bitcast.39), channel_id=1, replica_groups=mesh['row'=8,'col'=16] {'col'}, dimensions={0} | all-to-all | bytes 16384 | tf_op jit(solution)/shard_map/all_to_all | solution.py:490
  28.7 1.1 %gather.5 = f32[384,2,256]{2,1,0:T(2,128)S(1)} custom-call(s32[16,128]{1,0:T(8,128)S(1)} %bitcast.35, f32[512,2,256]{2,1,0:T(2,128)S(1)} %bitcast.48), custom_call_target="tpu_custom_call" | custom-call | tf_op jit(solution)/shard_map/gather/pallas_call | solution.py:49
  29.8 15.6 %all_to_all.59.got_ref = f32[384,2,256]{2,1,0:T(2,128)S(1)} all-to-all(f32[384,2,256]{2,1,0:T(2,128)S(1)} %gather.5), channel_id=1, replica_groups=mesh['row'=8,'col'=16] {'col'}, dimensions={0} | all-to-all | bytes 1572864 | tf_op jit(solution)/shard_map/all_to_all | solution.py:491
  45.5 0.3 forward.5
  45.8 12.8 %all_to_all.60.x_ref = f32[256,2,256]{2,1,0:T(2,128)S(1)} all-to-all(f32[256,2,256]{2,1,0:T(2,128)S(1)} %forward.5), channel_id=1, replica_groups=mesh['row'=8,'col'=16] {'row'}, dimensions={0} | all-to-all | bytes 1048576 | tf_op jit(solution)/shard_map/all_to_all | solution.py:492
  58.6 0.0 slice-done
  58.7 0.0 copy-start.9
  58.7 0.0 copy-start.11
  58.7 3.7 %blocks.1 = (f32[128,512]{1,0:T(8,128)S(1)}, f32[3,16,128]{2,1,0:T(8,128)S(1)}, s32[1]{0:T(128)}, s32[1]{0:T(128)}) custom-call(s32[1,128]{1,0:T(1,128)S(4)} %get-tuple-element.135.pos_ref, s32[2,16]{1,0:T(2,128)S(4)} %get-tuple-element.136.near_row_ref, s32[2,96]{1,0:T(2,128)S(4)} %get-tuple-element.137.far_row_ref, s32[16,128]{1,0:T(8,128)S(1)} %bitcast.36, ...), custom_call_target="tpu_custom_call" | custom-call | tf_op jit(solution)/shard_map/blocks/pallas_call | solution.py:338
  62.4 0.0 copy-start
  62.4 0.0 copy-start.2
  62.4 0.7 while.12
  63.1 11.9 %all_to_all.61.parts_ref = f32[16,8,512]{2,1,0:T(8,128)S(1)} all-to-all(f32[16,8,512]{2,1,0:T(8,128)S(1)} %bitcast.50), channel_id=1, replica_groups=mesh['row'=8,'col'=16] {'col'}, dimensions={0} | all-to-all | bytes 524288 | tf_op jit(solution)/shard_map/all_to_all | solution.py:509
  75.0 0.7 finish.1
  (19 shorter events, 0.0 us)
Async XLA Ops:
  1.4 57.2 %slice-start = ((s8[16777216]{0:T(1024)(128)(4,1)}), s8[4194304]{0:T(1024)(128)(4,1)S(1)}, s32[]{:S(2)}) async-start(s8[16777216]{0:T(1024)(128)(4,1)} %bitcast.41), calls=%async_computation.8 | async-start | bytes 8388608
  11.3 17.4 %copy-start.8 = (f32[2,131072]{1,0:T(2,128)S(1)}, f32[2,131072]{1,0:T(2,128)}, u32[]{:S(2)}) copy-start(f32[2,131072]{1,0:T(2,128)} %param.15) | copy-start | bytes 3145732
  11.3 47.3 %slice-start.1 = ((s8[16777216]{0:T(1024)(128)(4,1)}), s8[4194304]{0:T(1024)(128)(4,1)S(1)}, s32[]{:S(2)}) async-start(s8[16777216]{0:T(1024)(128)(4,1)} %bitcast.41), calls=%async_computation.9 | async-start | bytes 8388608
  11.3 47.3 %slice-start.2 = ((s8[16777216]{0:T(1024)(128)(4,1)}), s8[4194304]{0:T(1024)(128)(4,1)S(1)}, s32[]{:S(2)}) async-start(s8[16777216]{0:T(1024)(128)(4,1)} %bitcast.41), calls=%async_computation.10 | async-start | bytes 8388608
  11.3 47.3 %slice-start.3 = ((s8[16777216]{0:T(1024)(128)(4,1)}), s8[4194304]{0:T(1024)(128)(4,1)S(1)}, s32[]{:S(2)}) async-start(s8[16777216]{0:T(1024)(128)(4,1)} %bitcast.41), calls=%async_computation.11 | async-start | bytes 8388608
  11.3 47.3 %copy-start.7 = (bf16[1,1,96,32,512]{4,3,2,1,0:T(8,128)(2,1)S(1)}, bf16[1,1,96,32,512]{4,3,2,1,0:T(8,128)(2,1)}, u32[]{:S(2)}) copy-start(bf16[1,1,96,32,512]{4,3,2,1,0:T(8,128)(2,1)} %param.20) | copy-start | bytes 9437188
  13.0 45.6 %copy-start.1 = (s32[2048]{0:T(1024)S(1)}, s32[2048]{0:T(1024)}, u32[]{:S(2)}) copy-start(s32[2048]{0:T(1024)} %param.24) | copy-start | bytes 24580
  13.0 45.6 %copy-start.3 = (f32[40]{0:T(128)S(1)}, f32[40]{0:T(128)}, u32[]{:S(2)}) copy-start(f32[40]{0:T(128)} %a_hbm.1) | copy-start | bytes 484
  13.0 45.6 %copy-start.4 = (f32[40]{0:T(128)S(1)}, f32[40]{0:T(128)}, u32[]{:S(2)}) copy-start(f32[40]{0:T(128)} %b_hbm.1) | copy-start | bytes 484
  13.0 45.6 %copy-start.5 = (f32[40]{0:T(128)S(1)}, f32[40]{0:T(128)}, u32[]{:S(2)}) copy-start(f32[40]{0:T(128)} %s_hbm.1) | copy-start | bytes 484
  13.0 45.6 %copy-start.6 = (bf16[1,1,96,32,512]{4,3,2,1,0:T(8,128)(2,1)S(1)}, bf16[1,1,96,32,512]{4,3,2,1,0:T(8,128)(2,1)}, u32[]{:S(2)}) copy-start(bf16[1,1,96,32,512]{4,3,2,1,0:T(8,128)(2,1)} %param.19) | copy-start | bytes 9437188
  58.7 3.7 %copy-start.9 = (s32[1,1,2,16]{3,2,1,0:T(2,128)S(1)}, s32[1,1,2,16]{3,2,1,0:T(2,128)}, u32[]{:S(2)}) copy-start(s32[1,1,2,16]{3,2,1,0:T(2,128)} %param.18) | copy-start | bytes 388
  58.7 3.7 %copy-start.11 = (s32[1,1,2,96]{3,2,1,0:T(2,128)S(1)}, s32[1,1,2,96]{3,2,1,0:T(2,128)}, u32[]{:S(2)}) copy-start(s32[1,1,2,96]{3,2,1,0:T(2,128)} %param.21) | copy-start | bytes 2308
  62.4 12.6 %copy-start = (f32[2,2048]{1,0:T(2,128)S(1)}, f32[2,2048]{1,0:T(2,128)}, u32[]{:S(2)}) copy-start(f32[2,2048]{1,0:T(2,128)} %stress_ref.1) | copy-start | bytes 49156
  62.4 12.6 %copy-start.2 = (f32[2048]{0:T(1024)S(1)}, f32[2048]{0:T(1024)}, u32[]{:S(2)}) copy-start(f32[2048]{0:T(1024)} %param.23) | copy-start | bytes 24580

commit v9 on v8

--- a/solution.py
+++ b/solution.py
@@ -104,19 +104,8 @@
 
 
 def index_kernel(g_ref, *refs):
-    near_hbm, far_hbm = refs[0:2]
-    req_ref, snd_out, pos_out, near_out, far_out, snd_ref, pos_ref, sems = refs[-8:]
-    ctl = (refs[2][0] - 1, refs[3][0]) if len(refs) > 10 else None
-    clusters = [
-        pltpu.make_async_copy(near_hbm, near_out, sems.at[0]),
-        pltpu.make_async_copy(far_hbm, far_out, sems.at[1]),
-    ]
-    lists = [
-        pltpu.make_async_copy(pos_ref, pos_out, sems.at[2]),
-        pltpu.make_async_copy(snd_ref, snd_out, sems.at[3]),
-    ]
-    for copy in clusters:
-        copy.start()
+    req_ref, snd_ref, pos_ref = refs[-3:]
+    ctl = (refs[0][0] - 1, refs[1][0]) if len(refs) > 3 else None
     rho = g_ref[0, 6:7, :]
     tables = jnp.concatenate([g_ref[:, q, :] for q in range(4)], axis=1)
     n = iota((N_ROW, LANES), 1)
@@ -165,7 +154,6 @@
     over = jnp.where(fits[0], 0, jnp.where(fits[1] & fits[2], 1, 2))
     pos = jnp.clip(owner_row * CAP_ROW + slot2, 0, N_ROW * CAP_ROW - 1)
     pos_ref[...] = jnp.sum(jnp.where(row_label == rho, pos, 0).astype(f32), axis=0, keepdims=True).astype(i32)
-    lists[0].start()
     mine = owner_row == rho
     pos1 = jnp.clip((owner & (N_COL - 1)) * CAP_COL + slot1, 0, N_COL * CAP_COL - 1)
     snd = jnp.zeros((2 * N_ROW, LANES), f32)
@@ -174,7 +162,6 @@
         put = exact(sub == jnp.where(slot2[r : r + 1, :] < CAP_ROW, slot2[r : r + 1, :], -1))
         snd = snd + lax.dot_general(exact(value), put, NT, preferred_element_type=f32)
     snd_ref[...] = (snd[0:N_ROW] * 256.0 + snd[N_ROW : 2 * N_ROW]).astype(i32)
-    lists[1].start()
     req = jnp.zeros((2 * N_COL, LANES), f32)
     for r in range(N_ROW):
         sel = to_col[r * N_COL : (r + 1) * N_COL] > 0.5
@@ -183,46 +170,53 @@
         req = req + lax.dot_general(exact(value), put, NT, preferred_element_type=f32)
     req = (req[0:N_COL] * 256.0 + req[N_COL : 2 * N_COL]).astype(i32)
     req_ref[...] = jnp.where(iota((N_COL, LANES), 1) == LANES - 1, over, req)
-    for copy in clusters + lists:
-        copy.wait()
-
-
-def make_index(gathered, near_index, far_index, ctl=()):
-    scalars = ((N_ROW, LANES), (1, LANES), near_index.shape, far_index.shape)
+
+
+def make_index(gathered, ctl=()):
     return pl.pallas_call(
         index_kernel,
-        out_shape=(jax.ShapeDtypeStruct((N_COL, LANES), i32), *(pltpu.SMEM(one, i32) for one in scalars)),
-        in_specs=[VMEM, HBM, HBM] + [SMEM] * len(ctl),
-        out_specs=(VMEM, SMEM, SMEM, SMEM, SMEM),
-        scratch_shapes=[
-            pltpu.VMEM((N_ROW, LANES), i32),
-            pltpu.VMEM((1, LANES), i32),
-            pltpu.SemaphoreType.DMA((4,)),
-        ],
+        out_shape=(
+            jax.ShapeDtypeStruct((N_COL, LANES), i32),
+            jax.ShapeDtypeStruct((N_ROW, LANES), i32),
+            jax.ShapeDtypeStruct((1, LANES), i32),
+        ),
+        in_specs=[VMEM] + [SMEM] * len(ctl),
+        out_specs=(VMEM, VMEM, VMEM),
         compiler_params=SMALL,
         cost_estimate=pl.CostEstimate(flops=SPAN, transcendentals=0, bytes_accessed=0),
         name="index",
-    )(gathered, in_hbm(near_index), in_hbm(far_index), *ctl)
-
-
-def gather_kernel(idx_ref, slip_ref, out_ref):
+    )(gathered, *ctl)
+
+
+def gather_kernel(idx_ref, slip_ref, *refs):
+    lists, out_ref, held, sems = refs[:4], refs[4], refs[5:9], refs[9]
+    copies = [pltpu.make_async_copy(one, to, sems.at[k]) for k, (one, to) in enumerate(zip(lists, held))]
+    for copy in copies:
+        copy.start()
+
     def one_col(c, _):
         for k in range(CAP_COL):
             out_ref[c * CAP_COL + k] = slip_ref[idx_ref[c, k]]
         return 0
 
     lax.fori_loop(0, N_COL, one_col, 0)
-
-
-def gather_rows(idx, slip):
-    return call(
+    for copy in copies:
+        copy.wait()
+
+
+def gather_rows(idx, slip, lists):
+    return pl.pallas_call(
         gather_kernel,
-        (idx, slip),
-        [SMEM, VMEM],
-        (jax.ShapeDtypeStruct((N_COL * CAP_COL, 2, B), f32),),
-        (VMEM,),
-        "gather",
-    )[0]
+        out_shape=(
+            jax.ShapeDtypeStruct((N_COL * CAP_COL, 2, B), f32),
+            *(pltpu.SMEM(one.shape, i32) for one in lists),
+        ),
+        in_specs=[SMEM, VMEM] + [ANY] * len(lists),
+        out_specs=(VMEM,) + (SMEM,) * len(lists),
+        scratch_shapes=[pltpu.SemaphoreType.DMA((len(lists),))],
+        compiler_params=SMALL,
+        name="gather",
+    )(idx, slip, *lists)
 
 
 def forward_kernel(idx_ref, got_ref, out_ref):
@@ -486,9 +480,10 @@
     )
 
     def fetch(*ctl):
-        req, snd, *lists = make_index(gathered, near_index, far_index, ctl)
+        req, snd, pos = make_index(gathered, ctl)
         asked = lax.all_to_all(req, "col", 0, 0, tiled=True)
-        got = lax.all_to_all(gather_rows(asked, slip), "col", 0, 0, tiled=True)
+        reply, snd, *lists = gather_rows(asked, slip, (snd, pos, near_index, far_index))
+        got = lax.all_to_all(reply, "col", 0, 0, tiled=True)
         return lax.all_to_all(forward_rows(snd, got), "row", 0, 0, tiled=True), lists, asked
 
     x, lists, asked = fetch()

time: 76 us -> 75.6 us (level)
    pallas_call x0 -> x1, Pallas kernels: none -> 1.34 us  [gather_rows(): pl.pallas_call(gather_kernel, out_shape=(jax.ShapeDtypeStruct((N_COL * CA...]
    pallas_call x4 -> x3, Pallas kernels: 2.82 us -> 1.68 us  [call(): pl.pallas_call(kernel, out_shape=tuple(outs), in_specs=list(specs), out_s...]
where the time goes in v9:
time: 75.6 us; the launch traced here: 75.3 us
  blocking collectives  65.9 us (87%)
  Pallas kernels  7.81 us (10%)
  between operations  0.82 us (1%)
    all_to_all x1, blocking collectives, fetch(): asked = lax.all_to_all(req, 'col', 0, 0, tiled=True)  15.7 us
    all_to_all x1, blocking collectives, fetch(): got = lax.all_to_all(reply, 'col', 0, 0, tiled=True)  15.6 us
    all_to_all x1, blocking collectives, fetch(): lax.all_to_all(forward_rows(snd, got), 'row', 0, 0, tiled=True)  12.8 us
    all_to_all x1, blocking collectives, body(): parts = lax.all_to_all(summed, 'col', 0, 0, tiled=True)  11.9 us
    all_to_all x1, blocking collectives, body(): lax.all_to_all(make_payload(source_cluster, near_index, far_index), 'row'...  9.89 us
    pallas_call x1, Pallas kernels, block_sums(): pl.pallas_call(blocks_kernel, out_shape=(jax.ShapeDtypeStruct((RC_DEV, 2...  3.72 us
    pallas_call x3, Pallas kernels, call(): pl.pallas_call(kernel, out_shape=tuple(outs), in_specs=list(specs), out_s...  1.68 us

profile of v9, /device:TPU:0, one launch (start us, length us, event | category | flops | bytes accessed | tf_op | source)
XLA Modules:
  0.0 75.3 jit_solution(10115358593854629242)
XLA Ops:
  0.6 0.7 payload.1
  1.4 0.0 slice-start
  1.4 9.9 %all_to_all.57.g_ref = s32[8,8,128]{2,1,0:T(8,128)S(1)} all-to-all(s32[8,8,128]{2,1,0:T(8,128)S(1)} %payload.1), channel_id=1, replica_groups=mesh['row'=8,'col'=16] {'row'}, dimensions={0} | all-to-all | bytes 65536 | tf_op jit(solution)/shard_map/all_to_all | solution.py:478
  11.3 0.0 slice-start.2
  11.3 0.0 slice-start.3
  11.3 0.0 copy-start.7
  11.3 1.1 %index.5 = (s32[16,128]{1,0:T(8,128)S(1)}, s32[8,128]{1,0:T(8,128)S(1)}, s32[1,128]{1,0:T(1,128)S(1)}) custom-call(s32[8,8,128]{2,1,0:T(8,128)S(1)} %all_to_all.57.g_ref), custom_call_target="tpu_custom_call" | custom-call | flops 15000000512 | tf_op jit(solution)/shard_map/index/pallas_call | solution.py:176
  12.4 0.0 copy-start.3
  12.4 0.0 copy-start.4
  12.4 0.0 copy-start.5
  12.4 0.0 copy-start.6
  12.5 15.7 %all_to_all.58 = s32[16,1,128]{2,1,0:T(1,128)S(1)} all-to-all(s32[16,1,128]{2,1,0:T(1,128)S(1)} %bitcast.39), channel_id=1, replica_groups=mesh['row'=8,'col'=16] {'col'}, dimensions={0} | all-to-all | bytes 16384 | tf_op jit(solution)/shard_map/all_to_all | solution.py:484
  28.1 1.3 %gather.5 = (f32[384,2,256]{2,1,0:T(2,128)S(1)}, s32[8,128]{1,0:T(8,128)S(4)}, s32[1,128]{1,0:T(1,128)S(4)}, s32[2,16]{1,0:T(2,128)S(4)}, s32[2,96]{1,0:T(2,128)S(4)}) custom-call(s32[16,128]{1,0:T(8,128)S(1)} %bitcast.35, f32[512,2,256]{2,1,0:T(2,128)S(1)} %bitcast.48, s32[8,128]{1,0:T(8,128)S(1)} %get-tuple-element.142.refs_0_, ...), custom_call_target="tpu_custom_call" | custom-call | tf_op jit(solution)/shard_map/gather/pallas_call | solution.py:208
  29.5 15.6 %all_to_all.59.got_ref = f32[384,2,256]{2,1,0:T(2,128)S(1)} all-to-all(f32[384,2,256]{2,1,0:T(2,128)S(1)} %get-tuple-element.148), channel_id=1, replica_groups=mesh['row'=8,'col'=16] {'col'}, dimensions={0} | all-to-all | bytes 1572864 | tf_op jit(solution)/shard_map/all_to_all | solution.py:486
  45.1 0.3 forward.5
  45.4 12.8 %all_to_all.60.x_ref = f32[256,2,256]{2,1,0:T(2,128)S(1)} all-to-all(f32[256,2,256]{2,1,0:T(2,128)S(1)} %forward.5), channel_id=1, replica_groups=mesh['row'=8,'col'=16] {'row'}, dimensions={0} | all-to-all | bytes 1048576 | tf_op jit(solution)/shard_map/all_to_all | solution.py:487
  58.2 0.0 slice-done.3
  58.2 0.0 copy-done.7
  58.3 3.7 %blocks.1 = (f32[128,512]{1,0:T(8,128)S(1)}, f32[3,16,128]{2,1,0:T(8,128)S(1)}, s32[1]{0:T(128)}, s32[1]{0:T(128)}) custom-call(s32[1,128]{1,0:T(1,128)S(4)} %get-tuple-element.144.pos_ref, s32[2,16]{1,0:T(2,128)S(4)} %get-tuple-element.145.near_row_ref, s32[2,96]{1,0:T(2,128)S(4)} %get-tuple-element.146.far_row_ref, s32[16,128]{1,0:T(8,128)S(1)} %bitcast.36, ...), custom_call_target="tpu_custom_call" | custom-call | tf_op jit(solution)/shard_map/blocks/pallas_call | solution.py:332
  62.0 0.0 copy-start
  62.0 0.0 copy-start.2
  62.0 0.7 while.12
  62.7 11.9 %all_to_all.61.parts_ref = f32[16,8,512]{2,1,0:T(8,128)S(1)} all-to-all(f32[16,8,512]{2,1,0:T(8,128)S(1)} %bitcast.50), channel_id=1, replica_groups=mesh['row'=8,'col'=16] {'col'}, dimensions={0} | all-to-all | bytes 524288 | tf_op jit(solution)/shard_map/all_to_all | solution.py:504
  74.7 0.7 finish.1
  (19 shorter events, 0.0 us)
Async XLA Ops:
  1.4 56.9 %slice-start = ((s8[16777216]{0:T(1024)(128)(4,1)}), s8[4194304]{0:T(1024)(128)(4,1)S(1)}, s32[]{:S(2)}) async-start(s8[16777216]{0:T(1024)(128)(4,1)} %bitcast.41), calls=%async_computation.8 | async-start | bytes 8388608
  11.3 16.9 %copy-start.8 = (f32[2,131072]{1,0:T(2,128)S(1)}, f32[2,131072]{1,0:T(2,128)}, u32[]{:S(2)}) copy-start(f32[2,131072]{1,0:T(2,128)} %param.15) | copy-start | bytes 3145732
  11.3 16.9 %copy-start.9 = (s32[1,1,2,16]{3,2,1,0:T(2,128)S(1)}, s32[1,1,2,16]{3,2,1,0:T(2,128)}, u32[]{:S(2)}) copy-start(s32[1,1,2,16]{3,2,1,0:T(2,128)} %param.18) | copy-start | bytes 388
  11.3 16.9 %copy-start.10 = (s32[1,1,2,96]{3,2,1,0:T(2,128)S(1)}, s32[1,1,2,96]{3,2,1,0:T(2,128)}, u32[]{:S(2)}) copy-start(s32[1,1,2,96]{3,2,1,0:T(2,128)} %param.21) | copy-start | bytes 2308
  11.3 46.9 %slice-start.1 = ((s8[16777216]{0:T(1024)(128)(4,1)}), s8[4194304]{0:T(1024)(128)(4,1)S(1)}, s32[]{:S(2)}) async-start(s8[16777216]{0:T(1024)(128)(4,1)} %bitcast.41), calls=%async_computation.9 | async-start | bytes 8388608
  11.3 46.9 %slice-start.2 = ((s8[16777216]{0:T(1024)(128)(4,1)}), s8[4194304]{0:T(1024)(128)(4,1)S(1)}, s32[]{:S(2)}) async-start(s8[16777216]{0:T(1024)(128)(4,1)} %bitcast.41), calls=%async_computation.10 | async-start | bytes 8388608
  11.3 46.9 %slice-start.3 = ((s8[16777216]{0:T(1024)(128)(4,1)}), s8[4194304]{0:T(1024)(128)(4,1)S(1)}, s32[]{:S(2)}) async-start(s8[16777216]{0:T(1024)(128)(4,1)} %bitcast.41), calls=%async_computation.11 | async-start | bytes 8388608
  11.3 46.9 %copy-start.7 = (bf16[1,1,96,32,512]{4,3,2,1,0:T(8,128)(2,1)S(1)}, bf16[1,1,96,32,512]{4,3,2,1,0:T(8,128)(2,1)}, u32[]{:S(2)}) copy-start(bf16[1,1,96,32,512]{4,3,2,1,0:T(8,128)(2,1)} %param.20) | copy-start | bytes 9437188
  12.4 45.9 %copy-start.1 = (s32[2048]{0:T(1024)S(1)}, s32[2048]{0:T(1024)}, u32[]{:S(2)}) copy-start(s32[2048]{0:T(1024)} %param.24) | copy-start | bytes 24580
  12.4 45.9 %copy-start.3 = (f32[40]{0:T(128)S(1)}, f32[40]{0:T(128)}, u32[]{:S(2)}) copy-start(f32[40]{0:T(128)} %a_hbm.1) | copy-start | bytes 484
  12.4 45.8 %copy-start.4 = (f32[40]{0:T(128)S(1)}, f32[40]{0:T(128)}, u32[]{:S(2)}) copy-start(f32[40]{0:T(128)} %b_hbm.1) | copy-start | bytes 484
  12.4 45.8 %copy-start.5 = (f32[40]{0:T(128)S(1)}, f32[40]{0:T(128)}, u32[]{:S(2)}) copy-start(f32[40]{0:T(128)} %s_hbm.1) | copy-start | bytes 484
  12.4 45.8 %copy-start.6 = (bf16[1,1,96,32,512]{4,3,2,1,0:T(8,128)(2,1)S(1)}, bf16[1,1,96,32,512]{4,3,2,1,0:T(8,128)(2,1)}, u32[]{:S(2)}) copy-start(bf16[1,1,96,32,512]{4,3,2,1,0:T(8,128)(2,1)} %param.19) | copy-start | bytes 9437188
  62.0 12.6 %copy-start = (f32[2,2048]{1,0:T(2,128)S(1)}, f32[2,2048]{1,0:T(2,128)}, u32[]{:S(2)}) copy-start(f32[2,2048]{1,0:T(2,128)} %stress_ref.1) | copy-start | bytes 49156
  62.0 12.6 %copy-start.2 = (f32[2048]{0:T(1024)S(1)}, f32[2048]{0:T(1024)}, u32[]{:S(2)}) copy-start(f32[2048]{0:T(1024)} %param.23) | copy-start | bytes 24580

commit v10 on v9

--- a/solution.py
+++ b/solution.py
@@ -156,20 +156,21 @@
     pos_ref[...] = jnp.sum(jnp.where(row_label == rho, pos, 0).astype(f32), axis=0, keepdims=True).astype(i32)
     mine = owner_row == rho
     pos1 = jnp.clip((owner & (N_COL - 1)) * CAP_COL + slot1, 0, N_COL * CAP_COL - 1)
-    snd = jnp.zeros((2 * N_ROW, LANES), f32)
+    place = iota((CAP_ROW, LANES), 0)
+    snd = jnp.zeros((2 * N_ROW, CAP_ROW), f32)
+    req = jnp.zeros((2 * N_COL, CAP_ROW), f32)
     for r in range(N_ROW):
         value = split(jnp.where((row_label == r) & mine[r : r + 1, :], pos1[r : r + 1, :], 0))
-        put = exact(sub == jnp.where(slot2[r : r + 1, :] < CAP_ROW, slot2[r : r + 1, :], -1))
+        put = exact(place == slot2[r : r + 1, :])
         snd = snd + lax.dot_general(exact(value), put, NT, preferred_element_type=f32)
-    snd_ref[...] = (snd[0:N_ROW] * 256.0 + snd[N_ROW : 2 * N_ROW]).astype(i32)
-    req = jnp.zeros((2 * N_COL, LANES), f32)
-    for r in range(N_ROW):
         sel = to_col[r * N_COL : (r + 1) * N_COL] > 0.5
         value = split(jnp.where(sel, local[r : r + 1, :], 0))
-        put = exact(sub == jnp.where(slot1[r : r + 1, :] < CAP_COL, slot1[r : r + 1, :], -1))
+        put = exact(place == jnp.where(slot1[r : r + 1, :] < CAP_COL, slot1[r : r + 1, :], -1))
         req = req + lax.dot_general(exact(value), put, NT, preferred_element_type=f32)
-    req = (req[0:N_COL] * 256.0 + req[N_COL : 2 * N_COL]).astype(i32)
-    req_ref[...] = jnp.where(iota((N_COL, LANES), 1) == LANES - 1, over, req)
+    snd_ref[...] = jnp.zeros_like(snd_ref)
+    snd_ref[:, 0:CAP_ROW] = (snd[0:N_ROW] * 256.0 + snd[N_ROW : 2 * N_ROW]).astype(i32)
+    req_ref[...] = jnp.full(req_ref.shape, over, i32)
+    req_ref[:, 0:CAP_ROW] = (req[0:N_COL] * 256.0 + req[N_COL : 2 * N_COL]).astype(i32)
 
 
 def make_index(gathered, ctl=()):
@@ -188,11 +189,13 @@
     )(gathered, *ctl)
 
 
-def gather_kernel(idx_ref, slip_ref, *refs):
-    lists, out_ref, held, sems = refs[:4], refs[4], refs[5:9], refs[9]
-    copies = [pltpu.make_async_copy(one, to, sems.at[k]) for k, (one, to) in enumerate(zip(lists, held))]
+def gather_kernel(idx_hbm, slip_ref, *refs):
+    lists, out_ref, held, idx_ref, sems = refs[:4], refs[4], refs[5:9], refs[9], refs[10]
+    pairs = [(idx_hbm, idx_ref), *zip(lists, held)]
+    copies = [pltpu.make_async_copy(one, to, sems.at[k]) for k, (one, to) in enumerate(pairs)]
     for copy in copies:
         copy.start()
+    copies[0].wait()
 
     def one_col(c, _):
         for k in range(CAP_COL):
@@ -200,7 +203,7 @@
         return 0
 
     lax.fori_loop(0, N_COL, one_col, 0)
-    for copy in copies:
+    for copy in copies[1:]:
         copy.wait()
 
 
@@ -211,9 +214,9 @@
             jax.ShapeDtypeStruct((N_COL * CAP_COL, 2, B), f32),
             *(pltpu.SMEM(one.shape, i32) for one in lists),
         ),
-        in_specs=[SMEM, VMEM] + [ANY] * len(lists),
+        in_specs=[ANY, VMEM] + [ANY] * len(lists),
         out_specs=(VMEM,) + (SMEM,) * len(lists),
-        scratch_shapes=[pltpu.SemaphoreType.DMA((len(lists),))],
+        scratch_shapes=[pltpu.SMEM(idx.shape, i32), pltpu.SemaphoreType.DMA((1 + len(lists),))],
         compiler_params=SMALL,
         name="gather",
     )(idx, slip, *lists)
@@ -288,7 +291,7 @@
             add_far(out_ref, left_ref, right_ref, n, x_ref[pos_ref[0, NEAR + n]], far_row_ref[0, n])
         return 0
 
-    lax.fori_loop(0, N_ROW, some_far, 0)
+    lax.fori_loop(0, N_ROW, some_far, 0, unroll=4)
     for copy in small:
         copy.wait()
     over = asked_ref[0, LANES - 1]
@@ -320,7 +323,7 @@
         acc_ref[rows, :] = acc
         return 0
 
-    lax.fori_loop(0, 2 * B // CHUNK, some_rows, 0)
+    lax.fori_loop(0, 2 * B // CHUNK, some_rows, 0, unroll=2)
     out_ref[...] = out_ref[...] + acc_ref[...].T
     for copy in told:
         copy.wait()

time: 75.6 us -> 75.1 us (level)
  no operation moved by 1% of the time
where the time goes in v10:
time: 75.1 us; the launch traced here: 74.8 us
  blocking collectives  65.9 us (88%)
  Pallas kernels  7.27 us (10%)
  between operations  0.84 us (1%)
    all_to_all x1, blocking collectives, fetch(): asked = lax.all_to_all(req, 'col', 0, 0, tiled=True)  15.7 us
    all_to_all x1, blocking collectives, fetch(): got = lax.all_to_all(reply, 'col', 0, 0, tiled=True)  15.6 us
    all_to_all x1, blocking collectives, fetch(): lax.all_to_all(forward_rows(snd, got), 'row', 0, 0, tiled=True)  12.8 us
    all_to_all x1, blocking collectives, body(): parts = lax.all_to_all(summed, 'col', 0, 0, tiled=True)  11.9 us
    all_to_all x1, blocking collectives, body(): lax.all_to_all(make_payload(source_cluster, near_index, far_index), 'row'...  9.89 us
    pallas_call x1, Pallas kernels, block_sums(): pl.pallas_call(blocks_kernel, out_shape=(jax.ShapeDtypeStruct((RC_DEV, 2...  3.54 us
    pallas_call x3, Pallas kernels, call(): pl.pallas_call(kernel, out_shape=tuple(outs), in_specs=list(specs), out_s...  1.68 us

profile of v10, /device:TPU:0, one launch (start us, length us, event | category | flops | bytes accessed | tf_op | source)
XLA Modules:
  0.0 74.8 jit_solution(13159306475001320040)
XLA Ops:
  0.6 0.7 payload.1
  1.4 0.0 slice-start
  1.4 9.9 %all_to_all.57.g_ref = s32[8,8,128]{2,1,0:T(8,128)S(1)} all-to-all(s32[8,8,128]{2,1,0:T(8,128)S(1)} %payload.1), channel_id=1, replica_groups=mesh['row'=8,'col'=16] {'row'}, dimensions={0} | all-to-all | bytes 65536 | tf_op jit(solution)/shard_map/all_to_all | solution.py:481
  11.3 0.0 slice-start.2
  11.3 0.0 slice-start.3
  11.3 0.0 copy-start.7
  11.3 0.8 %index.5 = (s32[16,128]{1,0:T(8,128)S(1)}, s32[8,128]{1,0:T(8,128)S(1)}, s32[1,128]{1,0:T(1,128)S(1)}) custom-call(s32[8,8,128]{2,1,0:T(8,128)S(1)} %all_to_all.57.g_ref), custom_call_target="tpu_custom_call" | custom-call | flops 15000000512 | tf_op jit(solution)/shard_map/index/pallas_call | solution.py:177
  12.2 0.0 copy-start.1
  12.2 0.0 copy-start.3
  12.2 0.0 copy-start.4
  12.2 0.0 copy-start.5
  12.2 0.0 copy-start.6
  12.2 15.7 %all_to_all.58 = s32[16,1,128]{2,1,0:T(1,128)S(1)} all-to-all(s32[16,1,128]{2,1,0:T(1,128)S(1)} %bitcast.39), channel_id=1, replica_groups=mesh['row'=8,'col'=16] {'col'}, dimensions={0} | all-to-all | bytes 16384 | tf_op jit(solution)/shard_map/all_to_all | solution.py:487
  27.9 1.2 %gather.5 = (f32[384,2,256]{2,1,0:T(2,128)S(1)}, s32[8,128]{1,0:T(8,128)S(4)}, s32[1,128]{1,0:T(1,128)S(4)}, s32[2,16]{1,0:T(2,128)S(4)}, s32[2,96]{1,0:T(2,128)S(4)}) custom-call(s32[16,128]{1,0:T(8,128)S(1)} %bitcast.35, f32[512,2,256]{2,1,0:T(2,128)S(1)} %bitcast.48, s32[8,128]{1,0:T(8,128)S(1)} %get-tuple-element.142.refs_0_, ...), custom_call_target="tpu_custom_call" | custom-call | tf_op jit(solution)/shard_map/gather/pallas_call | solution.py:211
  29.1 15.6 %all_to_all.59.got_ref = f32[384,2,256]{2,1,0:T(2,128)S(1)} all-to-all(f32[384,2,256]{2,1,0:T(2,128)S(1)} %get-tuple-element.148), channel_id=1, replica_groups=mesh['row'=8,'col'=16] {'col'}, dimensions={0} | all-to-all | bytes 1572864 | tf_op jit(solution)/shard_map/all_to_all | solution.py:489
  44.8 0.3 forward.5
  45.0 12.8 %all_to_all.60.x_ref = f32[256,2,256]{2,1,0:T(2,128)S(1)} all-to-all(f32[256,2,256]{2,1,0:T(2,128)S(1)} %forward.5), channel_id=1, replica_groups=mesh['row'=8,'col'=16] {'row'}, dimensions={0} | all-to-all | bytes 1048576 | tf_op jit(solution)/shard_map/all_to_all | solution.py:490
  57.9 0.0 slice-done
  57.9 3.5 %blocks.1 = (f32[128,512]{1,0:T(8,128)S(1)}, f32[3,16,128]{2,1,0:T(8,128)S(1)}, s32[1]{0:T(128)}, s32[1]{0:T(128)}) custom-call(s32[1,128]{1,0:T(1,128)S(4)} %get-tuple-element.144.pos_ref, s32[2,16]{1,0:T(2,128)S(4)} %get-tuple-element.145.near_row_ref, s32[2,96]{1,0:T(2,128)S(4)} %get-tuple-element.146.far_row_ref, s32[16,128]{1,0:T(8,128)S(1)} %bitcast.36, ...), custom_call_target="tpu_custom_call" | custom-call | tf_op jit(solution)/shard_map/blocks/pallas_call | solution.py:335
  61.5 0.0 copy-start
  61.5 0.0 copy-start.2
  61.5 0.7 while.12
  62.2 11.9 %all_to_all.61.parts_ref = f32[16,8,512]{2,1,0:T(8,128)S(1)} all-to-all(f32[16,8,512]{2,1,0:T(8,128)S(1)} %bitcast.50), channel_id=1, replica_groups=mesh['row'=8,'col'=16] {'col'}, dimensions={0} | all-to-all | bytes 524288 | tf_op jit(solution)/shard_map/all_to_all | solution.py:507
  74.1 0.7 finish.1
  (19 shorter events, 0.0 us)
Async XLA Ops:
  1.4 56.5 %slice-start = ((s8[16777216]{0:T(1024)(128)(4,1)}), s8[4194304]{0:T(1024)(128)(4,1)S(1)}, s32[]{:S(2)}) async-start(s8[16777216]{0:T(1024)(128)(4,1)} %bitcast.41), calls=%async_computation.8 | async-start | bytes 8388608
  11.3 16.6 %copy-start.8 = (f32[2,131072]{1,0:T(2,128)S(1)}, f32[2,131072]{1,0:T(2,128)}, u32[]{:S(2)}) copy-start(f32[2,131072]{1,0:T(2,128)} %param.15) | copy-start | bytes 3145732
  11.3 16.6 %copy-start.9 = (s32[1,1,2,16]{3,2,1,0:T(2,128)S(1)}, s32[1,1,2,16]{3,2,1,0:T(2,128)}, u32[]{:S(2)}) copy-start(s32[1,1,2,16]{3,2,1,0:T(2,128)} %param.18) | copy-start | bytes 388
  11.3 16.6 %copy-start.10 = (s32[1,1,2,96]{3,2,1,0:T(2,128)S(1)}, s32[1,1,2,96]{3,2,1,0:T(2,128)}, u32[]{:S(2)}) copy-start(s32[1,1,2,96]{3,2,1,0:T(2,128)} %param.21) | copy-start | bytes 2308
  11.3 46.6 %slice-start.1 = ((s8[16777216]{0:T(1024)(128)(4,1)}), s8[4194304]{0:T(1024)(128)(4,1)S(1)}, s32[]{:S(2)}) async-start(s8[16777216]{0:T(1024)(128)(4,1)} %bitcast.41), calls=%async_computation.9 | async-start | bytes 8388608
  11.3 46.6 %slice-start.2 = ((s8[16777216]{0:T(1024)(128)(4,1)}), s8[4194304]{0:T(1024)(128)(4,1)S(1)}, s32[]{:S(2)}) async-start(s8[16777216]{0:T(1024)(128)(4,1)} %bitcast.41), calls=%async_computation.10 | async-start | bytes 8388608
  11.3 46.6 %slice-start.3 = ((s8[16777216]{0:T(1024)(128)(4,1)}), s8[4194304]{0:T(1024)(128)(4,1)S(1)}, s32[]{:S(2)}) async-start(s8[16777216]{0:T(1024)(128)(4,1)} %bitcast.41), calls=%async_computation.11 | async-start | bytes 8388608
  11.3 46.6 %copy-start.7 = (bf16[1,1,96,32,512]{4,3,2,1,0:T(8,128)(2,1)S(1)}, bf16[1,1,96,32,512]{4,3,2,1,0:T(8,128)(2,1)}, u32[]{:S(2)}) copy-start(bf16[1,1,96,32,512]{4,3,2,1,0:T(8,128)(2,1)} %param.20) | copy-start | bytes 9437188
  12.2 45.7 %copy-start.1 = (s32[2048]{0:T(1024)S(1)}, s32[2048]{0:T(1024)}, u32[]{:S(2)}) copy-start(s32[2048]{0:T(1024)} %param.24) | copy-start | bytes 24580
  12.2 45.7 %copy-start.3 = (f32[40]{0:T(128)S(1)}, f32[40]{0:T(128)}, u32[]{:S(2)}) copy-start(f32[40]{0:T(128)} %a_hbm.1) | copy-start | bytes 484
  12.2 45.7 %copy-start.4 = (f32[40]{0:T(128)S(1)}, f32[40]{0:T(128)}, u32[]{:S(2)}) copy-start(f32[40]{0:T(128)} %b_hbm.1) | copy-start | bytes 484
  12.2 45.7 %copy-start.5 = (f32[40]{0:T(128)S(1)}, f32[40]{0:T(128)}, u32[]{:S(2)}) copy-start(f32[40]{0:T(128)} %s_hbm.1) | copy-start | bytes 484
  12.2 45.7 %copy-start.6 = (bf16[1,1,96,32,512]{4,3,2,1,0:T(8,128)(2,1)S(1)}, bf16[1,1,96,32,512]{4,3,2,1,0:T(8,128)(2,1)}, u32[]{:S(2)}) copy-start(bf16[1,1,96,32,512]{4,3,2,1,0:T(8,128)(2,1)} %param.19) | copy-start | bytes 9437188
  61.5 12.6 %copy-start = (f32[2,2048]{1,0:T(2,128)S(1)}, f32[2,2048]{1,0:T(2,128)}, u32[]{:S(2)}) copy-start(f32[2,2048]{1,0:T(2,128)} %stress_ref.1) | copy-start | bytes 49156
  61.5 12.6 %copy-start.2 = (f32[2048]{0:T(1024)S(1)}, f32[2048]{0:T(1024)}, u32[]{:S(2)}) copy-start(f32[2048]{0:T(1024)} %param.23) | copy-start | bytes 24580

commit v11 on v10

--- a/solution.py
+++ b/solution.py
@@ -283,15 +283,19 @@
     ]
     for copy in small:
         copy.start()
-    out_ref[...] = jnp.zeros_like(out_ref)
-
-    def some_far(p, _):
-        for t in range(FP):
-            n = p * FP + t
-            add_far(out_ref, left_ref, right_ref, n, x_ref[pos_ref[0, NEAR + n]], far_row_ref[0, n])
+    xs = [x_ref[pos_ref[0, n]] for n in range(NEAR)]
+    lane = iota((CHUNK, LANES), 1)
+
+    def some_rows(q, _):
+        rows = pl.ds(pl.multiple_of(q * CHUNK, CHUNK), CHUNK)
+        acc = jnp.zeros((CHUNK, LANES), f32)
+        for n in range(NEAR):
+            acc = jnp.where(lane == near_row_ref[0, n], acc + near_sum(near_ref, n, rows, xs[n]), acc)
+        acc_ref[rows, :] = acc
         return 0
 
-    lax.fori_loop(0, N_ROW, some_far, 0, unroll=4)
+    lax.fori_loop(0, 2 * B // CHUNK, some_rows, 0, unroll=2)
+    out_ref[...] = acc_ref[...].T
     for copy in small:
         copy.wait()
     over = asked_ref[0, LANES - 1]
@@ -312,19 +316,13 @@
     for k in range(3):
         param_ref[k] = found[k]
 
-    xs = [x_ref[pos_ref[0, n]] for n in range(NEAR)]
-    lane = iota((CHUNK, LANES), 1)
-
-    def some_rows(q, _):
-        rows = pl.ds(pl.multiple_of(q * CHUNK, CHUNK), CHUNK)
-        acc = jnp.zeros((CHUNK, LANES), f32)
-        for n in range(NEAR):
-            acc = jnp.where(lane == near_row_ref[0, n], acc + near_sum(near_ref, n, rows, xs[n]), acc)
-        acc_ref[rows, :] = acc
+    def some_far(p, _):
+        for t in range(FP):
+            n = p * FP + t
+            add_far(out_ref, left_ref, right_ref, n, x_ref[pos_ref[0, NEAR + n]], far_row_ref[0, n])
         return 0
 
-    lax.fori_loop(0, 2 * B // CHUNK, some_rows, 0, unroll=2)
-    out_ref[...] = out_ref[...] + acc_ref[...].T
+    lax.fori_loop(0, N_ROW, some_far, 0, unroll=4)
     for copy in told:
         copy.wait()
 

time: 75.1 us -> 75.1 us (level)
  no operation moved by 1% of the time
where the time goes in v11:
time: 75.1 us; the launch traced here: 74.8 us
  blocking collectives  65.9 us (88%)
  Pallas kernels  7.28 us (10%)
  between operations  0.84 us (1%)
    all_to_all x1, blocking collectives, fetch(): asked = lax.all_to_all(req, 'col', 0, 0, tiled=True)  15.7 us
    all_to_all x1, blocking collectives, fetch(): got = lax.all_to_all(reply, 'col', 0, 0, tiled=True)  15.6 us
    all_to_all x1, blocking collectives, fetch(): lax.all_to_all(forward_rows(snd, got), 'row', 0, 0, tiled=True)  12.8 us
    all_to_all x1, blocking collectives, body(): parts = lax.all_to_all(summed, 'col', 0, 0, tiled=True)  11.9 us
    all_to_all x1, blocking collectives, body(): lax.all_to_all(make_payload(source_cluster, near_index, far_index), 'row'...  9.89 us
    pallas_call x1, Pallas kernels, block_sums(): pl.pallas_call(blocks_kernel, out_shape=(jax.ShapeDtypeStruct((RC_DEV, 2...  3.55 us
    pallas_call x3, Pallas kernels, call(): pl.pallas_call(kernel, out_shape=tuple(outs), in_specs=list(specs), out_s...  1.68 us

profile of v11, /device:TPU:0, one launch (start us, length us, event | category | flops | bytes accessed | tf_op | source)
XLA Modules:
  0.0 74.8 jit_solution(243594073432813464)
XLA Ops:
  0.6 0.7 payload.1
  1.4 0.0 slice-start
  1.4 9.9 %all_to_all.57.g_ref = s32[8,8,128]{2,1,0:T(8,128)S(1)} all-to-all(s32[8,8,128]{2,1,0:T(8,128)S(1)} %payload.1), channel_id=1, replica_groups=mesh['row'=8,'col'=16] {'row'}, dimensions={0} | all-to-all | bytes 65536 | tf_op jit(solution)/shard_map/all_to_all | solution.py:479
  11.3 0.0 slice-start.2
  11.3 0.0 slice-start.3
  11.3 0.0 copy-start.7
  11.3 0.8 %index.5 = (s32[16,128]{1,0:T(8,128)S(1)}, s32[8,128]{1,0:T(8,128)S(1)}, s32[1,128]{1,0:T(1,128)S(1)}) custom-call(s32[8,8,128]{2,1,0:T(8,128)S(1)} %all_to_all.57.g_ref), custom_call_target="tpu_custom_call" | custom-call | flops 15000000512 | tf_op jit(solution)/shard_map/index/pallas_call | solution.py:177
  12.2 0.0 copy-start.1
  12.2 0.0 copy-start.3
  12.2 0.0 copy-start.4
  12.2 0.0 copy-start.5
  12.2 0.0 copy-start.6
  12.2 15.7 %all_to_all.58 = s32[16,1,128]{2,1,0:T(1,128)S(1)} all-to-all(s32[16,1,128]{2,1,0:T(1,128)S(1)} %bitcast.39), channel_id=1, replica_groups=mesh['row'=8,'col'=16] {'col'}, dimensions={0} | all-to-all | bytes 16384 | tf_op jit(solution)/shard_map/all_to_all | solution.py:485
  27.9 1.2 %gather.5 = (f32[384,2,256]{2,1,0:T(2,128)S(1)}, s32[8,128]{1,0:T(8,128)S(4)}, s32[1,128]{1,0:T(1,128)S(4)}, s32[2,16]{1,0:T(2,128)S(4)}, s32[2,96]{1,0:T(2,128)S(4)}) custom-call(s32[16,128]{1,0:T(8,128)S(1)} %bitcast.35, f32[512,2,256]{2,1,0:T(2,128)S(1)} %bitcast.48, s32[8,128]{1,0:T(8,128)S(1)} %get-tuple-element.142.refs_0_, ...), custom_call_target="tpu_custom_call" | custom-call | tf_op jit(solution)/shard_map/gather/pallas_call | solution.py:211
  29.1 15.6 %all_to_all.59.got_ref = f32[384,2,256]{2,1,0:T(2,128)S(1)} all-to-all(f32[384,2,256]{2,1,0:T(2,128)S(1)} %get-tuple-element.148), channel_id=1, replica_groups=mesh['row'=8,'col'=16] {'col'}, dimensions={0} | all-to-all | bytes 1572864 | tf_op jit(solution)/shard_map/all_to_all | solution.py:487
  44.8 0.3 forward.5
  45.0 12.8 %all_to_all.60.x_ref = f32[256,2,256]{2,1,0:T(2,128)S(1)} all-to-all(f32[256,2,256]{2,1,0:T(2,128)S(1)} %forward.5), channel_id=1, replica_groups=mesh['row'=8,'col'=16] {'row'}, dimensions={0} | all-to-all | bytes 1048576 | tf_op jit(solution)/shard_map/all_to_all | solution.py:488
  57.9 0.0 slice-done
  57.9 3.5 %blocks.1 = (f32[128,512]{1,0:T(8,128)S(1)}, f32[3,16,128]{2,1,0:T(8,128)S(1)}, s32[1]{0:T(128)}, s32[1]{0:T(128)}) custom-call(s32[1,128]{1,0:T(1,128)S(4)} %get-tuple-element.144.pos_ref, s32[2,16]{1,0:T(2,128)S(4)} %get-tuple-element.145.near_row_ref, s32[2,96]{1,0:T(2,128)S(4)} %get-tuple-element.146.far_row_ref, s32[16,128]{1,0:T(8,128)S(1)} %bitcast.36, ...), custom_call_target="tpu_custom_call" | custom-call | tf_op jit(solution)/shard_map/blocks/pallas_call | solution.py:333
  61.5 0.0 copy-start
  61.5 0.0 copy-start.2
  61.5 0.7 while.12
  62.2 11.9 %all_to_all.61.parts_ref = f32[16,8,512]{2,1,0:T(8,128)S(1)} all-to-all(f32[16,8,512]{2,1,0:T(8,128)S(1)} %bitcast.50), channel_id=1, replica_groups=mesh['row'=8,'col'=16] {'col'}, dimensions={0} | all-to-all | bytes 524288 | tf_op jit(solution)/shard_map/all_to_all | solution.py:505
  74.1 0.7 finish.1
  (19 shorter events, 0.0 us)
Async XLA Ops:
  1.4 56.5 %slice-start = ((s8[16777216]{0:T(1024)(128)(4,1)}), s8[4194304]{0:T(1024)(128)(4,1)S(1)}, s32[]{:S(2)}) async-start(s8[16777216]{0:T(1024)(128)(4,1)} %bitcast.41), calls=%async_computation.8 | async-start | bytes 8388608
  11.3 16.6 %copy-start.8 = (f32[2,131072]{1,0:T(2,128)S(1)}, f32[2,131072]{1,0:T(2,128)}, u32[]{:S(2)}) copy-start(f32[2,131072]{1,0:T(2,128)} %param.15) | copy-start | bytes 3145732
  11.3 16.6 %copy-start.9 = (s32[1,1,2,16]{3,2,1,0:T(2,128)S(1)}, s32[1,1,2,16]{3,2,1,0:T(2,128)}, u32[]{:S(2)}) copy-start(s32[1,1,2,16]{3,2,1,0:T(2,128)} %param.18) | copy-start | bytes 388
  11.3 16.6 %copy-start.10 = (s32[1,1,2,96]{3,2,1,0:T(2,128)S(1)}, s32[1,1,2,96]{3,2,1,0:T(2,128)}, u32[]{:S(2)}) copy-start(s32[1,1,2,96]{3,2,1,0:T(2,128)} %param.21) | copy-start | bytes 2308
  11.3 46.6 %slice-start.1 = ((s8[16777216]{0:T(1024)(128)(4,1)}), s8[4194304]{0:T(1024)(128)(4,1)S(1)}, s32[]{:S(2)}) async-start(s8[16777216]{0:T(1024)(128)(4,1)} %bitcast.41), calls=%async_computation.9 | async-start | bytes 8388608
  11.3 46.6 %slice-start.2 = ((s8[16777216]{0:T(1024)(128)(4,1)}), s8[4194304]{0:T(1024)(128)(4,1)S(1)}, s32[]{:S(2)}) async-start(s8[16777216]{0:T(1024)(128)(4,1)} %bitcast.41), calls=%async_computation.10 | async-start | bytes 8388608
  11.3 46.6 %slice-start.3 = ((s8[16777216]{0:T(1024)(128)(4,1)}), s8[4194304]{0:T(1024)(128)(4,1)S(1)}, s32[]{:S(2)}) async-start(s8[16777216]{0:T(1024)(128)(4,1)} %bitcast.41), calls=%async_computation.11 | async-start | bytes 8388608
  11.3 46.6 %copy-start.7 = (bf16[1,1,96,32,512]{4,3,2,1,0:T(8,128)(2,1)S(1)}, bf16[1,1,96,32,512]{4,3,2,1,0:T(8,128)(2,1)}, u32[]{:S(2)}) copy-start(bf16[1,1,96,32,512]{4,3,2,1,0:T(8,128)(2,1)} %param.20) | copy-start | bytes 9437188
  12.2 45.7 %copy-start.1 = (s32[2048]{0:T(1024)S(1)}, s32[2048]{0:T(1024)}, u32[]{:S(2)}) copy-start(s32[2048]{0:T(1024)} %param.24) | copy-start | bytes 24580
  12.2 45.7 %copy-start.3 = (f32[40]{0:T(128)S(1)}, f32[40]{0:T(128)}, u32[]{:S(2)}) copy-start(f32[40]{0:T(128)} %a_hbm.1) | copy-start | bytes 484
  12.2 45.7 %copy-start.4 = (f32[40]{0:T(128)S(1)}, f32[40]{0:T(128)}, u32[]{:S(2)}) copy-start(f32[40]{0:T(128)} %b_hbm.1) | copy-start | bytes 484
  12.2 45.7 %copy-start.5 = (f32[40]{0:T(128)S(1)}, f32[40]{0:T(128)}, u32[]{:S(2)}) copy-start(f32[40]{0:T(128)} %s_hbm.1) | copy-start | bytes 484
  12.2 45.7 %copy-start.6 = (bf16[1,1,96,32,512]{4,3,2,1,0:T(8,128)(2,1)S(1)}, bf16[1,1,96,32,512]{4,3,2,1,0:T(8,128)(2,1)}, u32[]{:S(2)}) copy-start(bf16[1,1,96,32,512]{4,3,2,1,0:T(8,128)(2,1)} %param.19) | copy-start | bytes 9437188
  61.5 12.6 %copy-start = (f32[2,2048]{1,0:T(2,128)S(1)}, f32[2,2048]{1,0:T(2,128)}, u32[]{:S(2)}) copy-start(f32[2,2048]{1,0:T(2,128)} %stress_ref.1) | copy-start | bytes 49156
  61.5 12.6 %copy-start.2 = (f32[2048]{0:T(1024)S(1)}, f32[2048]{0:T(1024)}, u32[]{:S(2)}) copy-start(f32[2048]{0:T(1024)} %param.23) | copy-start | bytes 24580

commit v12 on v11

--- a/solution.py
+++ b/solution.py
@@ -294,7 +294,7 @@
         acc_ref[rows, :] = acc
         return 0
 
-    lax.fori_loop(0, 2 * B // CHUNK, some_rows, 0, unroll=2)
+    lax.fori_loop(0, 2 * B // CHUNK, some_rows, 0, unroll=4)
     out_ref[...] = acc_ref[...].T
     for copy in small:
         copy.wait()
@@ -322,7 +322,7 @@
             add_far(out_ref, left_ref, right_ref, n, x_ref[pos_ref[0, NEAR + n]], far_row_ref[0, n])
         return 0
 
-    lax.fori_loop(0, N_ROW, some_far, 0, unroll=4)
+    lax.fori_loop(0, N_ROW, some_far, 0, unroll=8)
     for copy in told:
         copy.wait()
 

time: 75.1 us -> 75.9 us (1.011)
  Pallas kernels: 7.28 us -> 8.04 us
    pallas_call x1, Pallas kernels: 3.55 us -> 4.31 us  [block_sums(): pl.pallas_call(blocks_kernel, out_shape=(jax.ShapeDtypeStruct((RC_DEV, 2...]
where the time goes in v12:
time: 75.9 us; the launch traced here: 75.6 us
  blocking collectives  65.9 us (87%)
  Pallas kernels  8.04 us (11%)
  between operations  0.84 us (1%)
    all_to_all x1, blocking collectives, fetch(): asked = lax.all_to_all(req, 'col', 0, 0, tiled=True)  15.7 us
    all_to_all x1, blocking collectives, fetch(): got = lax.all_to_all(reply, 'col', 0, 0, tiled=True)  15.6 us
    all_to_all x1, blocking collectives, fetch(): lax.all_to_all(forward_rows(snd, got), 'row', 0, 0, tiled=True)  12.8 us
    all_to_all x1, blocking collectives, body(): parts = lax.all_to_all(summed, 'col', 0, 0, tiled=True)  11.9 us
    all_to_all x1, blocking collectives, body(): lax.all_to_all(make_payload(source_cluster, near_index, far_index), 'row'...  9.89 us
    pallas_call x1, Pallas kernels, block_sums(): pl.pallas_call(blocks_kernel, out_shape=(jax.ShapeDtypeStruct((RC_DEV, 2...  4.31 us
    pallas_call x3, Pallas kernels, call(): pl.pallas_call(kernel, out_shape=tuple(outs), in_specs=list(specs), out_s...  1.68 us

profile of v12, /device:TPU:0, one launch (start us, length us, event | category | flops | bytes accessed | tf_op | source)
XLA Modules:
  0.0 75.6 jit_solution(14014021417653520590)
XLA Ops:
  0.6 0.7 payload.1
  1.4 0.0 slice-start
  1.4 9.9 %all_to_all.57.g_ref = s32[8,8,128]{2,1,0:T(8,128)S(1)} all-to-all(s32[8,8,128]{2,1,0:T(8,128)S(1)} %payload.1), channel_id=1, replica_groups=mesh['row'=8,'col'=16] {'row'}, dimensions={0} | all-to-all | bytes 65536 | tf_op jit(solution)/shard_map/all_to_all | solution.py:479
  11.3 0.0 slice-start.2
  11.3 0.0 slice-start.3
  11.3 0.0 copy-start.7
  11.3 0.8 %index.5 = (s32[16,128]{1,0:T(8,128)S(1)}, s32[8,128]{1,0:T(8,128)S(1)}, s32[1,128]{1,0:T(1,128)S(1)}) custom-call(s32[8,8,128]{2,1,0:T(8,128)S(1)} %all_to_all.57.g_ref), custom_call_target="tpu_custom_call" | custom-call | flops 15000000512 | tf_op jit(solution)/shard_map/index/pallas_call | solution.py:177
  12.2 0.0 copy-start.1
  12.2 0.0 copy-start.3
  12.2 0.0 copy-start.4
  12.2 0.0 copy-start.5
  12.2 0.0 copy-start.6
  12.2 15.7 %all_to_all.58 = s32[16,1,128]{2,1,0:T(1,128)S(1)} all-to-all(s32[16,1,128]{2,1,0:T(1,128)S(1)} %bitcast.39), channel_id=1, replica_groups=mesh['row'=8,'col'=16] {'col'}, dimensions={0} | all-to-all | bytes 16384 | tf_op jit(solution)/shard_map/all_to_all | solution.py:485
  27.9 1.2 %gather.5 = (f32[384,2,256]{2,1,0:T(2,128)S(1)}, s32[8,128]{1,0:T(8,128)S(4)}, s32[1,128]{1,0:T(1,128)S(4)}, s32[2,16]{1,0:T(2,128)S(4)}, s32[2,96]{1,0:T(2,128)S(4)}) custom-call(s32[16,128]{1,0:T(8,128)S(1)} %bitcast.35, f32[512,2,256]{2,1,0:T(2,128)S(1)} %bitcast.48, s32[8,128]{1,0:T(8,128)S(1)} %get-tuple-element.142.refs_0_, ...), custom_call_target="tpu_custom_call" | custom-call | tf_op jit(solution)/shard_map/gather/pallas_call | solution.py:211
  29.1 15.6 %all_to_all.59.got_ref = f32[384,2,256]{2,1,0:T(2,128)S(1)} all-to-all(f32[384,2,256]{2,1,0:T(2,128)S(1)} %get-tuple-element.148), channel_id=1, replica_groups=mesh['row'=8,'col'=16] {'col'}, dimensions={0} | all-to-all | bytes 1572864 | tf_op jit(solution)/shard_map/all_to_all | solution.py:487
  44.8 0.3 forward.5
  45.0 12.8 %all_to_all.60.x_ref = f32[256,2,256]{2,1,0:T(2,128)S(1)} all-to-all(f32[256,2,256]{2,1,0:T(2,128)S(1)} %forward.5), channel_id=1, replica_groups=mesh['row'=8,'col'=16] {'row'}, dimensions={0} | all-to-all | bytes 1048576 | tf_op jit(solution)/shard_map/all_to_all | solution.py:488
  57.9 0.0 slice-done
  57.9 4.3 %blocks.1 = (f32[128,512]{1,0:T(8,128)S(1)}, f32[3,16,128]{2,1,0:T(8,128)S(1)}, s32[1]{0:T(128)}, s32[1]{0:T(128)}) custom-call(s32[1,128]{1,0:T(1,128)S(4)} %get-tuple-element.144.pos_ref, s32[2,16]{1,0:T(2,128)S(4)} %get-tuple-element.145.near_row_ref, s32[2,96]{1,0:T(2,128)S(4)} %get-tuple-element.146.far_row_ref, s32[16,128]{1,0:T(8,128)S(1)} %bitcast.36, ...), custom_call_target="tpu_custom_call" | custom-call | tf_op jit(solution)/shard_map/blocks/pallas_call | solution.py:333
  62.3 0.0 copy-start
  62.3 0.0 copy-start.2
  62.3 0.7 while.12
  62.9 11.9 %all_to_all.61.parts_ref = f32[16,8,512]{2,1,0:T(8,128)S(1)} all-to-all(f32[16,8,512]{2,1,0:T(8,128)S(1)} %bitcast.50), channel_id=1, replica_groups=mesh['row'=8,'col'=16] {'col'}, dimensions={0} | all-to-all | bytes 524288 | tf_op jit(solution)/shard_map/all_to_all | solution.py:505
  74.9 0.7 finish.1
  (19 shorter events, 0.0 us)
Async XLA Ops:
  1.4 56.5 %slice-start = ((s8[16777216]{0:T(1024)(128)(4,1)}), s8[4194304]{0:T(1024)(128)(4,1)S(1)}, s32[]{:S(2)}) async-start(s8[16777216]{0:T(1024)(128)(4,1)} %bitcast.41), calls=%async_computation.8 | async-start | bytes 8388608
  11.3 16.6 %copy-start.8 = (f32[2,131072]{1,0:T(2,128)S(1)}, f32[2,131072]{1,0:T(2,128)}, u32[]{:S(2)}) copy-start(f32[2,131072]{1,0:T(2,128)} %param.15) | copy-start | bytes 3145732
  11.3 16.6 %copy-start.9 = (s32[1,1,2,16]{3,2,1,0:T(2,128)S(1)}, s32[1,1,2,16]{3,2,1,0:T(2,128)}, u32[]{:S(2)}) copy-start(s32[1,1,2,16]{3,2,1,0:T(2,128)} %param.18) | copy-start | bytes 388
  11.3 16.6 %copy-start.10 = (s32[1,1,2,96]{3,2,1,0:T(2,128)S(1)}, s32[1,1,2,96]{3,2,1,0:T(2,128)}, u32[]{:S(2)}) copy-start(s32[1,1,2,96]{3,2,1,0:T(2,128)} %param.21) | copy-start | bytes 2308
  11.3 46.6 %slice-start.1 = ((s8[16777216]{0:T(1024)(128)(4,1)}), s8[4194304]{0:T(1024)(128)(4,1)S(1)}, s32[]{:S(2)}) async-start(s8[16777216]{0:T(1024)(128)(4,1)} %bitcast.41), calls=%async_computation.9 | async-start | bytes 8388608
  11.3 46.6 %slice-start.2 = ((s8[16777216]{0:T(1024)(128)(4,1)}), s8[4194304]{0:T(1024)(128)(4,1)S(1)}, s32[]{:S(2)}) async-start(s8[16777216]{0:T(1024)(128)(4,1)} %bitcast.41), calls=%async_computation.10 | async-start | bytes 8388608
  11.3 46.6 %slice-start.3 = ((s8[16777216]{0:T(1024)(128)(4,1)}), s8[4194304]{0:T(1024)(128)(4,1)S(1)}, s32[]{:S(2)}) async-start(s8[16777216]{0:T(1024)(128)(4,1)} %bitcast.41), calls=%async_computation.11 | async-start | bytes 8388608
  11.3 46.6 %copy-start.7 = (bf16[1,1,96,32,512]{4,3,2,1,0:T(8,128)(2,1)S(1)}, bf16[1,1,96,32,512]{4,3,2,1,0:T(8,128)(2,1)}, u32[]{:S(2)}) copy-start(bf16[1,1,96,32,512]{4,3,2,1,0:T(8,128)(2,1)} %param.20) | copy-start | bytes 9437188
  12.2 45.7 %copy-start.1 = (s32[2048]{0:T(1024)S(1)}, s32[2048]{0:T(1024)}, u32[]{:S(2)}) copy-start(s32[2048]{0:T(1024)} %param.24) | copy-start | bytes 24580
  12.2 45.7 %copy-start.3 = (f32[40]{0:T(128)S(1)}, f32[40]{0:T(128)}, u32[]{:S(2)}) copy-start(f32[40]{0:T(128)} %a_hbm.1) | copy-start | bytes 484
  12.2 45.7 %copy-start.4 = (f32[40]{0:T(128)S(1)}, f32[40]{0:T(128)}, u32[]{:S(2)}) copy-start(f32[40]{0:T(128)} %b_hbm.1) | copy-start | bytes 484
  12.2 45.7 %copy-start.5 = (f32[40]{0:T(128)S(1)}, f32[40]{0:T(128)}, u32[]{:S(2)}) copy-start(f32[40]{0:T(128)} %s_hbm.1) | copy-start | bytes 484
  12.2 45.7 %copy-start.6 = (bf16[1,1,96,32,512]{4,3,2,1,0:T(8,128)(2,1)S(1)}, bf16[1,1,96,32,512]{4,3,2,1,0:T(8,128)(2,1)}, u32[]{:S(2)}) copy-start(bf16[1,1,96,32,512]{4,3,2,1,0:T(8,128)(2,1)} %param.19) | copy-start | bytes 9437188
  62.3 12.6 %copy-start = (f32[2,2048]{1,0:T(2,128)S(1)}, f32[2,2048]{1,0:T(2,128)}, u32[]{:S(2)}) copy-start(f32[2,2048]{1,0:T(2,128)} %stress_ref.1) | copy-start | bytes 49156
  62.3 12.6 %copy-start.2 = (f32[2048]{0:T(1024)S(1)}, f32[2048]{0:T(1024)}, u32[]{:S(2)}) copy-start(f32[2048]{0:T(1024)} %param.23) | copy-start | bytes 24580
